TPU v7x, 32 devices: a whole 2x2x4 slice. The times are simulated.
32 devices in a mesh: row: 4 (over y, x), col: 8 (over z, core).
Axes of the slice: x: 2, y: 2, z: 4, core: 2. Of those that a mesh axis runs over, the one named last changes fastest.
Arguments:
- tokens: bfloat16 [16384, 1536], P(('row', 'col'))
- g_attn: bfloat16 [1536], P(('row', 'col')), may hold values from 0.5 to 1.5
- w_query: bfloat16 [1536, 1536], P('row', 'col'), may hold values from -0.15625 to 0.15625
- key_projection: bfloat16 [1536, 512], P('row', 'col'), may hold values from -0.15625 to 0.15625
- value_projection: bfloat16 [1536, 512], P('row', 'col'), may hold values from -0.15625 to 0.15625
- w_out: bfloat16 [1536, 1536], P('row', 'col'), may hold values from -0.625 to 0.625
- g_moe: bfloat16 [1536], P(('row', 'col')), may hold values from 0.5 to 1.5
- w_router: bfloat16 [1536, 32], P('row', 'col'), may hold values from -0.078125 to 0.078125
- e_gate: bfloat16 [32, 1536, 512], P('col', 'row'), may hold values from -0.15625 to 0.15625
- e_up: bfloat16 [32, 1536, 512], P('col', 'row'), may hold values from -0.15625 to 0.15625
- e_down: bfloat16 [32, 512, 1536], P('col', None, 'row'), may hold values from -0.5 to 0.5
- s_gate: bfloat16 [1536, 1024], P('row', 'col'), may hold values from -0.15625 to 0.15625
- s_up: bfloat16 [1536, 1024], P('row', 'col'), may hold values from -0.15625 to 0.15625
- s_down: bfloat16 [1024, 1536], P('row', 'col'), may hold values from -0.375 to 0.375
- routes: int32 [16384, 6], P(('row', 'col')), may hold values from 0 to 31, all different within a row; in each aligned block of 512 rows (0 to 511, 512 to 1023, ...) at most 128 rows name the same one
- deal: int32 [32, 4], P(('row', 'col')), may hold values from 0 to 3, as said below
- lengths: int32 [32, 4], replicated, may hold values from 1 to 256, as said below
- cotangent: bfloat16 [16384, 1536], P(('row', 'col')), may hold values from -6 to 6
Outputs:
- output: bfloat16 [16384, 1536], P(('row', 'col'))
- grad_tokens: float32 [16384, 1536], P(('row', 'col'))
- grad_g_attn: float32 [1536], P(('row', 'col'))
- grad_w_query: float32 [1536, 1536], P('row', 'col')
- grad_w_key: float32 [1536, 512], P('row', 'col')
- grad_w_value: float32 [1536, 512], P('row', 'col')
- grad_w_out: float32 [1536, 1536], P('row', 'col')
- grad_g_moe: float32 [1536], P(('row', 'col'))
- grad_w_router: float32 [1536, 32], P('row', 'col')
- grad_e_gate: float32 [32, 1536, 512], P('col', 'row')
- grad_e_up: float32 [32, 1536, 512], P('col', 'row')
- grad_e_down: float32 [32, 512, 1536], P('col', None, 'row')
- grad_s_gate: float32 [1536, 1024], P('row', 'col')
- grad_s_up: float32 [1536, 1024], P('row', 'col')
- grad_s_down: float32 [1024, 1536], P('row', 'col')
Inputs may be any that keep to these rules, and one draw needn't show every extreme that they name: Each row is an ordering of 0 to 3: device g sends its j-th sequence to the device with the same col index whose row index is deal[g, j]. lengths[d, k] is the length of the sequence that device d receives from the device of row index k with d's col index; the 4 sequences that one device sends sum to 512 tokens, and each device sends one of exactly 256. `routes`: among the rows of one device no expert is named more than 128 times.
All inputs are finite; a program needn't handle non-finite values.
Results may differ from a plain program's by a relative error of at most 0.018.
Values may be sent and summed in bfloat16 or wider, within the bound.
A program may use at most 320 MiB of HBM per device.

v0:
```python
import jax
import jax.numpy as jnp
from jax import lax
from jax.sharding import PartitionSpec as P

MODEL_WIDTH = 1536
QUERY_HEADS = 12
KEY_VALUE_HEADS = 4
HEAD_SIZE = 128
TOP = 6
EXP_DEV = 4


norm_eps = 1e-05
masked_score = -1e30


def rms_scale(rows):
    return lax.rsqrt(jnp.mean(rows * rows, axis=-1, keepdims=True) + norm_eps)


def silu_parts(values):
    sigmoid_of = jax.nn.sigmoid(values)
    return (values * sigmoid_of, sigmoid_of * (1.0 + values * (1.0 - sigmoid_of)))


def norm_back(grad_normed, unit_rows, scale_rows, gain):
    grad_unit = grad_normed * gain
    grad_rows = scale_rows * (
        grad_unit - unit_rows * jnp.mean(grad_unit * unit_rows, axis=-1, keepdims=True)
    )
    return (grad_rows, jnp.sum(grad_normed * unit_rows, axis=0))


def matmul(left, right):
    return jnp.dot(left, right, preferred_element_type=jnp.float32)


def slot_mask(slot_lens, slot_extent):
    position = jnp.arange(slot_extent, dtype=jnp.int32)
    causal = position[None, :] <= position[:, None]
    key_live = slot_lens[:, None] > position[None, :]
    allowed = causal[None, :, :] & key_live[:, None, :]
    return allowed[:, None, None, :, :]


def split_heads(block_content, local_slots, slot_extent):
    head_groups = QUERY_HEADS // KEY_VALUE_HEADS
    query_block = block_content[:, :, : QUERY_HEADS * HEAD_SIZE].reshape(
        local_slots, slot_extent, KEY_VALUE_HEADS, head_groups, HEAD_SIZE
    )
    key_block = block_content[
        :, :, QUERY_HEADS * HEAD_SIZE : (QUERY_HEADS + KEY_VALUE_HEADS) * HEAD_SIZE
    ].reshape(local_slots, slot_extent, KEY_VALUE_HEADS, HEAD_SIZE)
    value_block = block_content[:, :, (QUERY_HEADS + KEY_VALUE_HEADS) * HEAD_SIZE :].reshape(
        local_slots, slot_extent, KEY_VALUE_HEADS, HEAD_SIZE
    )
    return (query_block, key_block, value_block)


def masked_scores(query_block, key_block, allowed):
    scores = jnp.einsum(
        "nqhgd,nkhd->nhgqk", query_block, key_block, preferred_element_type=jnp.float32
    ) * HEAD_SIZE ** (-0.5)
    return jnp.where(allowed, scores, masked_score)


def attend_layout(dealt, recv_lens):
    slot_count, slot_extent, row_width = dealt.shape
    total_rows = slot_count * slot_extent
    block_row_list = min(total_rows, max(512, slot_extent))
    local_slots = block_row_list // slot_extent
    block_count = total_rows // block_row_list
    blocked = dealt.reshape(block_count, local_slots, slot_extent, row_width)
    lens_blocked = recv_lens.reshape(block_count, local_slots)
    return (block_row_list, block_count, local_slots, lens_blocked, blocked)


def attend_forward(dealt, recv_lens):
    slot_count, slot_extent, row_width = dealt.shape
    block_row_list, block_count, local_slots, lens_blocked, blocked = attend_layout(
        dealt, recv_lens
    )

    def one_block(block_args):
        lens_blk, block_content = block_args
        query_block, key_block, value_block = split_heads(block_content, local_slots, slot_extent)
        scores = masked_scores(query_block, key_block, slot_mask(lens_blk, slot_extent))
        row_peak = jnp.max(scores, axis=-1, keepdims=True)
        raw_weights = jnp.exp(scores - row_peak)
        row_total = jnp.sum(raw_weights, axis=-1, keepdims=True)
        attn_probs = (raw_weights / row_total).astype(jnp.bfloat16)
        mixed = jnp.einsum(
            "nhgqk,nkhd->nqhgd", attn_probs, value_block, preferred_element_type=jnp.float32
        )
        return (
            mixed.reshape(block_row_list, QUERY_HEADS * HEAD_SIZE).astype(jnp.bfloat16),
            row_peak + jnp.log(row_total),
        )

    mixed_blocks, log_totals = lax.map(one_block, (lens_blocked, blocked))
    return (mixed_blocks.reshape(slot_count, slot_extent, QUERY_HEADS * HEAD_SIZE), log_totals)


def attend_backward(dealt, recv_lens, log_totals, grad_mixed):
    slot_count, slot_extent, row_width = dealt.shape
    block_row_list, block_count, local_slots, lens_blocked, blocked = attend_layout(
        dealt, recv_lens
    )
    grad_blocked = grad_mixed.reshape(
        block_count, local_slots, slot_extent, QUERY_HEADS * HEAD_SIZE
    )
    score_scale = HEAD_SIZE ** (-0.5)

    def one_block(block_args):
        lens_blk, block_content, log_blk, gradient_block = block_args
        query_block, key_block, value_block = split_heads(block_content, local_slots, slot_extent)
        scores = masked_scores(query_block, key_block, slot_mask(lens_blk, slot_extent))
        attn_probs = jnp.exp(scores - log_blk)
        gradient_heads = gradient_block.reshape(
            local_slots, slot_extent, KEY_VALUE_HEADS, QUERY_HEADS // KEY_VALUE_HEADS, HEAD_SIZE
        )
        grad_probs = jnp.einsum(
            "nqhgd,nkhd->nhgqk", gradient_heads, value_block, preferred_element_type=jnp.float32
        )
        inner_sum = jnp.sum(attn_probs * grad_probs, axis=-1, keepdims=True)
        grad_scores = (attn_probs * (grad_probs - inner_sum)).astype(jnp.bfloat16)
        grad_query = (
            jnp.einsum(
                "nhgqk,nkhd->nqhgd", grad_scores, key_block, preferred_element_type=jnp.float32
            )
            * score_scale
        )
        gradient_key = (
            jnp.einsum(
                "nhgqk,nqhgd->nkhd", grad_scores, query_block, preferred_element_type=jnp.float32
            )
            * score_scale
        )
        gradient_value = jnp.einsum(
            "nhgqk,nqhgd->nkhd",
            attn_probs.astype(jnp.bfloat16),
            gradient_heads,
            preferred_element_type=jnp.float32,
        )
        joined = jnp.concatenate(
            [
                grad_query.reshape(block_row_list, QUERY_HEADS * HEAD_SIZE),
                gradient_key.reshape(block_row_list, KEY_VALUE_HEADS * HEAD_SIZE),
                gradient_value.reshape(block_row_list, KEY_VALUE_HEADS * HEAD_SIZE),
            ],
            axis=1,
        )
        return joined.astype(jnp.bfloat16)

    grad_blocks = lax.map(one_block, (lens_blocked, blocked, log_totals, grad_blocked))
    return grad_blocks.reshape(slot_count, slot_extent, row_width)


def home_maps(deal_row, lengths, token_total, slot_extent):
    row_here = lax.axis_index("row")
    col_here = lax.axis_index("col")
    col_count = lax.axis_size("col")
    seq_count = deal_row.shape[0]
    device_id = row_here * col_count + col_here
    dest_global = deal_row * col_count + col_here
    own_lens = lengths[dest_global, row_here]
    seq_ends = jnp.cumsum(own_lens)
    starts = seq_ends - own_lens
    places = jnp.arange(token_total, dtype=jnp.int32)
    seq_of = jnp.sum((places[:, None] >= seq_ends[None, :]).astype(jnp.int32), axis=1)
    seq_pick = (seq_of[:, None] == jnp.arange(seq_count, dtype=jnp.int32)[None, :]).astype(
        jnp.int32
    )
    start_of = jnp.sum(seq_pick * starts[None, :], axis=1)
    slot_of = jnp.sum(seq_pick * deal_row[None, :], axis=1)
    home_index = slot_of * slot_extent + (places - start_of)
    buffer_rows = jnp.arange(seq_count * slot_extent, dtype=jnp.int32)
    slot_match = (deal_row[None, :] == (buffer_rows // slot_extent)[:, None]).astype(jnp.int32)
    slot_length = jnp.sum(slot_match * own_lens[None, :], axis=1)
    slot_start = jnp.sum(slot_match * starts[None, :], axis=1)
    position = buffer_rows % slot_extent
    buffer_live = position < slot_length
    buffer_token = jnp.where(buffer_live, slot_start + position, 0)
    recv_lens = lengths[device_id]
    return (home_index, buffer_token, buffer_live, recv_lens)


def route_maps(routes, experts, capacity):
    flat_routes = routes.reshape(-1)
    onehot = (flat_routes[:, None] == jnp.arange(experts, dtype=jnp.int32)[None, :]).astype(
        jnp.int32
    )
    route_ranks = jnp.sum((jnp.cumsum(onehot, axis=0) - 1) * onehot, axis=1)
    route_slots = flat_routes * capacity + route_ranks
    slot_owner = (
        jnp.full((experts * capacity,), -1, jnp.int32)
        .at[route_slots]
        .set(jnp.arange(flat_routes.shape[0], dtype=jnp.int32))
    )
    return (route_slots, slot_owner)


def on_device(
    tokens,
    g_attn,
    w_query,
    key_projection,
    value_projection,
    w_out,
    g_moe,
    w_router,
    e_gate,
    e_up,
    e_down,
    s_gate,
    s_up,
    s_down,
    routes,
    deal,
    lengths,
    cotangent,
):
    row_count = lax.axis_size("row")
    col_count = lax.axis_size("col")
    token_total = tokens.shape[0]
    slot_extent = 2 * token_total // row_count
    experts = EXP_DEV * col_count
    capacity = 4 * token_total * TOP // (3 * experts)
    query_key_value_width = (QUERY_HEADS + 2 * KEY_VALUE_HEADS) * HEAD_SIZE
    gain_attn_piece = g_attn.reshape(1, 1, -1)
    gain_moe_piece = g_moe.reshape(1, 1, -1)
    (
        part_query,
        part_key,
        part_value,
        part_out,
        part_router,
        part_sgate,
        part_sup,
        part_sdown,
        part_gain_attn,
        part_gain_moe,
    ) = (
        lax.all_gather(w_query, "col", axis=1, tiled=True),
        lax.all_gather(key_projection, "col", axis=1, tiled=True),
        lax.all_gather(value_projection, "col", axis=1, tiled=True),
        lax.all_gather(w_out, "col", axis=1, tiled=True),
        lax.all_gather(w_router, "col", axis=1, tiled=True),
        lax.all_gather(s_gate, "col", axis=1, tiled=True),
        lax.all_gather(s_up, "col", axis=1, tiled=True),
        lax.all_gather(s_down, "col", axis=1, tiled=True),
        lax.all_gather(gain_attn_piece, "col", axis=1, tiled=True),
        lax.all_gather(gain_moe_piece, "col", axis=1, tiled=True),
    )
    (
        full_query,
        full_key,
        full_value,
        full_out,
        full_router,
        full_sgate,
        full_sup,
        full_sdown,
        full_gain_attn,
        full_gain_moe,
        full_egate,
        full_expert_up,
        full_edown,
    ) = (
        lax.all_gather(part_query, "row", axis=0, tiled=True),
        lax.all_gather(part_key, "row", axis=0, tiled=True),
        lax.all_gather(part_value, "row", axis=0, tiled=True),
        lax.all_gather(part_out, "row", axis=0, tiled=True),
        lax.all_gather(part_router, "row", axis=0, tiled=True),
        lax.all_gather(part_sgate, "row", axis=0, tiled=True),
        lax.all_gather(part_sup, "row", axis=0, tiled=True),
        lax.all_gather(part_sdown, "row", axis=0, tiled=True),
        lax.all_gather(part_gain_attn, "row", axis=0, tiled=True),
        lax.all_gather(part_gain_moe, "row", axis=0, tiled=True),
        lax.all_gather(e_gate, "row", axis=1, tiled=True),
        lax.all_gather(e_up, "row", axis=1, tiled=True),
        lax.all_gather(e_down, "row", axis=2, tiled=True),
    )
    gain_attn = full_gain_attn.reshape(-1).astype(jnp.float32)
    gain_moe = full_gain_moe.reshape(-1).astype(jnp.float32)
    tokens_f = tokens.astype(jnp.float32)
    scale_one = rms_scale(tokens_f)
    unit_one = tokens_f * scale_one
    normed_one = (unit_one * gain_attn).astype(jnp.bfloat16)
    projected = jnp.concatenate(
        [
            matmul(normed_one, full_query),
            matmul(normed_one, full_key),
            matmul(normed_one, full_value),
        ],
        axis=1,
    ).astype(jnp.bfloat16)
    home_index, buffer_token, buffer_live, recv_lens = home_maps(
        deal.reshape(-1), lengths, token_total, slot_extent
    )
    send_rows = jnp.where(buffer_live[:, None], jnp.take(projected, buffer_token, axis=0), 0)
    dealt = lax.all_to_all(
        send_rows.reshape(row_count, slot_extent, query_key_value_width),
        "row",
        split_axis=0,
        concat_axis=0,
        tiled=True,
    )
    mixed_dest, log_totals = attend_forward(dealt, recv_lens)
    mixed_back = lax.all_to_all(mixed_dest, "row", split_axis=0, concat_axis=0, tiled=True)
    mixed_home = jnp.take(
        mixed_back.reshape(row_count * slot_extent, QUERY_HEADS * HEAD_SIZE), home_index, axis=0
    )
    after_attn = tokens_f + matmul(mixed_home, full_out)
    scale_two = rms_scale(after_attn)
    unit_two = after_attn * scale_two
    normed_two = (unit_two * gain_moe).astype(jnp.bfloat16)
    logits = matmul(normed_two, full_router)
    route_picks = (
        routes[:, :, None] == jnp.arange(experts, dtype=jnp.int32)[None, None, :]
    ).astype(jnp.float32)
    chosen = jnp.sum(route_picks * logits[:, None, :], axis=-1)
    gate_raw = jnp.exp(chosen - jnp.max(chosen, axis=-1, keepdims=True))
    gate_weights = gate_raw / jnp.sum(gate_raw, axis=-1, keepdims=True)
    route_slots, slot_owner = route_maps(routes, experts, capacity)
    filled = slot_owner >= 0
    owner_token = jnp.where(filled, slot_owner // TOP, 0)
    owner_route = jnp.where(filled, slot_owner, 0)
    send_moe = jnp.where(filled[:, None], jnp.take(normed_two, owner_token, axis=0), 0)
    expert_input = lax.all_to_all(
        send_moe.reshape(col_count, EXP_DEV * capacity, MODEL_WIDTH),
        "col",
        split_axis=0,
        concat_axis=0,
        tiled=True,
    )
    expert_input = expert_input.reshape(col_count, EXP_DEV, capacity, MODEL_WIDTH)
    gate_part = jnp.einsum(
        "hlwz,lze->hlwe", expert_input, full_egate, preferred_element_type=jnp.float32
    )
    up_portion = jnp.einsum(
        "hlwz,lze->hlwe", expert_input, full_expert_up, preferred_element_type=jnp.float32
    )
    gate_activation, gate_slope = silu_parts(gate_part)
    hidden = (gate_activation * up_portion).astype(jnp.bfloat16)
    expert_out = jnp.einsum(
        "sjcf,jfd->sjcd", hidden, full_edown, preferred_element_type=jnp.float32
    ).astype(jnp.bfloat16)
    returned = lax.all_to_all(
        expert_out.reshape(col_count, EXP_DEV * capacity, MODEL_WIDTH),
        "col",
        split_axis=0,
        concat_axis=0,
        tiled=True,
    )
    routed = jnp.take(
        returned.reshape(experts * capacity, MODEL_WIDTH), route_slots, axis=0
    ).reshape(token_total, TOP, MODEL_WIDTH)
    moe_sum = jnp.sum(gate_weights[:, :, None] * routed.astype(jnp.float32), axis=1)
    shared_gate = matmul(normed_two, full_sgate)
    shared_up = matmul(normed_two, full_sup)
    shared_act, shared_slope = silu_parts(shared_gate)
    shared_hidden = (shared_act * shared_up).astype(jnp.bfloat16)
    shared_out = matmul(shared_hidden, full_sdown)
    output = (after_attn + moe_sum + shared_out).astype(jnp.bfloat16)
    grad_out_f = cotangent.astype(jnp.float32)
    grad_sdown = matmul(shared_hidden.T, cotangent)
    grad_shared = matmul(cotangent, full_sdown.T)
    grad_sgate_b = (grad_shared * shared_up * shared_slope).astype(jnp.bfloat16)
    grad_sup_b = (grad_shared * shared_act).astype(jnp.bfloat16)
    grad_sgate = matmul(normed_two.T, grad_sgate_b)
    grad_sup = matmul(normed_two.T, grad_sup_b)
    grad_normed_two = matmul(grad_sgate_b, full_sgate.T) + matmul(grad_sup_b, full_sup.T)
    grad_gates = jnp.einsum("trd,td->tr", routed, cotangent, preferred_element_type=jnp.float32)
    grad_chosen = gate_weights * (
        grad_gates - jnp.sum(gate_weights * grad_gates, axis=-1, keepdims=True)
    )
    grad_logits = jnp.sum(route_picks * grad_chosen[:, :, None], axis=1).astype(jnp.bfloat16)
    grad_router = matmul(normed_two.T, grad_logits)
    grad_normed_two = grad_normed_two + matmul(grad_logits, full_router.T)
    flat_gates = gate_weights.reshape(-1)
    slot_grads = (
        jnp.take(cotangent, owner_token, axis=0).astype(jnp.float32)
        * jnp.take(flat_gates, owner_route)[:, None]
    )
    send_grads = jnp.where(filled[:, None], slot_grads, 0.0).astype(jnp.bfloat16)
    grad_expert_out = lax.all_to_all(
        send_grads.reshape(col_count, EXP_DEV * capacity, MODEL_WIDTH),
        "col",
        split_axis=0,
        concat_axis=0,
        tiled=True,
    )
    grad_expert_out = grad_expert_out.reshape(col_count, EXP_DEV, capacity, MODEL_WIDTH)
    grad_edown = jnp.einsum(
        "sjcf,sjcd->jfd", hidden, grad_expert_out, preferred_element_type=jnp.float32
    )
    gradient_hidden = jnp.einsum(
        "sjcd,jfd->sjcf", grad_expert_out, full_edown, preferred_element_type=jnp.float32
    )
    grad_egate_b = (gradient_hidden * up_portion * gate_slope).astype(jnp.bfloat16)
    gradient_expert_up_batch = (gradient_hidden * gate_activation).astype(jnp.bfloat16)
    grad_egate = jnp.einsum(
        "eyxw,eyxh->ywh", expert_input, grad_egate_b, preferred_element_type=jnp.float32
    )
    gradient_expert_up = jnp.einsum(
        "eyxw,eyxh->ywh", expert_input, gradient_expert_up_batch, preferred_element_type=jnp.float32
    )
    grad_in = (
        jnp.einsum("mboa,bha->mboh", grad_egate_b, full_egate, preferred_element_type=jnp.float32)
        + jnp.einsum(
            "mboa,bha->mboh",
            gradient_expert_up_batch,
            full_expert_up,
            preferred_element_type=jnp.float32,
        )
    ).astype(jnp.bfloat16)
    grad_in_home = lax.all_to_all(
        grad_in.reshape(col_count, EXP_DEV * capacity, MODEL_WIDTH),
        "col",
        split_axis=0,
        concat_axis=0,
        tiled=True,
    )
    grad_routed = jnp.take(
        grad_in_home.reshape(experts * capacity, MODEL_WIDTH), route_slots, axis=0
    ).reshape(token_total, TOP, MODEL_WIDTH)
    grad_normed_two = grad_normed_two + jnp.sum(grad_routed.astype(jnp.float32), axis=1)
    grad_two, grad_gain_moe = norm_back(grad_normed_two, unit_two, scale_two, gain_moe)
    grad_after = grad_out_f + grad_two
    grad_attn_b = grad_after.astype(jnp.bfloat16)
    grad_wout = matmul(mixed_home.T, grad_attn_b)
    grad_mixed = matmul(grad_attn_b, full_out.T).astype(jnp.bfloat16)
    send_back = jnp.where(buffer_live[:, None], jnp.take(grad_mixed, buffer_token, axis=0), 0)
    grad_dest = lax.all_to_all(
        send_back.reshape(row_count, slot_extent, QUERY_HEADS * HEAD_SIZE),
        "row",
        split_axis=0,
        concat_axis=0,
        tiled=True,
    )
    grad_proj_dest = attend_backward(dealt, recv_lens, log_totals, grad_dest)
    grad_proj_back = lax.all_to_all(grad_proj_dest, "row", split_axis=0, concat_axis=0, tiled=True)
    gradient_projection = jnp.take(
        grad_proj_back.reshape(row_count * slot_extent, query_key_value_width), home_index, axis=0
    )
    grad_query_b = gradient_projection[:, : QUERY_HEADS * HEAD_SIZE]
    gradient_key_batch = gradient_projection[
        :, QUERY_HEADS * HEAD_SIZE : (QUERY_HEADS + KEY_VALUE_HEADS) * HEAD_SIZE
    ]
    gradient_value_batch = gradient_projection[:, (QUERY_HEADS + KEY_VALUE_HEADS) * HEAD_SIZE :]
    grad_wquery = matmul(normed_one.T, grad_query_b)
    grad_wkey = matmul(normed_one.T, gradient_key_batch)
    grad_wvalue = matmul(normed_one.T, gradient_value_batch)
    grad_normed_one = (
        matmul(grad_query_b, full_query.T)
        + matmul(gradient_key_batch, full_key.T)
        + matmul(gradient_value_batch, full_value.T)
    )
    grad_one, grad_gain_attn = norm_back(grad_normed_one, unit_one, scale_one, gain_attn)
    grad_tokens = grad_after + grad_one
    gain_attn_term = grad_gain_attn.reshape(row_count, col_count, -1)
    gain_moe_term = grad_gain_moe.reshape(row_count, col_count, -1)
    col_sums = (
        lax.psum_scatter(grad_wquery, "col", scatter_dimension=1, tiled=True),
        lax.psum_scatter(grad_wkey, "col", scatter_dimension=1, tiled=True),
        lax.psum_scatter(grad_wvalue, "col", scatter_dimension=1, tiled=True),
        lax.psum_scatter(grad_wout, "col", scatter_dimension=1, tiled=True),
        lax.psum_scatter(grad_router, "col", scatter_dimension=1, tiled=True),
        lax.psum_scatter(grad_sgate, "col", scatter_dimension=1, tiled=True),
        lax.psum_scatter(grad_sup, "col", scatter_dimension=1, tiled=True),
        lax.psum_scatter(grad_sdown, "col", scatter_dimension=1, tiled=True),
        lax.psum_scatter(gain_attn_term, "col", scatter_dimension=1, tiled=True),
        lax.psum_scatter(gain_moe_term, "col", scatter_dimension=1, tiled=True),
    )
    row_sums = (
        lax.psum_scatter(col_sums[0], "row", scatter_dimension=0, tiled=True),
        lax.psum_scatter(col_sums[1], "row", scatter_dimension=0, tiled=True),
        lax.psum_scatter(col_sums[2], "row", scatter_dimension=0, tiled=True),
        lax.psum_scatter(col_sums[3], "row", scatter_dimension=0, tiled=True),
        lax.psum_scatter(col_sums[4], "row", scatter_dimension=0, tiled=True),
        lax.psum_scatter(col_sums[5], "row", scatter_dimension=0, tiled=True),
        lax.psum_scatter(col_sums[6], "row", scatter_dimension=0, tiled=True),
        lax.psum_scatter(col_sums[7], "row", scatter_dimension=0, tiled=True),
        lax.psum_scatter(col_sums[8], "row", scatter_dimension=0, tiled=True),
        lax.psum_scatter(col_sums[9], "row", scatter_dimension=0, tiled=True),
        lax.psum_scatter(grad_egate, "row", scatter_dimension=1, tiled=True),
        lax.psum_scatter(gradient_expert_up, "row", scatter_dimension=1, tiled=True),
        lax.psum_scatter(grad_edown, "row", scatter_dimension=2, tiled=True),
    )
    dense_sums = (
        row_sums[0],
        row_sums[1],
        row_sums[2],
        row_sums[3],
        row_sums[4],
        row_sums[5],
        row_sums[6],
        row_sums[7],
        row_sums[8],
        row_sums[9],
    )
    expert_sums = (row_sums[10], row_sums[11], row_sums[12])
    return (
        output,
        grad_tokens,
        dense_sums[8].reshape(-1),
        dense_sums[0],
        dense_sums[1],
        dense_sums[2],
        dense_sums[3],
        dense_sums[9].reshape(-1),
        dense_sums[4],
        expert_sums[0],
        expert_sums[1],
        expert_sums[2],
        dense_sums[5],
        dense_sums[6],
        dense_sums[7],
    )


def solution(mesh):
    placed = (
        P(("row", "col"), None),
        P(("row", "col")),
        P("row", "col"),
        P("row", "col"),
        P("row", "col"),
        P("row", "col"),
        P(("row", "col")),
        P("row", "col"),
        P("col", "row", None),
        P("col", "row", None),
        P("col", None, "row"),
        P("row", "col"),
        P("row", "col"),
        P("row", "col"),
        P(("row", "col"), None),
        P(("row", "col"), None),
        P(),
        P(("row", "col"), None),
    )
    return jax.shard_map(
        on_device,
        mesh=mesh,
        in_specs=placed,
        out_specs=(
            P(("row", "col"), None),
            P(("row", "col"), None),
            P(("row", "col")),
            P("row", "col"),
            P("row", "col"),
            P("row", "col"),
            P("row", "col"),
            P(("row", "col")),
            P("row", "col"),
            P("col", "row", None),
            P("col", "row", None),
            P("col", None, "row"),
            P("row", "col"),
            P("row", "col"),
            P("row", "col"),
        ),
        check_vma=False,
    )
```

profile of v0, /device:TPU:2, one launch (start us, length us, event | category | flops | bytes accessed | tf_op | source)
XLA Modules:
  0.0 3134.5 jit_solution(18137597629366899619)
XLA Ops:
  8.8 16.6 all_gather.75
  25.4 17.1 all_gather.73
  45.0 16.7 all-reduce.10
  61.8 8.0 all_gather.70
  71.4 19.7 all-gather.22.cloned.1.call-done
  93.6 30.1 all-gather.20.cloned.1.call-done
  126.9 55.4 %all-gather.18.cloned.1.call-done = bf16[1536,1536]{0,1:T(8,128)(2,1)} async-done(((bf16[384,1536]{0,1:T(8,128)(2,1)}), bf16[1536,1536]{0,1:T(8,128)(2,1)}) %all-gather.18.cloned.1.call-update) | async-done | bytes 4718608 | tf_op jit(solution)/shard_map/all_gather | solution.py:271
  206.8 9.2 reduce-window.18
  217.5 71.6 %all-to-all-done = bf16[4,256,2560]{2,1,0:T(8,128)(2,1)} async-done(((bf16[4,256,2560]{2,1,0:T(8,128)(2,1)}), bf16[4,256,2560]{2,1,0:T(8,128)(2,1)}, u32[]{:S(2)}, u32[]{:S(2)}) %all-to-all-start) | async-done | bytes 5242912 | tf_op jit(solution)/shard_map/all_to_all | solution.py:303
  289.1 8.0 copy.228
  297.0 33.5 %while.22 = (s32[]{:T(128)}, bf16[2,512,1536]{2,1,0:T(8,128)(2,1)}, f32[2,2,4,3,256,1]{4,3,2,1,5,0:T(4,128)S(1)}, bf16[2,2,256,2560]{2,3,1,0:T(8,128)(2,1)}, s32[2,2]{1,0:T(2,128)S(1)}, /*index=5*/s32[]{:T(128)}) while((s32[]{:T(128)}, bf16[2,512,1536]{2,1,0:T(8,128)(2,1)}, f32[2,2,4,3,256,1]{4,3,2,1,5,0:T(4,128)S(1)}, ...), condition=%wide.region_10.11_spmd, body=%wide.region_7.10_spmd.sunk | while | flops 825158144 | bytes 43869300 | solution.py:101
  336.1 61.1 %all_gather.80 = bf16[4,8,48]{2,1,0:T(8,128)(2,1)S(1)} all-gather(bf16[1,8,48]{2,1,0:T(8,128)(2,1)S(1)} %reshape.731), channel_id=1, replica_groups=mesh['row'=4,'col'=8] {'row'}, dimensions={0}, use_global_device_ids=true | all-gather | bytes 3840 | tf_op jit(solution)/shard_map/all_gather | solution.py:280
  398.8 12.0 scatter_custom_fusion
  422.8 19.2 gather_fusion.6
  442.0 11.6 select_select_fusion
  460.5 272.3 %all-to-all-done.2 = bf16[8,512,1536]{2,1,0:T(8,128)(2,1)} async-done(((bf16[8,512,1536]{2,1,0:T(8,128)(2,1)}), bf16[8,512,1536]{2,1,0:T(8,128)(2,1)}, u32[]{:S(2)}, u32[]{:S(2)}) %all-to-all-start.2) | async-done | bytes 12582944 | tf_op jit(solution)/shard_map/all_to_all | solution.py:331
  732.8 14.4 fusion.42
  747.2 15.8 fusion.49
  763.0 12.7 fusion.44
  775.7 10.7 copy.238
  792.2 279.7 %all-gather.2 = bf16[8,4,384]{2,1,0:T(4,128)(2,1)S(1)} all-gather(bf16[1,4,384]{2,1,0:T(4,128)(2,1)S(1)} %bitcast.423), channel_id=1, replica_groups=mesh['row'=4,'col'=8] {'col'}, dimensions={0}, use_global_device_ids=true | all-gather | bytes 27648 | tf_op jit(solution)/shard_map/all_gather | solution.py:249
  1071.9 19.3 gather_fusion.8
  1091.1 8.4 all_gather.82
  1100.9 25.5 gather_fusion.7
  1126.4 8.3 broadcast_select_fusion
  1134.6 15.3 reshape.629
  1150.0 9.1 fusion.79
  1159.6 23.0 gather_fusion.3
  1182.7 12.8 select_convert_fusion
  1201.0 283.1 %all_gather.86 = bf16[384,1024]{1,0:T(8,128)(2,1)} all-gather(bf16[384,128]{1,0:T(8,128)(2,1)S(1)} %copy-done.31), channel_id=1, replica_groups=mesh['row'=4,'col'=8] {'col'}, dimensions={1}, use_global_device_ids=true | all-gather | bytes 884736 | tf_op jit(solution)/shard_map/all_gather | solution.py:250
  1484.2 15.7 all_gather.88
  1499.9 17.2 all_gather.90
  1517.2 18.1 fusion.48
  1535.3 15.5 fusion.60
  1550.8 19.7 fusion.45
  1570.5 10.7 copy.241
  1597.1 22.7 all-gather.38.cloned.1.call-done
  1648.7 294.9 %all-to-all-done.5 = bf16[8,512,1536]{2,1,0:T(8,128)(2,1)} async-done(((bf16[8,512,1536]{2,1,0:T(8,128)(2,1)}), bf16[8,512,1536]{2,1,0:T(8,128)(2,1)}, u32[]{:S(2)}, u32[]{:S(2)}) %all-to-all-start.5) | async-done | bytes 12582944 | tf_op jit(solution)/shard_map/all_to_all | solution.py:419
  1943.6 25.9 gather_fusion.9
  1969.5 11.5 select_convert_fusion.1
  1981.0 21.2 reshape.643
  2002.3 15.2 reduce_sum.211
  2049.7 30.8 all-to-all-done.6
  2085.1 69.9 %while.23 = (s32[]{:T(128)}, bf16[2,512,2560]{2,1,0:T(8,128)(2,1)}, bf16[2,2,256,2560]{2,3,1,0:T(8,128)(2,1)}, s32[2,2]{1,0:T(2,128)S(1)}, f32[2,2,4,3,256,1]{4,...) while((s32[]{:T(128)}, bf16[2,512,2560]{2,1,0:T(8,128)(2,1)}, ...), condition=%wide.region_26.29_spmd, body=%wide.region_24.28_spmd.sunk | while | flops 2047273472 | bytes 159163728 | solution.py:156
  2155.0 63.9 %all_to_all.40 = bf16[4,256,2560]{2,1,0:T(8,128)(2,1)} all-to-all(bf16[4,256,2560]{2,1,0:T(8,128)(2,1)} %bitcast.405), channel_id=1, replica_groups=mesh['row'=4,'col'=8] {'row'}, dimensions={0} | all-to-all | bytes 10485760 | tf_op jit(solution)/shard_map/all_to_all | solution.py:444
  2218.9 9.3 gather_fusion.5
  2249.9 8.3 fusion.83
  2260.3 13.8 convolution_bitcast_fusion.2
  2274.2 13.5 convolution_bitcast_fusion.1
  2287.8 15.0 fusion.55
  2303.7 10.8 reduce-scatter.29.cloned.1.call-done
  2314.6 100.9 %reduce-scatter.33.cloned.1.call-done = f32[1536,192]{0,1:T(8,128)} async-done(((f32[1536,1536]{0,1:T(8,128)}), f32[1536,192]{0,1:T(8,128)}) %reduce-scatter.33.cloned.1.call-update) | async-done | bytes 1179664 | tf_op jit(solution)/shard_map/reduce_scatter | solution.py:469
  2416.2 34.4 %multiply_reduce_fusion = f32[512,1536]{1,0:T(8,128)S(1)} fusion(bf16[512,6,1536]{2,1,0:T(8,128)(2,1)} %reshape.629, f32[512,6]{1,0:T(8,128)S(1)} %copy-done.18), kind=kLoop, calls=%fused_computation.66 | loop fusion | flops 13369344 | bytes 12595200 | tf_op jit(solution)/shard_map/reduce_sum | solution.py:360
  2455.3 89.6 %reduce-scatter.21.cloned.1.call-done = f32[1536,192]{0,1:T(8,128)} async-done(((f32[1536,1536]{0,1:T(8,128)}), f32[1536,192]{0,1:T(8,128)}) %reduce-scatter.21.cloned.1.call-update) | async-done | bytes 1179664 | tf_op jit(solution)/shard_map/reduce_scatter | solution.py:466
  2556.4 26.0 all-reduce.8
  2583.0 8.0 all-reduce.9
  2603.0 29.7 reduce-scatter.53.cloned.1.call-done
  2632.7 124.6 %reduce-scatter.37.cloned.1.call-done = f32[4,384,512]{2,1,0:T(8,128)} async-done(((f32[4,1536,512]{2,1,0:T(8,128)}), f32[4,384,512]{2,1,0:T(8,128)}) %reduce-scatter.37.cloned.1.call-update) | async-done | bytes 3145744 | tf_op jit(solution)/shard_map/reduce_scatter | solution.py:488
  2757.3 124.6 %reduce-scatter.39.cloned.1.call-done = f32[4,384,512]{2,1,0:T(8,128)} async-done(((f32[4,1536,512]{2,1,0:T(8,128)}), f32[4,384,512]{2,1,0:T(8,128)}) %reduce-scatter.39.cloned.1.call-update) | async-done | bytes 3145744 | tf_op jit(solution)/shard_map/reduce_scatter | solution.py:489
  2881.9 124.6 %reduce-scatter.41.cloned.1.call-done = f32[4,512,384]{2,1,0:T(8,128)} async-done(((f32[4,512,1536]{2,1,0:T(8,128)}), f32[4,512,384]{2,1,0:T(8,128)}) %reduce-scatter.41.cloned.1.call-update) | async-done | bytes 3145744 | tf_op jit(solution)/shard_map/reduce_scatter | solution.py:490
  3006.5 28.2 reduce-scatter.27.cloned.1.call-done
  3034.7 28.0 reduce-scatter.31.cloned.1.call-done
  3062.7 32.2 %reduce-scatter.35.cloned.1.call-done = f32[384,192]{0,1:T(8,128)} async-done(((f32[1536,192]{0,1:T(8,128)}), f32[384,192]{0,1:T(8,128)}) %reduce-scatter.35.cloned.1.call-update) | async-done | bytes 294928 | tf_op jit(solution)/shard_map/reduce_scatter | solution.py:481
  3094.9 32.3 %reduce-scatter.23.cloned.1.call-done = f32[384,192]{0,1:T(8,128)} async-done(((f32[1536,192]{0,1:T(8,128)}), f32[384,192]{0,1:T(8,128)}) %reduce-scatter.23.cloned.1.call-update) | async-done | bytes 294928 | tf_op jit(solution)/shard_map/reduce_scatter | solution.py:478
  (436 shorter events, 312.7 us)
Async XLA Ops:
  7.2 62.7 %copy-start = (s32[32,4]{0,1:T(4,128)S(1)}, s32[32,4]{0,1:T(4,128)}, u32[]{:S(2)}) copy-start(s32[32,4]{0,1:T(4,128)} %param.42) | copy-start | bytes 1540
  7.2 36.0 %copy-start.59 = (u32[32]{0:T(128)S(1)}, u32[32]{0:T(128)}, u32[]{:S(2)}) copy-start(u32[32]{0:T(128)} %constant.258) | copy-start | bytes 388
  7.2 37.3 %copy-start.62 = (bf16[48]{0:T(256)(128)(2,1)S(1)}, bf16[48]{0:T(256)(128)(2,1)}, u32[]{:S(2)}) copy-start(bf16[48]{0:T(256)(128)(2,1)} %param.27) | copy-start | bytes 292
  7.2 37.5 %copy-start.63 = (bf16[48]{0:T(256)(128)(2,1)S(1)}, bf16[48]{0:T(256)(128)(2,1)}, u32[]{:S(2)}) copy-start(bf16[48]{0:T(256)(128)(2,1)} %param.32) | copy-start | bytes 292
  7.2 62.6 %copy-start.57 = (s32[1,4]{1,0:T(1,128)S(1)}, s32[1,4]{1,0:T(1,128)}, u32[]{:S(2)}) copy-start(s32[1,4]{1,0:T(1,128)} %param.41) | copy-start | bytes 52
  7.2 63.6 %copy-start.13 = (bf16[512,1536]{1,0:T(8,128)(2,1)S(1)}, bf16[512,1536]{1,0:T(8,128)(2,1)}, u32[]{:S(2)}) copy-start(bf16[512,1536]{1,0:T(8,128)(2,1)} %param.26) | copy-start | bytes 4718596
  7.3 35.3 %all-gather.16.cloned.1.call-start = ((), (), s32[]{:S(2)}) async-start(), calls=%async_computation.26 | async-start | bytes 1327104 | tf_op jit(solution)/shard_map/all_gather | solution.py:245
  8.0 63.3 %all-gather.24.cloned.1.call-start = ((), (), s32[]{:S(2)}) async-start(), calls=%async_computation.30 | async-start | bytes 1327104 | tf_op jit(solution)/shard_map/all_gather | solution.py:248
  8.7 82.4 %all-gather.22.cloned.1.call-start = ((), (), s32[]{:S(2)}) async-start(), calls=%async_computation.29 | async-start | bytes 1966080 | tf_op jit(solution)/shard_map/all_gather | solution.py:273
  25.4 98.3 %all-gather.20.cloned.1.call-start = ((), (), s32[]{:S(2)}) async-start(), calls=%async_computation.28 | async-start | bytes 1966080 | tf_op jit(solution)/shard_map/all_gather | solution.py:272
  42.5 139.8 %all-gather.18.cloned.1.call-start = ((), (), s32[]{:S(2)}) async-start(), calls=%async_computation.27 | async-start | bytes 5898240 | tf_op jit(solution)/shard_map/all_gather | solution.py:271
  43.1 371.6 %all-gather.26.cloned.1.call-start = ((), (), s32[]{:S(2)}) async-start(), calls=%async_computation.31 | async-start | bytes 5898240 | tf_op jit(solution)/shard_map/all_gather | solution.py:274
  69.9 112.5 %copy-start.33 = (f32[1536]{0:T(1024)}, f32[1536]{0:T(1024)S(1)}, u32[]{:S(2)}) copy-start(f32[1536]{0:T(1024)S(1)} %reshape.641) | copy-start | bytes 18436
  71.3 111.0 %copy-start.47 = (f32[512]{0:T(512)}, f32[512]{0:T(512)S(1)}, u32[]{:S(2)}) copy-start(f32[512]{0:T(512)S(1)} %add_rsqrt_fusion.1) | copy-start | bytes 6148
  71.4 116.2 %copy-start.40 = (s32[1024]{0:T(1024)}, s32[1024]{0:T(1024)S(1)}, u32[]{:S(2)}) copy-start(s32[1024]{0:T(1024)S(1)} %broadcast_clamp_fusion.2) | copy-start | bytes 12292
  71.4 122.5 %copy-start.51 = (pred[4,256]{1,0:T(4,128)(4,1)}, pred[4,256]{1,0:T(4,128)(4,1)S(1)}, u32[]{:S(2)}) copy-start(pred[4,256]{1,0:T(4,128)(4,1)S(1)} %get-tuple-element.123) | copy-start | bytes 3076
  71.4 122.5 %copy-start.53 = (pred[4,256]{1,0:T(4,128)(4,1)}, pred[4,256]{1,0:T(4,128)(4,1)S(1)}, u32[]{:S(2)}) copy-start(pred[4,256]{1,0:T(4,128)(4,1)S(1)} %get-tuple-element.124) | copy-start | bytes 3076
  199.7 89.4 %all-to-all-start = ((bf16[4,256,2560]{2,1,0:T(8,128)(2,1)}), bf16[4,256,2560]{2,1,0:T(8,128)(2,1)}, u32[]{:S(2)}, u32[]{:S(2)}) async-start(bf16[4,256,2560]{2,1,0:T(8,128)(2,1)} %select_select_fusion.1), calls=%async_computation | async-start | bytes 10485760 | tf_op jit(solution)/shard_map/all_to_all | solution.py:303
  205.4 255.2 %all-gather.28.cloned.1.call-start = ((), (), s32[]{:S(2)}) async-start(), calls=%async_computation.32 | async-start | bytes 7864320 | tf_op jit(solution)/shard_map/all_gather | solution.py:281
  331.2 80.5 %all-to-all-start.1 = ((bf16[4,256,1536]{2,1,0:T(8,128)(2,1)}), bf16[4,256,1536]{2,1,0:T(8,128)(2,1)S(1)}, u32[]{:S(2)}, u32[]{:S(2)}) async-start(bf16[4,256,1536]{2,1,0:T(8,128)(2,1)} %bitcast.406), calls=%async_computation.1 | async-start | bytes 6291456 | tf_op jit(solution)/shard_map/all_to_all | solution.py:311
  411.1 30.9 copy-start.36
  411.1 30.9 copy-start.38
  453.6 279.2 %all-to-all-start.2 = ((bf16[8,512,1536]{2,1,0:T(8,128)(2,1)}), bf16[8,512,1536]{2,1,0:T(8,128)(2,1)}, u32[]{:S(2)}, u32[]{:S(2)}) async-start(bf16[8,512,1536]{2,1,0:T(8,128)(2,1)} %bitcast.399), calls=%async_computation.2 | async-start | bytes 25165824 | tf_op jit(solution)/shard_map/all_to_all | solution.py:331
  459.0 288.2 %all-gather.30.cloned.1.call-start = ((), (), s32[]{:S(2)}) async-start(), calls=%async_computation.33 | async-start | bytes 7864320 | tf_op jit(solution)/shard_map/all_gather | solution.py:282
  459.8 303.2 %all-gather.32.cloned.1.call-start = ((), (), s32[]{:S(2)}) async-start(), calls=%async_computation.34 | async-start | bytes 7864320 | tf_op jit(solution)/shard_map/all_gather | solution.py:283
  786.4 285.4 %copy-start.2 = (bf16[512,1536]{1,0:T(8,128)(2,1)S(1)}, bf16[512,1536]{1,0:T(8,128)(2,1)}, u32[]{:S(2)}) copy-start(bf16[512,1536]{1,0:T(8,128)(2,1)} %param.43) | copy-start | bytes 4718596
  786.4 314.4 %all-to-all-start.3 = ((bf16[8,512,1536]{2,1,0:T(8,128)(2,1)}), bf16[8,512,1536]{2,1,0:T(8,128)(2,1)}, u32[]{:S(2)}, u32[]{:S(2)}) async-start(bf16[8,512,1536]{2,1,0:T(8,128)(2,1)} %bitcast.400), calls=%async_computation.3 | async-start | bytes 25165824 | tf_op jit(solution)/shard_map/all_to_all | solution.py:350
  1099.5 26.8 copy-start.45
  1195.5 288.7 %copy-start.32 = (bf16[384,128]{1,0:T(8,128)(2,1)S(1)}, bf16[384,128]{1,0:T(8,128)(2,1)}, u32[]{:S(2)}) copy-start(bf16[384,128]{1,0:T(8,128)(2,1)} %param.38) | copy-start | bytes 294916
  1195.5 321.7 %all-to-all-start.4 = ((bf16[8,512,1536]{2,1,0:T(8,128)(2,1)}), bf16[8,512,1536]{2,1,0:T(8,128)(2,1)}, u32[]{:S(2)}, u32[]{:S(2)}) async-start(bf16[8,512,1536]{2,1,0:T(8,128)(2,1)} %bitcast.398), calls=%async_computation.4 | async-start | bytes 25165824 | tf_op jit(solution)/shard_map/all_to_all | solution.py:388
  1200.9 386.1 %all-gather.34.cloned.1.call-start = ((), (), s32[]{:S(2)}) async-start(), calls=%async_computation.35 | async-start | bytes 3932160 | tf_op jit(solution)/shard_map/all_gather | solution.py:276
  1484.1 108.0 %all-gather.36.cloned.1.call-start = ((), (), s32[]{:S(2)}) async-start(), calls=%async_computation.36 | async-start | bytes 3932160 | tf_op jit(solution)/shard_map/all_gather | solution.py:277
  1499.9 119.9 %all-gather.38.cloned.1.call-start = ((), (), s32[]{:S(2)}) async-start(), calls=%async_computation.37 | async-start | bytes 3932160 | tf_op jit(solution)/shard_map/all_gather | solution.py:278
  1581.2 362.4 %all-to-all-start.5 = ((bf16[8,512,1536]{2,1,0:T(8,128)(2,1)}), bf16[8,512,1536]{2,1,0:T(8,128)(2,1)}, u32[]{:S(2)}, u32[]{:S(2)}) async-start(bf16[8,512,1536]{2,1,0:T(8,128)(2,1)} %bitcast.397), calls=%async_computation.5 | async-start | bytes 25165824 | tf_op jit(solution)/shard_map/all_to_all | solution.py:419
  1586.8 661.0 %all-reduce.13.cloned.1.call-start = ((), (), s32[]{:S(2)}) async-start(), calls=%async_computation.56 | async-start | bytes 393216
  1628.4 629.9 %reduce-scatter.43.cloned.1.call-start = ((), (), s32[]{:S(2)}) async-start(), calls=%async_computation.49 | async-start | bytes 7077888 | tf_op jit(solution)/shard_map/reduce_scatter | solution.py:471
  1634.3 624.8 %reduce-scatter.47.cloned.1.call-start = ((), (), s32[]{:S(2)}) async-start(), calls=%async_computation.51 | async-start | bytes 7077888 | tf_op jit(solution)/shard_map/reduce_scatter | solution.py:472
  1943.6 25.9 copy-start.46
  2039.7 40.8 %all-to-all-start.6 = ((bf16[4,256,1536]{2,1,0:T(8,128)(2,1)}), bf16[4,256,1536]{2,1,0:T(8,128)(2,1)}, u32[]{:S(2)}, u32[]{:S(2)}) async-start(bf16[4,256,1536]{2,1,0:T(8,128)(2,1)} %select_select_fusion.2), calls=%async_computation.6 | async-start | bytes 6291456 | tf_op jit(solution)/shard_map/all_to_all | solution.py:436
  2045.1 214.7 %reduce-scatter.51.cloned.1.call-start = ((), (), s32[]{:S(2)}) async-start(), calls=%async_computation.53 | async-start | bytes 7077888 | tf_op jit(solution)/shard_map/reduce_scatter | solution.py:473
  2049.6 35.5 %copy-start.25 = (f32[2,2,4,3,256,1]{4,3,2,1,5,0:T(4,128)S(1)}, f32[2,2,4,3,256,1]{4,3,2,1,5,0:T(4,128)}, u32[]{:S(2)}) copy-start(f32[2,2,4,3,256,1]{4,3,2,1,5,0:T(4,128)} %copy-done.24) | copy-start | bytes 147460
  2049.6 35.4 %copy-start.65 = (s32[2,2]{1,0:T(2,128)S(1)}, s32[2,2]{1,0:T(2,128)}, u32[]{:S(2)}) copy-start(s32[2,2]{1,0:T(2,128)} %copy-done.64) | copy-start | bytes 52
  2049.6 253.3 %reduce-scatter.25.cloned.1.call-start = ((), (), s32[]{:S(2)}) async-start(), calls=%async_computation.40 | async-start | bytes 3538944 | tf_op jit(solution)/shard_map/reduce_scatter | solution.py:467
  2155.0 64.0 %copy-start.50 = (s32[1024]{0:T(1024)S(1)}, s32[1024]{0:T(1024)}, u32[]{:S(2)}) copy-start(s32[1024]{0:T(1024)} %copy-done.49) | copy-start | bytes 12292
  2234.6 79.8 %reduce-scatter.29.cloned.1.call-start = ((), (), s32[]{:S(2)}) async-start(), calls=%async_computation.42 | async-start | bytes 3538944 | tf_op jit(solution)/shard_map/reduce_scatter | solution.py:468
  2238.6 176.8 %reduce-scatter.33.cloned.1.call-start = ((), (), s32[]{:S(2)}) async-start(), calls=%async_computation.44 | async-start | bytes 10616832 | tf_op jit(solution)/shard_map/reduce_scatter | solution.py:469
  2247.1 206.4 %reduce-scatter.55.cloned.1.call-start = ((), (), s32[]{:S(2)}) async-start(), calls=%async_computation.55 | async-start | bytes 983040
  2249.8 295.0 %reduce-scatter.21.cloned.1.call-start = ((), (), s32[]{:S(2)}) async-start(), calls=%async_computation.38 | async-start | bytes 10616832 | tf_op jit(solution)/shard_map/reduce_scatter | solution.py:466
  2258.2 340.0 %reduce-scatter.45.cloned.1.call-start = ((), (), s32[]{:S(2)}) async-start(), calls=%async_computation.50 | async-start | bytes 983040 | tf_op jit(solution)/shard_map/reduce_scatter | solution.py:483
  2259.0 344.0 %reduce-scatter.49.cloned.1.call-start = ((), (), s32[]{:S(2)}) async-start(), calls=%async_computation.52 | async-start | bytes 983040 | tf_op jit(solution)/shard_map/reduce_scatter | solution.py:484
  2259.7 373.0 %reduce-scatter.53.cloned.1.call-start = ((), (), s32[]{:S(2)}) async-start(), calls=%async_computation.54 | async-start | bytes 983040 | tf_op jit(solution)/shard_map/reduce_scatter | solution.py:485
  2260.3 497.0 %reduce-scatter.37.cloned.1.call-start = ((), (), s32[]{:S(2)}) async-start(), calls=%async_computation.46 | async-start | bytes 15728640 | tf_op jit(solution)/shard_map/reduce_scatter | solution.py:488
  2274.2 607.7 %reduce-scatter.39.cloned.1.call-start = ((), (), s32[]{:S(2)}) async-start(), calls=%async_computation.47 | async-start | bytes 15728640 | tf_op jit(solution)/shard_map/reduce_scatter | solution.py:489
  2287.8 718.7 %reduce-scatter.41.cloned.1.call-start = ((), (), s32[]{:S(2)}) async-start(), calls=%async_computation.48 | async-start | bytes 15728640 | tf_op jit(solution)/shard_map/reduce_scatter | solution.py:490
  2302.9 112.6 %copy-start.66 = (u32[32]{0:T(128)S(1)}, u32[32]{0:T(128)}, u32[]{:S(2)}) copy-start(u32[32]{0:T(128)} %constant.274) | copy-start | bytes 388
  2302.9 113.3 %copy-start.18 = (f32[512,6]{1,0:T(8,128)S(1)}, f32[512,6]{1,0:T(8,128)}, u32[]{:S(2)}) copy-start(f32[512,6]{1,0:T(8,128)} %copy-done.17) | copy-start | bytes 36868
  2302.9 731.7 %reduce-scatter.27.cloned.1.call-start = ((), (), s32[]{:S(2)}) async-start(), calls=%async_computation.41 | async-start | bytes 491520 | tf_op jit(solution)/shard_map/reduce_scatter | solution.py:479
  2303.7 759.0 %reduce-scatter.31.cloned.1.call-start = ((), (), s32[]{:S(2)}) async-start(), calls=%async_computation.43 | async-start | bytes 491520 | tf_op jit(solution)/shard_map/reduce_scatter | solution.py:480
  2314.5 780.4 %reduce-scatter.35.cloned.1.call-start = ((), (), s32[]{:S(2)}) async-start(), calls=%async_computation.45 | async-start | bytes 1474560 | tf_op jit(solution)/shard_map/reduce_scatter | solution.py:481
  2415.5 711.7 %reduce-scatter.23.cloned.1.call-start = ((), (), s32[]{:S(2)}) async-start(), calls=%async_computation.39 | async-start | bytes 1474560 | tf_op jit(solution)/shard_map/reduce_scatter | solution.py:478
  2416.2 34.4 %copy-start.10 = (f32[512,1536]{1,0:T(8,128)S(1)}, f32[512,1536]{1,0:T(8,128)}, u32[]{:S(2)}) copy-start(f32[512,1536]{1,0:T(8,128)} %copy-done.8) | copy-start | bytes 9437188
  2416.2 34.4 %copy-start.60 = (bf16[1024,1536]{0,1:T(8,128)(2,1)S(1)}, bf16[1024,1536]{0,1:T(8,128)(2,1)}, u32[]{:S(2)}) copy-start(bf16[1024,1536]{0,1:T(8,128)(2,1)} %all-gather.38.cloned.1.call-done) | copy-start | bytes 9437188
  2416.2 34.4 %copy-start.70 = (bf16[512,1024]{1,0:T(8,128)(2,1)S(1)}, bf16[512,1024]{1,0:T(8,128)(2,1)}, u32[]{:S(2)}) copy-start(bf16[512,1024]{1,0:T(8,128)(2,1)} %get-tuple-element.137) | copy-start | bytes 3145732
  2593.3 533.9 %copy-start.1 = (s32[32,4]{0,1:T(4,128)S(1)}, s32[32,4]{0,1:T(4,128)}, u32[]{:S(2)}) copy-start(s32[32,4]{0,1:T(4,128)} %param.42) | copy-start | bytes 1540
  (54 other events, 348.1 us)
Sparse Core Ops, SparseCore 0:
  9.7 25.6 all-gather.15
  37.1 21.5 all-gather.23
  60.5 30.5 all-gather.21
  92.8 30.8 all-gather.19
  125.4 56.9 all-gather.17
  184.0 105.5 all-gather.25
  291.4 101.8 all-gather.27
  461.7 71.4 all-gather.29
  535.0 69.9 all-gather.31
  1484.2 44.1 all-gather.33
  1530.3 43.9 all-gather.35
  1576.0 43.7 all-gather.37
  1628.5 60.0 all-reduce.12
  1690.8 178.8 reduce-scatter.42
  1872.0 108.0 reduce-scatter.46
  2049.7 67.9 reduce-scatter.50
  2234.8 37.9 reduce-scatter.24
  2275.1 39.3 reduce-scatter.28
  2316.9 98.4 reduce-scatter.32
  2418.4 24.4 reduce-scatter.54
  2445.3 99.5 reduce-scatter.20
  2548.6 24.3 reduce-scatter.44
  2576.8 26.1 reduce-scatter.48
  2606.5 26.0 reduce-scatter.52
  2636.7 120.6 reduce-scatter.36
  2761.1 120.7 reduce-scatter.38
  2885.7 120.6 reduce-scatter.40
  3010.1 24.5 reduce-scatter.26
  3038.3 24.4 reduce-scatter.30
  3066.3 28.5 reduce-scatter.34
  3098.6 28.5 reduce-scatter.22
where the time goes:
time: 3150 us; the launch traced here: 3130 us
  waiting for transfers between devices  1530 us (49%)
  blocking collectives  822 us (26%)
  local copies, waits for them, and re-layouts  301 us (10%)
  matrix products  283 us (9%)
  other arithmetic  136 us (4%)
  starting transfers between devices  39.7 us (1%)
    all_to_all x1, waiting for transfers between devices, on_device(): lax.all_to_all(grad_in.reshape(col_count, EXP_DEV * capacity, MODEL_WIDTH...  295 us
    all_gather x1, blocking collectives, on_device(): lax.all_gather(s_gate, 'col', axis=1, tiled=True)  283 us
    all_gather x1, blocking collectives, on_device(): lax.all_gather(w_router, 'col', axis=1, tiled=True)  280 us
    all_to_all x1, waiting for transfers between devices, on_device(): lax.all_to_all(send_moe.reshape(col_count, EXP_DEV * capacity, MODEL_WIDT...  272 us
    reduce_scatter x1, waiting for transfers between devices, on_device(): lax.psum_scatter(grad_egate, 'row', scatter_dimension=1, tiled=True)  125 us
    reduce_scatter x1, waiting for transfers between devices, on_device(): lax.psum_scatter(gradient_expert_up, 'row', scatter_dimension=1, tiled=True)  125 us
    reduce_scatter x1, waiting for transfers between devices, on_device(): lax.psum_scatter(grad_edown, 'row', scatter_dimension=2, tiled=True)  125 us
    dot_general x24, matrix products, matmul(): return jnp.dot(left, right, preferred_element_type=jnp.float32)  106 us
  transfers between devices with their start and end apart: 38, of which 20 were waited for; matrix products, arithmetic and copies ran while one was open for 19% of the time, Pallas kernels for 0%

commit v1 on v0

v1 whole, which is shorter than its diff:
```python
import functools

import jax
import jax.numpy as jnp
from jax import lax
from jax.experimental import pallas as pl
from jax.experimental.pallas import tpu as pltpu
from jax.sharding import PartitionSpec as P

MODEL_WIDTH = 1536
QUERY_HEADS = 12
KEY_VALUE_HEADS = 4
GROUP = QUERY_HEADS // KEY_VALUE_HEADS
HEAD_SIZE = 128
TOP = 6
EXP_DEV = 4

norm_eps = 1e-05
masked_score = -1e30
BF = jnp.bfloat16
F32 = jnp.float32


def rms_scale(rows):
    return lax.rsqrt(jnp.mean(rows * rows, axis=-1, keepdims=True) + norm_eps)


def silu_parts(values):
    sigmoid_of = jax.nn.sigmoid(values)
    return (values * sigmoid_of, sigmoid_of * (1.0 + values * (1.0 - sigmoid_of)))


def norm_back(grad_normed, unit_rows, scale_rows, gain):
    grad_unit = grad_normed * gain
    grad_rows = scale_rows * (
        grad_unit - unit_rows * jnp.mean(grad_unit * unit_rows, axis=-1, keepdims=True)
    )
    return (grad_rows, jnp.sum(grad_normed * unit_rows, axis=0))


def mm(left, right):
    return jnp.dot(left, right, preferred_element_type=F32)


def mm_nt(left, right):
    return lax.dot_general(left, right, (((1,), (1,)), ((), ())), preferred_element_type=F32)


def mm_tn(left, right):
    return lax.dot_general(left, right, (((0,), (0,)), ((), ())), preferred_element_type=F32)


def ein(spec, a, b):
    return jnp.einsum(spec, a, b, preferred_element_type=F32)


def allowed_mask(seg_col, seg_row):
    total = seg_col.shape[0]
    q_at = lax.broadcasted_iota(jnp.int32, (total, total), 0)
    k_at = lax.broadcasted_iota(jnp.int32, (total, total), 1)
    return (seg_col == seg_row) & (k_at <= q_at)


def attend_forward_kernel(q_ref, k_ref, v_ref, segc_ref, segr_ref, mixed_ref, lse_ref):
    allowed = allowed_mask(segc_ref[...], segr_ref[...])
    keys = k_ref[...]
    values = v_ref[...]
    for g in range(GROUP):
        cols = slice(g * HEAD_SIZE, (g + 1) * HEAD_SIZE)
        scores = mm_nt(q_ref[:, cols], keys) * HEAD_SIZE ** (-0.5)
        scores = jnp.where(allowed, scores, masked_score)
        peak = jnp.max(scores, axis=-1, keepdims=True)
        raw = jnp.exp(scores - peak)
        total = jnp.sum(raw, axis=-1, keepdims=True)
        probs = (raw * (1.0 / total)).astype(BF)
        mixed_ref[:, cols] = mm(probs, values).astype(BF)
        lse_ref[0, :, g : g + 1] = peak + jnp.log(total)


def attend_backward_kernel(
    q_ref, k_ref, v_ref, gm_ref, segc_ref, segr_ref, lse_ref, gq_ref, gk_ref, gv_ref
):
    allowed = allowed_mask(segc_ref[...], segr_ref[...])
    keys = k_ref[...]
    values = v_ref[...]
    scale = HEAD_SIZE ** (-0.5)
    grad_key = None
    for g in range(GROUP):
        cols = slice(g * HEAD_SIZE, (g + 1) * HEAD_SIZE)
        query = q_ref[:, cols]
        grad_mixed = gm_ref[:, cols]
        scores = mm_nt(query, keys) * scale
        probs = jnp.where(allowed, jnp.exp(scores - lse_ref[0, :, g : g + 1]), 0.0)
        grad_probs = mm_nt(grad_mixed, values)
        inner = jnp.sum(probs * grad_probs, axis=-1, keepdims=True)
        grad_scores = (probs * (grad_probs - inner)).astype(BF)
        gq_ref[:, cols] = (mm(grad_scores, keys) * scale).astype(BF)
        part_key = mm_tn(grad_scores, query)
        part_value = mm_tn(probs.astype(BF), grad_mixed)
        if grad_key is None:
            grad_key, grad_value = part_key, part_value
        else:
            grad_key, grad_value = grad_key + part_key, grad_value + part_value
    gk_ref[...] = (grad_key * scale).astype(BF)
    gv_ref[...] = grad_value.astype(BF)


def attention_specs(total):
    wide = pl.BlockSpec((total, GROUP * HEAD_SIZE), lambda h: (0, h))
    narrow = pl.BlockSpec((total, HEAD_SIZE), lambda h: (0, h))
    seg_col = pl.BlockSpec((total, 1), lambda h: (0, 0))
    seg_row = pl.BlockSpec((1, total), lambda h: (0, 0))
    lse = pl.BlockSpec((1, total, GROUP), lambda h: (h, 0, 0))
    return wide, narrow, seg_col, seg_row, lse


def attend_forward(queries, keys, values, segment):
    total = queries.shape[0]
    wide, narrow, seg_col, seg_row, lse = attention_specs(total)
    return pl.pallas_call(
        attend_forward_kernel,
        grid=(KEY_VALUE_HEADS,),
        in_specs=[wide, narrow, narrow, seg_col, seg_row],
        out_specs=[wide, lse],
        out_shape=[
            jax.ShapeDtypeStruct(queries.shape, BF),
            jax.ShapeDtypeStruct((KEY_VALUE_HEADS, total, GROUP), F32),
        ],
        compiler_params=pltpu.CompilerParams(vmem_limit_bytes=48 * 1024 * 1024),
        name="attend_forward",
    )(queries, keys, values, segment[:, None], segment[None, :])


def attend_backward(queries, keys, values, grad_mixed, segment, log_totals):
    total = queries.shape[0]
    wide, narrow, seg_col, seg_row, lse = attention_specs(total)
    return pl.pallas_call(
        attend_backward_kernel,
        grid=(KEY_VALUE_HEADS,),
        in_specs=[wide, narrow, narrow, wide, seg_col, seg_row, lse],
        out_specs=[wide, narrow, narrow],
        out_shape=[
            jax.ShapeDtypeStruct(queries.shape, BF),
            jax.ShapeDtypeStruct(keys.shape, BF),
            jax.ShapeDtypeStruct(keys.shape, BF),
        ],
        compiler_params=pltpu.CompilerParams(vmem_limit_bytes=48 * 1024 * 1024),
        name="attend_backward",
    )(queries, keys, values, grad_mixed, segment[:, None], segment[None, :], log_totals)


def on_device(
    tokens,
    g_attn,
    w_query,
    key_projection,
    value_projection,
    w_out,
    g_moe,
    w_router,
    e_gate,
    e_up,
    e_down,
    s_gate,
    s_up,
    s_down,
    routes,
    deal,
    lengths,
    cotangent,
):
    rows_n = lax.axis_size("row")
    cols_n = lax.axis_size("col")
    row_here = lax.axis_index("row")
    col_here = lax.axis_index("col")
    both = ("row", "col")
    total = tokens.shape[0]
    width = MODEL_WIDTH
    experts = EXP_DEV * cols_n
    cap = 4 * total * TOP // (3 * experts)

    q_w, k_w = w_query.shape[1], key_projection.shape[1]
    bundle = jnp.concatenate([w_query.T, key_projection.T, value_projection.T, w_out.T], axis=0)
    full = lax.all_gather(bundle, both, axis=0).reshape(
        (rows_n, cols_n) + bundle.shape
    )

    def piece(lo, extent):
        part = full[:, :, lo : lo + extent]
        return part.transpose(1, 2, 0, 3).reshape(cols_n * extent, width)

    wq_t = piece(0, q_w)
    wk_t = piece(q_w, k_w)
    wv_t = piece(q_w + k_w, k_w)
    wo_t = piece(q_w + 2 * k_w, q_w)
    gain_attn = lax.all_gather(g_attn, both, axis=0, tiled=True).astype(F32)
    gain_moe = lax.all_gather(g_moe, both, axis=0, tiled=True).astype(F32)
    router = lax.all_gather(
        lax.all_gather(w_router, "col", axis=1, tiled=True), "row", axis=0, tiled=True
    )
    egate = lax.all_gather(e_gate, "row", axis=1, tiled=True)
    eup = lax.all_gather(e_up, "row", axis=1, tiled=True)
    edown = lax.all_gather(e_down, "row", axis=2, tiled=True)
    sgate = lax.all_gather(s_gate, "row", axis=0, tiled=True)
    sup = lax.all_gather(s_up, "row", axis=0, tiled=True)
    units = s_gate.shape[1]
    per_row = s_down.shape[0] // units
    sdown_cols = lax.all_gather(s_down, "col", axis=1, tiled=True)
    sdown_mine = lax.dynamic_slice_in_dim(sdown_cols, (col_here % per_row) * units, units, 0)
    sdown = lax.dynamic_index_in_dim(
        lax.all_gather(sdown_mine, "row", axis=0), col_here // per_row, 0, keepdims=False
    )
    dy_all = lax.all_gather(cotangent, "col", axis=0)
    routes_all = lax.all_gather(routes, "col", axis=0)

    own_lens = lengths[deal.reshape(-1) * cols_n + col_here, row_here]
    seq_ends = jnp.cumsum(own_lens)
    places = jnp.arange(total, dtype=jnp.int32)
    segment = jnp.sum((places[:, None] >= seq_ends[None, :]).astype(jnp.int32), axis=1)

    tokens_f = tokens.astype(F32)
    scale_one = rms_scale(tokens_f)
    unit_one = tokens_f * scale_one
    normed_one = (unit_one * gain_attn).astype(BF)
    queries = mm_nt(normed_one, wq_t).astype(BF)
    keys = mm_nt(normed_one, wk_t).astype(BF)
    values = mm_nt(normed_one, wv_t).astype(BF)
    mixed, log_totals = attend_forward(queries, keys, values, segment)
    after_attn = tokens_f + mm_nt(mixed, wo_t)
    scale_two = rms_scale(after_attn)
    unit_two = after_attn * scale_two
    normed_two = (unit_two * gain_moe).astype(BF)
    logits = mm(normed_two, router)
    route_picks = (
        routes[:, :, None] == jnp.arange(experts, dtype=jnp.int32)[None, None, :]
    ).astype(F32)
    chosen = jnp.sum(route_picks * logits[:, None, :], axis=-1)
    gate_raw = jnp.exp(chosen - jnp.max(chosen, axis=-1, keepdims=True))
    gate_weights = gate_raw / jnp.sum(gate_raw, axis=-1, keepdims=True)

    x_all = lax.all_gather(normed_two, "col", axis=0)
    gates_all = lax.all_gather(gate_weights, "col", axis=0)
    mine = col_here * EXP_DEV + jnp.arange(EXP_DEV, dtype=jnp.int32)
    hits = routes_all[:, :, :, None] == mine
    hit = jnp.any(hits, axis=2)
    gate = jnp.sum(jnp.where(hits, gates_all[:, :, :, None], 0.0), axis=2)
    rank = jnp.where(hit, jnp.cumsum(hit.astype(jnp.int32), axis=1) - 1, -1)
    rank = rank.transpose(0, 2, 1)
    gate = gate.transpose(0, 2, 1)
    pick = rank[:, :, None, :] == jnp.arange(cap, dtype=jnp.int32)[None, None, :, None]
    slot_gate = jnp.sum(jnp.where(pick, gate[:, :, None, :], 0.0), axis=-1)
    pick_b = pick.astype(BF)
    xs = ein("sept,std->sepd", pick_b, x_all).astype(BF)
    dys = ein("sept,std->sepd", pick_b, dy_all).astype(BF)
    gate_part = ein("sepd,edf->sepf", xs, egate)
    up_part = ein("sepd,edf->sepf", xs, eup)
    act, slope = silu_parts(gate_part)
    hidden_f = (act * up_part).astype(BF).astype(F32)
    gated_hidden = (hidden_f * slot_gate[..., None]).astype(BF)
    weighted = ein("sepf,efd->sepd", gated_hidden, edown).astype(BF)
    out_part = ein("sept,sepd->std", pick_b, weighted)
    grad_hidden = ein("sepd,efd->sepf", dys, edown)
    slot_ggw = jnp.sum(hidden_f * grad_hidden, axis=-1)
    ggw = jnp.sum(jnp.where(pick, slot_ggw[..., None], 0.0), axis=2)
    grad_hidden = grad_hidden * slot_gate[..., None]
    geg = (grad_hidden * up_part * slope).astype(BF)
    geu = (grad_hidden * act).astype(BF)
    grad_edown = ein("sepf,sepd->efd", gated_hidden, dys)
    grad_egate = ein("sepd,sepf->edf", xs, geg)
    grad_eup = ein("sepd,sepf->edf", xs, geu)
    grad_in = (ein("sepf,edf->sepd", geg, egate) + ein("sepf,edf->sepd", geu, eup)).astype(BF)
    gx_part = ein("sept,sepd->std", pick_b, grad_in)
    x_flat = x_all.reshape(cols_n * total, width)
    dy_flat = dy_all.reshape(cols_n * total, width)
    s_act, s_slope = silu_parts(mm(x_flat, sgate))
    s_upv = mm(x_flat, sup)
    s_hidden = (s_act * s_upv).astype(BF)
    gsh = mm_nt(dy_flat, sdown)
    gsg = (gsh * s_upv * s_slope).astype(BF)
    gsu = (gsh * s_act).astype(BF)
    out_part = out_part + mm(s_hidden, sdown).reshape(out_part.shape)
    gx_part = gx_part + (mm_nt(gsg, sgate) + mm_nt(gsu, sup)).reshape(gx_part.shape)
    grad_sgate = mm_tn(x_flat, gsg)
    grad_sup = mm_tn(x_flat, gsu)
    grad_sdown = mm_tn(s_hidden, dy_flat)

    gx = lax.psum_scatter(gx_part.astype(BF), "col", scatter_dimension=0)
    moe = lax.psum_scatter(out_part.astype(BF), "col", scatter_dimension=0)
    output = (after_attn + moe.astype(F32)).astype(BF)
    ggw_home = lax.all_to_all(ggw, "col", split_axis=0, concat_axis=0, tiled=True)
    ggw_home = ggw_home.reshape(experts, total).T

    grad_gates = jnp.sum(route_picks * ggw_home[:, None, :], axis=-1)
    grad_chosen = gate_weights * (
        grad_gates - jnp.sum(gate_weights * grad_gates, axis=-1, keepdims=True)
    )
    grad_logits = jnp.sum(route_picks * grad_chosen[:, :, None], axis=1).astype(BF)
    grad_router = mm_tn(normed_two, grad_logits)
    grad_normed_two = gx.astype(F32) + mm_nt(grad_logits, router)
    grad_two, grad_gain_moe = norm_back(grad_normed_two, unit_two, scale_two, gain_moe)
    grad_after = cotangent.astype(F32) + grad_two
    grad_attn_b = grad_after.astype(BF)
    grad_wout = mm_tn(grad_attn_b, mixed)
    grad_mixed = mm(grad_attn_b, wo_t).astype(BF)
    gq, gk, gv = attend_backward(queries, keys, values, grad_mixed, segment, log_totals)
    grad_wq = mm_tn(gq, normed_one)
    grad_wk = mm_tn(gk, normed_one)
    grad_wv = mm_tn(gv, normed_one)
    grad_normed_one = mm(gq, wq_t) + mm(gk, wk_t) + mm(gv, wv_t)
    grad_one, grad_gain_attn = norm_back(grad_normed_one, unit_one, scale_one, gain_attn)
    grad_tokens = grad_after + grad_one

    def cut(grad):
        part = grad.reshape(cols_n, grad.shape[0] // cols_n, rows_n, width // rows_n)
        return part.transpose(2, 0, 1, 3)

    grads = jnp.concatenate(
        [cut(grad_wq), cut(grad_wk), cut(grad_wv), cut(grad_wout)], axis=2
    ).astype(BF)
    grads = lax.psum_scatter(
        grads.reshape((rows_n * cols_n,) + bundle.shape), both, scatter_dimension=0
    ).astype(F32)
    out_wq = grads[:q_w].T
    out_wk = grads[q_w : q_w + k_w].T
    out_wv = grads[q_w + k_w : q_w + 2 * k_w].T
    out_wo = grads[q_w + 2 * k_w :].T
    out_g_attn = lax.psum_scatter(grad_gain_attn, both, scatter_dimension=0, tiled=True)
    out_g_moe = lax.psum_scatter(grad_gain_moe, both, scatter_dimension=0, tiled=True)
    out_router = lax.psum_scatter(
        lax.psum_scatter(grad_router, "col", scatter_dimension=1, tiled=True),
        "row",
        scatter_dimension=0,
        tiled=True,
    )

    def row_sum(grad, dim):
        return lax.psum_scatter(
            grad.astype(BF), "row", scatter_dimension=dim, tiled=True
        ).astype(F32)

    out_eg = row_sum(grad_egate, 1)
    out_eu = row_sum(grad_eup, 1)
    out_ed = row_sum(grad_edown, 2)
    out_sg = row_sum(grad_sgate, 0)
    out_su = row_sum(grad_sup, 0)
    sd_sum = lax.psum(grad_sdown.astype(BF), "row")
    sd_parts = sd_sum.reshape(units, cols_n, width // cols_n).transpose(1, 0, 2)
    sd_home = lax.all_to_all(sd_parts, "col", split_axis=0, concat_axis=0, tiled=True)
    out_sd = lax.dynamic_slice_in_dim(sd_home, row_here * per_row, per_row, 0)
    out_sd = out_sd.reshape(per_row * units, width // cols_n).astype(F32)
    return (
        output,
        grad_tokens,
        out_g_attn,
        out_wq,
        out_wk,
        out_wv,
        out_wo,
        out_g_moe,
        out_router,
        out_eg,
        out_eu,
        out_ed,
        out_sg,
        out_su,
        out_sd,
    )


def solution(mesh):
    both = P(("row", "col"), None)
    flat = P(("row", "col"))
    tile = P("row", "col")
    wide = P("col", "row", None)
    down = P("col", None, "row")
    return jax.shard_map(
        on_device,
        mesh=mesh,
        in_specs=(
            both, flat, tile, tile, tile, tile, flat, tile, wide, wide, down,
            tile, tile, tile, both, both, P(), both,
        ),
        out_specs=(
            both, both, flat, tile, tile, tile, tile, flat, tile, wide, wide, down,
            tile, tile, tile,
        ),
        check_vma=False,
    )
```

time: 3150 us -> 1560 us (0.50)
  waiting for transfers between devices: 1530 us -> 822 us
  blocking collectives: 822 us -> 178 us
  local copies, waits for them, and re-layouts: 301 us -> 114 us
  other arithmetic: 136 us -> 67 us
  matrix products: 283 us -> 328 us
    all_to_all x7 -> x2, waiting for transfers between devices: 670 us -> 0.01 us  [the longest x1 0.01 us: on_device(): lax.all_to_all(ggw, 'col', split_axis=0, concat_axis=0, tiled=True)]
    all_gather x8 -> x6, blocking collectives: 427 us -> 79.6 us  [the longest x1 16 us: on_device(): sdown_cols = lax.all_gather(s_down, 'col', axis=1, tiled=True)]
    reduce_scatter x17 -> x7, waiting for transfers between devices: 730 us -> 420 us  [the longest x4 159 us: row_sum(): lax.psum_scatter(grad.astype(BF), 'row', scatter_dimension=dim, tiled=True)]
    all_gather x1, blocking collectives: 280 us -> 14.1 us  [on_device(): lax.all_gather(w_router, 'col', axis=1, tiled=True)]
    all_gather x12 -> x7, waiting for transfers between devices: 128 us -> 329 us  [the longest x1 87.8 us: on_device(): x_all = lax.all_gather(normed_two, 'col', axis=0)]
    gather x10 -> x1, local copies, waits for them, and re-layouts: 138 us -> 0.65 us  [on_device(): own_lens = lengths[deal.reshape(-1) * cols_n + col_here, row_here]]
    unnamed x33 -> x21, waiting for transfers between devices: 6.38 us -> 73.4 us
    all_to_all x1 -> x0, blocking collectives: 63.9 us -> none  [on_device(): lax.all_to_all(grad_proj_dest, 'row', split_axis=0, concat_axis=0, tiled=...]
  transfers between devices with their start and end apart: 38 -> 20, of which waited for: 20 -> 14; matrix products, arithmetic and copies ran while one was open for 19% -> 30% of each run, Pallas kernels for 0% -> 1%
where the time goes in v1:
time: 1560 us
  waiting for transfers between devices  822 us (53%)
  matrix products  328 us (21%)
  blocking collectives  178 us (11%)
  local copies, waits for them, and re-layouts  114 us (7%)
  other arithmetic  67 us (4%)
  Pallas kernels  21.4 us (1%)
  between operations  16.2 us (1%)
    dot_general x13, matrix products, ein(): return jnp.einsum(spec, a, b, preferred_element_type=F32)  195 us
    reduce_scatter x4, waiting for transfers between devices, row_sum(): lax.psum_scatter(grad.astype(BF), 'row', scatter_dimension=dim, tiled=True)  159 us
    reduce_scatter x1, waiting for transfers between devices, on_device(): moe = lax.psum_scatter(out_part.astype(BF), 'col', scatter_dimension=0)  125 us
    reduce_scatter x1, waiting for transfers between devices, on_device(): lax.psum_scatter(grads.reshape((rows_n * cols_n,) + bundle.shape), both,...  101 us
    all_gather x1, waiting for transfers between devices, on_device(): x_all = lax.all_gather(normed_two, 'col', axis=0)  87.8 us
    unnamed x2, blocking collectives  84 us
    unnamed x21, waiting for transfers between devices  73.4 us
    all_gather x1, waiting for transfers between devices, on_device(): egate = lax.all_gather(e_gate, 'row', axis=1, tiled=True)  57.5 us
  transfers between devices with their start and end apart: 20, of which 14 were waited for; matrix products, arithmetic and copies ran while one was open for 30% of the time, Pallas kernels for 1%

profile of v1, /device:TPU:2, one launch (start us, length us, event | category | flops | bytes accessed | tf_op | source)
XLA Modules:
  0.0 1555.6 jit_solution(3957092748247707487)
XLA Ops:
  9.3 16.0 %all_gather.80 = bf16[256,1536]{0,1:T(8,128)(2,1)S(1)} all-gather(bf16[256,192]{0,1:T(8,128)(2,1)} %param.31), channel_id=1, replica_groups=mesh['row'=4,'col'=8] {'col'}, dimensions={1}, use_global_device_ids=true | all-gather | bytes 884736 | tf_op jit(solution)/shard_map/all_gather | solution.py:208
  28.2 43.6 %all-reduce.7 = (bf16[1536]{0:T(1024)(128)(2,1)S(1)}, bf16[1536]{0:T(1024)(128)(2,1)S(1)}) all-reduce(bf16[1536]{0:T(1024)(128)(2,1)S(1)} %dynamic-update-slice, bf16[1536]{0:T(1024)(128)(2,1)S(1)} %dynamic-update-slice.1), channel_id=1, replica_groups=mesh['row'=4,'col'=8] {'row','col'}, use_global_device_ids=true, to_apply=%add.1 | all-reduce | flops 3072 | bytes 12288
  72.5 37.5 %all-gather.20.cloned.1.call-done = bf16[16384,384]{1,0:T(8,128)(2,1)} async-done(((bf16[512,384]{1,0:T(8,128)(2,1)}), bf16[16384,384]{1,0:T(8,128)(2,1)}) %all-gather.20.cloned.1.call-update) | async-done | bytes 12582928 | tf_op jit(solution)/shard_map/all_gather | solution.py:184
  110.0 7.0 fusion.91
  117.0 6.2 copy.222
  141.2 7.3 attend_forward.1
  148.5 5.4 multiply_reduce_fusion.2
  159.1 14.1 all-gather.5
  173.2 14.4 all-gather.1
  192.8 14.9 all_gather.75
  207.7 9.2 all_gather.78
  217.0 9.7 all_gather.79
  229.4 31.9 %all-gather.26.cloned.1.call-done = bf16[4096,1536]{1,0:T(8,128)(2,1)} async-done(((bf16[512,1536]{1,0:T(8,128)(2,1)}), bf16[4096,1536]{1,0:T(8,128)(2,1)}) %all-gather.26.cloned.1.call-update) | async-done | bytes 12582928 | tf_op jit(solution)/shard_map/all_gather | solution.py:213
  261.3 13.2 convolution_convert_fusion
  275.2 15.4 all_gather.76
  291.6 87.8 %all-gather.22.cloned.1.call-done = bf16[4096,1536]{1,0:T(8,128)(2,1)} async-done(((bf16[512,1536]{1,0:T(8,128)(2,1)}), bf16[4096,1536]{1,0:T(8,128)(2,1)}) %all-gather.22.cloned.1.call-update) | async-done | bytes 12582928 | tf_op jit(solution)/shard_map/all_gather | solution.py:241
  379.4 13.3 convolution_convert_fusion.1
  392.6 56.9 %all-gather.16.cloned.1.call-done = bf16[4,1536,512]{2,1,0:T(8,128)(2,1)} async-done(((bf16[4,384,512]{2,1,0:T(8,128)(2,1)}), bf16[4,1536,512]{2,1,0:T(8,128)(2,1)}) %all-gather.16.cloned.1.call-update) | async-done | bytes 6291472 | tf_op jit(solution)/shard_map/all_gather | solution.py:202
  449.5 14.4 fusion.9
  463.9 57.5 %all-gather.14.cloned.1.call-done = bf16[4,1536,512]{2,1,0:T(8,128)(2,1)} async-done(((bf16[4,384,512]{2,1,0:T(8,128)(2,1)}), bf16[4,1536,512]{2,1,0:T(8,128)(2,1)}) %all-gather.14.cloned.1.call-update) | async-done | bytes 6291472 | tf_op jit(solution)/shard_map/all_gather | solution.py:201
  521.4 14.4 fusion.11
  535.9 57.4 %all-gather.18.cloned.1.call-done = bf16[4,512,1536]{2,1,0:T(8,128)(2,1)} async-done(((bf16[4,512,384]{2,1,0:T(8,128)(2,1)}), bf16[4,512,1536]{2,1,0:T(8,128)(2,1)}) %all-gather.18.cloned.1.call-update) | async-done | bytes 6291472 | tf_op jit(solution)/shard_map/all_gather | solution.py:203
  593.2 18.0 %fusion.14 = (f32[8,4,128]{2,0,1:T(8,128)S(1)}, bf16[8,4,128,512]{3,2,0,1:T(8,128)(2,1)}, f32[4,8,128,512]{3,2,1,0:T(8,128)}) fusion(f32[4,8,128,512]{3,2,1,0:T(8,128)} %fusion.9, f32[4,8,128,512]{3,2,1,0:T(8,128)} %fusion.11, bf16[4,512,1536]{2,1,0:T(8,128)(2,1)} %all-gather.18.cloned.1.call-done, bf16[8,4,128,1536]{3,2,1,0:T(8,128)(2,1)} %convolution_convert_fusion), kind=kOutput, calls=%fused_computation.28 | convolution fusion | flops 6461321216 | bytes 48250880 | tf_op jit(solution)/shard_map/sepd,efd->sepf/dot_general | solution.py:54
  611.3 8.8 select_reduce_fusion
  620.1 4.6 all-to-all-start
  624.8 6.8 fusion.95
  631.6 6.6 fusion.94
  638.2 5.8 multiply_convert_fusion.2
  644.0 10.2 fusion.96
  654.2 13.9 multiply_convert_fusion
  668.1 15.0 fusion.32
  683.1 19.7 %fusion.162 = bf16[8,4,128,1536]{3,2,1,0:T(8,128)(2,1)} fusion(f32[4,8,128,1536]{3,2,0,1:T(8,128)} %fusion.32, bf16[4,1536,512]{2,1,0:T(8,128)(2,1)} %all-gather.16.cloned.1.call-done, bf16[8,4,128,512]{3,2,0,1:T(8,128)(2,1)} %get-tuple-element.37), kind=kOutput, calls=%fused_computation.14.clone.2 | convolution fusion | flops 6455033856 | bytes 48234496 | tf_op jit(solution)/shard_map/sepf,edf->sepd/dot_general | solution.py:54
  702.8 16.7 %convolution_add_fusion = f32[4096,1536]{1,0:T(8,128)} fusion(f32[4096,1536]{1,0:T(8,128)} %fusion.96, bf16[4096,128]{1,0:T(8,128)(2,1)} %get-tuple-element.43, bf16[1536,128]{1,0:T(8,128)(2,1)S(1)} %all_gather.79), kind=kOutput, calls=%fused_computation.6 | convolution fusion | flops 1616904192 | bytes 51773440 | tf_op jit(solution)/shard_map/dot_general | solution.py:46
  720.8 18.8 %fusion = bf16[8,512,1536]{2,1,0:T(8,128)(2,1)} fusion(f32[8,512,1536]{2,1,0:T(8,128)} %bitcast.291, s32[8,4,512]{2,1,0:T(4,128)S(1)} %copy.172, bf16[8,4,128,1536]{3,2,1,0:T(8,128)(2,1)} %fusion.162), kind=kOutput, calls=%fused_computation.2 | convolution fusion | flops 6457131008 | bytes 50397184 | tf_op jit(solution)/shard_map/sept,sepd->std/dot_general | solution.py:54
  739.7 13.0 fusion.166
  752.8 15.9 %fusion.3 = f32[8,512,1536,1]{2,1,3,0:T(8,128)} fusion(s32[8,4,512]{2,1,0:T(4,128)S(1)} %copy.172, bf16[8,4,128,1536]{3,2,1,0:T(8,128)(2,1)} %fusion.166), kind=kOutput, calls=%fused_computation.15 | convolution fusion | flops 6444548096 | bytes 37814272 | tf_op jit(solution)/shard_map/sept,sepd->std/dot_general | solution.py:54
  768.7 14.5 fusion.1
  783.4 8.1 convolution_convert_fusion.9
  796.9 7.4 convolution_convert_fusion.10
  804.4 7.4 convolution_convert_fusion.11
  811.8 13.9 bitcast_convert_fusion
  825.7 11.3 copy.217
  837.0 8.1 copy.231
  845.2 12.8 bitcast_convert_fusion.1
  858.4 12.7 bitcast_convert_fusion.2
  871.2 35.4 %reduce-scatter.16.cloned.1.call-done = bf16[1,512,1536]{2,1,0:T(8,128)(2,1)} async-done(((bf16[8,512,1536]{2,1,0:T(8,128)(2,1)}), bf16[1,512,1536]{2,1,0:T(8,128)(2,1)}) %reduce-scatter.16.cloned.1.call-update) | async-done | bytes 1572880 | tf_op jit(solution)/shard_map/reduce_scatter | solution.py:287
  906.7 5.1 multiply_reduce_fusion
  911.7 124.8 %reduce-scatter.14.cloned.1.call-done = bf16[1,512,1536]{2,1,0:T(8,128)(2,1)} async-done(((bf16[8,512,1536]{2,1,0:T(8,128)(2,1)}), bf16[1,512,1536]{2,1,0:T(8,128)(2,1)}) %reduce-scatter.14.cloned.1.call-update) | async-done | bytes 1572880 | tf_op jit(solution)/shard_map/reduce_scatter | solution.py:288
  1036.5 5.5 multiply_add_fusion
  1048.1 9.1 reshape.317
  1057.2 5.7 copy.191
  1062.8 6.2 convolution_convert_fusion.7.gm_ref
  1069.1 14.1 attend_backward.1
  1104.0 6.8 convolution_convert_fusion.4
  1110.8 9.0 reshape.314
  1123.4 8.2 pad_maximum_fusion
  1139.9 25.5 %reduce-scatter.24.cloned.1.call-done = bf16[384,128]{1,0:T(8,128)(2,1)} async-done(((bf16[1536,128]{1,0:T(8,128)(2,1)}), bf16[384,128]{1,0:T(8,128)(2,1)}) %reduce-scatter.24.cloned.1.call-update) | async-done | bytes 98320 | tf_op jit(solution)/shard_map/reduce_scatter | solution.py:337
  1167.7 70.7 %reduce-scatter.30.cloned.1.call-done = bf16[384,2048]{1,0:T(8,128)(2,1)} async-done(((bf16[1536,2048]{1,0:T(8,128)(2,1)}), bf16[384,2048]{1,0:T(8,128)(2,1)}) %reduce-scatter.30.cloned.1.call-update) | async-done | bytes 1572880
  1249.6 61.9 %reduce-scatter.22.cloned.1.call-done = bf16[4,384,512]{2,1,0:T(8,128)(2,1)} async-done(((bf16[4,1536,512]{2,1,0:T(8,128)(2,1)}), bf16[4,384,512]{2,1,0:T(8,128)(2,1)}) %reduce-scatter.22.cloned.1.call-update) | async-done | bytes 1572880 | tf_op jit(solution)/shard_map/reduce_scatter | solution.py:337
  1315.0 69.6 %reduce-scatter.20.cloned.1.call-done = bf16[4,384,512]{2,1,0:T(8,128)(2,1)} async-done(((bf16[4,1536,512]{2,1,0:T(8,128)(2,1)}), bf16[4,384,512]{2,1,0:T(8,128)(2,1)}) %reduce-scatter.20.cloned.1.call-update) | async-done | bytes 1572880 | tf_op jit(solution)/shard_map/reduce_scatter | solution.py:337
  1388.1 5.0 fusion.97
  1398.0 40.4 %all-reduce.6 = (f32[1536]{0:T(1024)S(1)}, f32[1536]{0:T(1024)S(1)}) all-reduce(f32[1536]{0:T(1024)S(1)} %get-tuple-element.27, f32[1536]{0:T(1024)S(1)} %get-tuple-element.25), channel_id=9, replica_groups=mesh['row'=4,'col'=8] {'row','col'}, use_global_device_ids=true, to_apply=%region_22.23.clone | all-reduce | flops 3072 | bytes 24576
  1439.6 5.3 fusion.59
  1444.9 101.1 %reduce-scatter.18.cloned.1.call-done = bf16[1,512,384]{2,1,0:T(8,128)(2,1)} async-done(((bf16[32,512,384]{2,1,0:T(8,128)(2,1)}), bf16[1,512,384]{2,1,0:T(8,128)(2,1)}) %reduce-scatter.18.cloned.1.call-update) | async-done | bytes 393232 | tf_op jit(solution)/shard_map/reduce_scatter | solution.py:320
  (253 shorter events, 112.7 us)
Async XLA Ops:
  7.2 19.7 %copy-start = (s32[32,4]{0,1:T(4,128)S(1)}, s32[32,4]{0,1:T(4,128)}, u32[]{:S(2)}) copy-start(s32[32,4]{0,1:T(4,128)} %param.34) | copy-start | bytes 1540
  7.2 19.7 %copy-start.53 = (s32[1,4]{1,0:T(1,128)S(1)}, s32[1,4]{1,0:T(1,128)}, u32[]{:S(2)}) copy-start(s32[1,4]{1,0:T(1,128)} %param.33) | copy-start | bytes 52
  7.2 20.6 %copy-start.54 = (bf16[48]{0:T(256)(128)(2,1)S(1)}, bf16[48]{0:T(256)(128)(2,1)}, u32[]{:S(2)}) copy-start(bf16[48]{0:T(256)(128)(2,1)} %param.19) | copy-start | bytes 292
  7.2 20.8 %copy-start.55 = (bf16[48]{0:T(256)(128)(2,1)S(1)}, bf16[48]{0:T(256)(128)(2,1)}, u32[]{:S(2)}) copy-start(bf16[48]{0:T(256)(128)(2,1)} %param.24) | copy-start | bytes 292
  7.2 64.9 %copy-start.14 = (bf16[512,1536]{1,0:T(8,128)(2,1)S(1)}, bf16[512,1536]{1,0:T(8,128)(2,1)}, u32[]{:S(2)}) copy-start(bf16[512,1536]{1,0:T(8,128)(2,1)} %param.18) | copy-start | bytes 4718596
  7.2 102.8 %all-gather.20.cloned.1.call-start = ((), (), s32[]{:S(2)}) async-start(), calls=%async_computation.22 | async-start | bytes 12976128 | tf_op jit(solution)/shard_map/all_gather | solution.py:184
  9.2 217.4 %all-gather.24.cloned.1.call-start = ((), (), s32[]{:S(2)}) async-start(), calls=%async_computation.24 | async-start | bytes 1966080 | tf_op jit(solution)/shard_map/all_gather | solution.py:211
  26.1 235.2 %all-gather.26.cloned.1.call-start = ((), (), s32[]{:S(2)}) async-start(), calls=%async_computation.25 | async-start | bytes 14155776 | tf_op jit(solution)/shard_map/all_gather | solution.py:213
  26.8 352.5 %all-gather.22.cloned.1.call-start = ((), (), s32[]{:S(2)}) async-start(), calls=%async_computation.23 | async-start | bytes 14155776 | tf_op jit(solution)/shard_map/all_gather | solution.py:241
  71.8 66.6 %copy-start.41 = (f32[1536]{0:T(1024)}, f32[1536]{0:T(1024)S(1)}, u32[]{:S(2)}) copy-start(f32[1536]{0:T(1024)S(1)} %convert_element_type.152) | copy-start | bytes 18436
  71.9 82.2 %copy-start.37 = (f32[1536]{0:T(1024)}, f32[1536]{0:T(1024)S(1)}, u32[]{:S(2)}) copy-start(f32[1536]{0:T(1024)S(1)} %convert_element_type.158) | copy-start | bytes 18436
  72.0 69.2 %copy-start.7 = (s32[512]{0:T(512)}, s32[512]{0:T(512)S(1)}, u32[]{:S(2)}) copy-start(s32[512]{0:T(512)S(1)} %convert_reduce_fusion) | copy-start | bytes 6148
  72.5 66.0 %copy-start.49 = (f32[512]{0:T(512)}, f32[512]{0:T(512)S(1)}, u32[]{:S(2)}) copy-start(f32[512]{0:T(512)S(1)} %add_rsqrt_fusion.1) | copy-start | bytes 6148
  129.9 6.4 copy-start.22
  131.4 6.0 copy-start.24
  141.2 12.8 copy-start.2
  157.1 16.1 %copy-start.36 = (s32[512,6]{0,1:T(8,128)S(1)}, s32[512,6]{0,1:T(8,128)}, u32[]{:S(2)}) copy-start(s32[512,6]{0,1:T(8,128)} %param.32) | copy-start | bytes 36868
  157.1 50.6 %copy-start.39 = (bf16[384,128]{1,0:T(8,128)(2,1)S(1)}, bf16[384,128]{1,0:T(8,128)(2,1)}, u32[]{:S(2)}) copy-start(bf16[384,128]{1,0:T(8,128)(2,1)} %param.29) | copy-start | bytes 294916
  157.1 59.8 %copy-start.40 = (bf16[384,128]{1,0:T(8,128)(2,1)S(1)}, bf16[384,128]{1,0:T(8,128)(2,1)}, u32[]{:S(2)}) copy-start(bf16[384,128]{1,0:T(8,128)(2,1)} %param.30) | copy-start | bytes 294916
  157.2 292.3 %all-gather.16.cloned.1.call-start = ((), (), s32[]{:S(2)}) async-start(), calls=%async_computation.12 | async-start | bytes 7864320 | tf_op jit(solution)/shard_map/all_gather | solution.py:202
  157.8 363.6 %all-gather.14.cloned.1.call-start = ((), (), s32[]{:S(2)}) async-start(), calls=%async_computation.11 | async-start | bytes 7864320 | tf_op jit(solution)/shard_map/all_gather | solution.py:201
  158.3 434.9 %all-gather.18.cloned.1.call-start = ((), (), s32[]{:S(2)}) async-start(), calls=%async_computation.13 | async-start | bytes 7864320 | tf_op jit(solution)/shard_map/all_gather | solution.py:203
  207.7 66.8 %copy-start.34 = (bf16[1536,32]{0,1:T(8,128)(2,1)}, bf16[1536,32]{0,1:T(8,128)(2,1)S(1)}, u32[]{:S(2)}) copy-start(bf16[1536,32]{0,1:T(8,128)(2,1)S(1)} %all_gather.75) | copy-start | bytes 294916
  261.3 13.2 copy-start.13
  275.2 16.3 %copy-start.43 = (f32[512]{0:T(512)}, f32[512]{0:T(512)S(1)}, u32[]{:S(2)}) copy-start(f32[512]{0:T(512)S(1)} %reduce_max.9) | copy-start | bytes 6148
  275.2 16.3 %copy-start.47 = (f32[512]{0:T(512)}, f32[512]{0:T(512)S(1)}, u32[]{:S(2)}) copy-start(f32[512]{0:T(512)S(1)} %fusion.77) | copy-start | bytes 6148
  620.1 99.4 %all-to-all-start = ((f32[8,4,512]{2,1,0:T(4,128)}), f32[8,4,512]{2,1,0:T(4,128)S(1)}, u32[]{:S(2)}, u32[]{:S(2)}) async-start(f32[8,4,512]{2,1,0:T(4,128)} %get-tuple-element.29), calls=%async_computation.2 | async-start | bytes 131072 | tf_op jit(solution)/shard_map/all_to_all | solution.py:290
  624.7 170.1 %all-reduce.13.cloned.1.call-start = ((), (), s32[]{:S(2)}) async-start(), calls=%async_computation.28 | async-start | bytes 393216
  624.7 6.8 copy-start.30
  624.8 13.4 slice-start
  624.8 13.4 slice-start.1
  631.6 6.6 slice-start.2
  644.0 10.2 copy-start.32
  644.0 10.2 copy-start.29
  702.8 16.8 %copy-start.44 = (f32[512]{0:T(512)S(1)}, f32[512]{0:T(512)}, u32[]{:S(2)}) copy-start(f32[512]{0:T(512)} %copy-done.43) | copy-start | bytes 6148
  702.8 16.8 %copy-start.48 = (f32[512]{0:T(512)S(1)}, f32[512]{0:T(512)}, u32[]{:S(2)}) copy-start(f32[512]{0:T(512)} %copy-done.47) | copy-start | bytes 6148
  720.8 185.9 %reduce-scatter.16.cloned.1.call-start = ((), (), s32[]{:S(2)}) async-start(), calls=%async_computation.15 | async-start | bytes 14155776 | tf_op jit(solution)/shard_map/reduce_scatter | solution.py:287
  739.7 296.8 %reduce-scatter.14.cloned.1.call-start = ((), (), s32[]{:S(2)}) async-start(), calls=%async_computation.14 | async-start | bytes 14155776 | tf_op jit(solution)/shard_map/reduce_scatter | solution.py:288
  752.8 15.9 %copy-start.20 = (bf16[4096,128]{1,0:T(8,128)(2,1)S(1)}, bf16[4096,128]{1,0:T(8,128)(2,1)}, u32[]{:S(2)}) copy-start(bf16[4096,128]{1,0:T(8,128)(2,1)} %get-tuple-element.45) | copy-start | bytes 3145732
  783.2 10.4 copy-start.56
  783.2 13.7 copy-start.31
  783.2 348.4 %all-reduce.11.cloned.1.call-start = ((), (), s32[]{:S(2)}) async-start(), calls=%async_computation.21 | async-start | bytes 786432 | tf_op jit(solution)/shard_map/psum | solution.py:346
  793.5 341.7 %reduce-scatter.28.cloned.1.call-start = ((), (), s32[]{:S(2)}) async-start(), calls=%async_computation.26 | async-start | bytes 983040
  796.9 7.5 copy-start.33
  796.9 341.5 %reduce-scatter.26.cloned.1.call-start = ((), (), s32[]{:S(2)}) async-start(), calls=%async_computation.20 | async-start | bytes 491520 | tf_op jit(solution)/shard_map/reduce_scatter | solution.py:337
  804.3 361.2 %reduce-scatter.24.cloned.1.call-start = ((), (), s32[]{:S(2)}) async-start(), calls=%async_computation.19 | async-start | bytes 491520 | tf_op jit(solution)/shard_map/reduce_scatter | solution.py:337
  811.8 426.7 %reduce-scatter.30.cloned.1.call-start = ((), (), s32[]{:S(2)}) async-start(), calls=%async_computation.27 | async-start | bytes 7864320
  845.1 466.4 %reduce-scatter.22.cloned.1.call-start = ((), (), s32[]{:S(2)}) async-start(), calls=%async_computation.18 | async-start | bytes 7864320 | tf_op jit(solution)/shard_map/reduce_scatter | solution.py:337
  858.0 526.6 %reduce-scatter.20.cloned.1.call-start = ((), (), s32[]{:S(2)}) async-start(), calls=%async_computation.17 | async-start | bytes 7864320 | tf_op jit(solution)/shard_map/reduce_scatter | solution.py:337
  871.1 35.5 %copy-start.35 = (bf16[1536,32]{0,1:T(8,128)(2,1)S(1)}, bf16[1536,32]{0,1:T(8,128)(2,1)}, u32[]{:S(2)}) copy-start(bf16[1536,32]{0,1:T(8,128)(2,1)} %copy-done.34) | copy-start | bytes 294916
  871.1 35.5 %copy-start.38 = (f32[1536]{0:T(1024)S(1)}, f32[1536]{0:T(1024)}, u32[]{:S(2)}) copy-start(f32[1536]{0:T(1024)} %copy-done.37) | copy-start | bytes 18436
  871.1 35.5 %copy-start.46 = (f32[512]{0:T(512)S(1)}, f32[512]{0:T(512)}, u32[]{:S(2)}) copy-start(f32[512]{0:T(512)} %copy-done.45) | copy-start | bytes 6148
  871.2 165.4 %copy-start.21 = (bf16[512,1536]{1,0:T(8,128)(2,1)S(1)}, bf16[512,1536]{1,0:T(8,128)(2,1)}, u32[]{:S(2)}) copy-start(bf16[512,1536]{1,0:T(8,128)(2,1)} %param.35) | copy-start | bytes 4718596
  871.2 674.8 %reduce-scatter.18.cloned.1.call-start = ((), (), s32[]{:S(2)}) async-start(), calls=%async_computation.16 | async-start | bytes 12976128 | tf_op jit(solution)/shard_map/reduce_scatter | solution.py:320
  1036.5 7.2 copy-start.10
  1062.8 6.2 copy-start.4
  1062.8 6.2 copy-start.6
  1062.8 6.2 copy-start.8
  1069.0 15.3 copy-start.15
  1069.0 15.3 copy-start.42
  1069.0 15.3 copy-start.50
  1131.6 35.4 %all-to-all-start.1 = ((bf16[8,128,192]{1,2,0:T(8,128)(2,1)}), bf16[8,128,192]{1,2,0:T(8,128)(2,1)S(1)}, u32[]{:S(2)}, u32[]{:S(2)}) async-start(bf16[8,128,192]{1,2,0:T(8,128)(2,1)} %all-reduce.11.cloned.1.call-done), calls=%async_computation.8 | async-start | bytes 786432 | tf_op jit(solution)/shard_map/all_to_all | solution.py:348
  1395.0 44.6 %copy-start.17 = (bf16[512,1536]{1,0:T(8,128)(2,1)S(1)}, bf16[512,1536]{1,0:T(8,128)(2,1)}, u32[]{:S(2)}) copy-start(bf16[512,1536]{1,0:T(8,128)(2,1)} %param.18) | copy-start | bytes 4718596
  1439.6 109.0 %copy-start.1 = (s32[32,4]{0,1:T(4,128)S(1)}, s32[32,4]{0,1:T(4,128)}, u32[]{:S(2)}) copy-start(s32[32,4]{0,1:T(4,128)} %param.34) | copy-start | bytes 1540
  (16 other events, 48.2 us)
Sparse Core Ops, SparseCore 0:
  11.7 98.3 all-gather.19
  112.4 29.2 all-gather.23
  143.3 117.9 all-gather.25
  263.4 115.9 all-gather.21
  381.0 68.4 all-gather.15
  451.2 70.1 all-gather.13
  523.2 69.9 all-gather.17
  720.9 55.0 all-reduce.12
  778.4 128.1 reduce-scatter.15
  908.9 127.5 reduce-scatter.13
  1039.8 42.4 all-reduce.10
  1085.0 26.0 reduce-scatter.27
  1113.9 24.4 reduce-scatter.25
  1141.0 24.4 reduce-scatter.23
  1168.3 70.0 reduce-scatter.29
  1241.3 70.1 reduce-scatter.21
  1314.3 70.2 reduce-scatter.19
  1390.5 155.4 reduce-scatter.17

commit v2 on v1

--- a/solution.py
+++ b/solution.py
@@ -147,6 +147,819 @@
         compiler_params=pltpu.CompilerParams(vmem_limit_bytes=48 * 1024 * 1024),
         name="attend_backward",
     )(queries, keys, values, grad_mixed, segment[:, None], segment[None, :], log_totals)
+
+
+def remote(src, dst, send_sem, recv_sem, device):
+    return pltpu.make_async_remote_copy(
+        src_ref=src,
+        dst_ref=dst,
+        send_sem=send_sem,
+        recv_sem=recv_sem,
+        device_id=device,
+        device_id_type=pl.DeviceIdType.MESH,
+    )
+
+
+class Place:
+    def __init__(self, rows_n, cols_n):
+        self.rows_n = rows_n
+        self.chips = cols_n // 2
+        self.row = lax.axis_index("row")
+        self.col = lax.axis_index("col")
+        self.chip = lax.div(self.col, 2)
+        self.core = lax.rem(self.col, 2)
+        self.other = self.col + 1 - 2 * self.core
+
+    def peer_row(self, step):
+        return lax.rem(self.row + step, self.rows_n)
+
+    def greet(self, with_rows, with_downs=0):
+        barrier = pltpu.get_barrier_semaphore()
+
+        def hello(row, col):
+            pl.semaphore_signal(
+                barrier, inc=1, device_id=(row, col), device_id_type=pl.DeviceIdType.MESH
+            )
+
+        hello(self.row, self.other)
+
+        @pl.when(self.chip > 0)
+        def _():
+            hello(self.row, self.col - 2)
+
+        @pl.when(self.chip < self.chips - 1)
+        def _():
+            hello(self.row, self.col + 2)
+
+        count = (
+            1
+            + (self.chip > 0).astype(jnp.int32)
+            + (self.chip < self.chips - 1).astype(jnp.int32)
+        )
+        if with_rows:
+            for step in range(1, self.rows_n):
+                hello(self.peer_row(step), self.col)
+            count = count + (self.rows_n - 1)
+        pl.semaphore_wait(barrier, count)
+
+
+class LineGather:
+    def __init__(self, place, src, dst, core_sems, line_sems, recv_sems, local_sem):
+        self.at = place
+        self.src, self.dst = src, dst
+        self.core_sems, self.line_sems, self.recv_sems = core_sems, line_sems, recv_sems
+        self.local = pltpu.make_async_copy(src, dst.at[place.col], local_sem)
+
+    def to_core(self, block, src=None):
+        at = self.at
+        src = self.dst.at[block] if src is None else src
+        return remote(
+            src, self.dst.at[block], self.core_sems.at[block], self.recv_sems.at[block],
+            (at.row, at.other),
+        )
+
+    def to_line(self, block, way, src=None):
+        at = self.at
+        src = self.dst.at[block] if src is None else src
+        return remote(
+            src,
+            self.dst.at[block],
+            self.line_sems.at[block, (way + 1) // 2],
+            self.recv_sems.at[block],
+            (at.row, at.col + 2 * way),
+        )
+
+    def ends(self, way):
+        return self.at.chip < self.at.chips - 1 if way > 0 else self.at.chip > 0
+
+    def start(self):
+        self.local.start()
+        for way in (1, -1):
+
+            @pl.when(self.ends(way))
+            def _():
+                self.to_line(self.at.col, way, self.src).start()
+
+        self.to_core(self.at.col, self.src).start()
+
+    def arrivals(self, dist, act):
+        for way in (1, -1):
+            chip = self.at.chip - way * dist
+            near = chip >= 0 if way > 0 else chip < self.at.chips
+
+            @pl.when(near)
+            def _():
+                act(2 * chip + self.at.core, way)
+
+    def step(self, dist, extra=None):
+        def act(block, way):
+            self.to_core(block).wait_recv()
+
+            @pl.when(self.ends(way))
+            def _():
+                self.to_line(block, way).start()
+
+            self.to_core(block).start()
+            if extra is not None:
+                extra(block)
+
+        self.arrivals(dist, act)
+
+    def finish(self):
+        self.local.wait()
+        self.to_core(self.at.col, self.src).wait_send()
+        for way in (1, -1):
+
+            @pl.when(self.ends(way))
+            def _():
+                self.to_line(self.at.col, way, self.src).wait_send()
+
+        def act(block, way):
+            self.to_core(block).wait_send()
+
+            @pl.when(self.ends(way))
+            def _():
+                self.to_line(block, way).wait_send()
+
+        for dist in range(1, self.at.chips):
+            self.arrivals(dist, act)
+        for chip in range(self.at.chips):
+            self.to_core(2 * chip + 1 - self.at.core).wait_recv()
+
+
+def gather_sems(cols_n):
+    return [
+        pltpu.SemaphoreType.DMA((cols_n,)),
+        pltpu.SemaphoreType.DMA((cols_n, 2)),
+        pltpu.SemaphoreType.DMA((cols_n,)),
+        pltpu.SemaphoreType.DMA,
+    ]
+
+
+ANY = pl.BlockSpec(memory_space=pl.ANY)
+
+
+def line_gather(arrays, collective_id, rows_n, cols_n):
+    n = len(arrays)
+
+    def kernel(*refs):
+        srcs, dsts, sems = refs[:n], refs[n : 2 * n], refs[2 * n :]
+        place = Place(rows_n, cols_n)
+        place.greet(False)
+        jobs = [
+            LineGather(place, srcs[i], dsts[i], *sems[4 * i : 4 * i + 4]) for i in range(n)
+        ]
+        for job in jobs:
+            job.start()
+        for dist in range(1, place.chips):
+            for job in jobs:
+                job.step(dist)
+        for job in jobs:
+            job.finish()
+
+    return pl.pallas_call(
+        kernel,
+        in_specs=[ANY] * n,
+        out_specs=[ANY] * n,
+        out_shape=[jax.ShapeDtypeStruct((cols_n,) + a.shape, a.dtype) for a in arrays],
+        scratch_shapes=gather_sems(cols_n) * n,
+        compiler_params=pltpu.CompilerParams(collective_id=collective_id, has_side_effects=True),
+        name="line_gather",
+    )(*arrays)
+
+
+def first_gather(bundle, cotangent, routes_t, shared, collective_id, rows_n, cols_n):
+    def kernel(
+        bundle_ref, dy_ref, rt_ref, sh_ref, full_ref, dy_all, rt_all, sh_all, *sems
+    ):
+        place = Place(rows_n, cols_n)
+        b_sems, sems = sems[:4], sems[4:]
+        d_sems, sems = sems[:4], sems[4:]
+        r_sems, sems = sems[:4], sems[4:]
+        row_send, row_core, row_recv, sh_send, sh_recv, sh_local = sems
+        place.greet(True)
+        row, col = place.row, place.col
+        weights = LineGather(place, bundle_ref, full_ref.at[row], *b_sems)
+        grads = LineGather(place, dy_ref, dy_all, *d_sems)
+        picks = LineGather(place, rt_ref, rt_all, *r_sems)
+
+        def to_row(block, step, src=None):
+            home = full_ref.at[row, block]
+            return remote(
+                home if src is None else src, home, row_send.at[block, step],
+                row_recv.at[row, block], (place.peer_row(step), col),
+            )
+
+        def push(block, src=None):
+            for step in range(1, rows_n):
+                to_row(block, step, src).start()
+
+        def from_row(other_row, block):
+            home = full_ref.at[other_row, block]
+            return remote(
+                home, home, row_core.at[other_row, block], row_recv.at[other_row, block],
+                (row, place.other),
+            )
+
+        def shared_to(step):
+            return remote(
+                sh_ref, sh_all.at[row], sh_send.at[step], sh_recv.at[row],
+                (place.peer_row(step), col),
+            )
+
+        weights.start()
+        push(col, bundle_ref)
+        shared_here = pltpu.make_async_copy(sh_ref, sh_all.at[row], sh_local)
+        shared_here.start()
+        for step in range(1, rows_n):
+            shared_to(step).start()
+        for dist in range(1, place.chips):
+            weights.step(dist, push)
+        grads.start()
+        picks.start()
+        for dist in range(1, place.chips - 1):
+            grads.step(dist)
+            picks.step(dist)
+        for step in range(1, rows_n):
+            other_row = place.peer_row(step)
+
+            @pl.loop(0, place.chips)
+            def _(chip):
+                copy = from_row(other_row, 2 * chip + place.core)
+                copy.wait_recv()
+                copy.start()
+
+        grads.step(place.chips - 1)
+        picks.step(place.chips - 1)
+        weights.finish()
+        grads.finish()
+        picks.finish()
+        shared_here.wait()
+        for step in range(1, rows_n):
+            other_row = place.peer_row(step)
+            shared_to(step).wait_send()
+            remote(
+                sh_ref, sh_all.at[other_row], sh_send.at[0], sh_recv.at[other_row],
+                (other_row, col),
+            ).wait_recv()
+
+            @pl.loop(0, place.chips)
+            def _(chip):
+                to_row(2 * chip + place.core, step).wait_send()
+                from_row(other_row, 2 * chip + place.core).wait_send()
+                from_row(other_row, 2 * chip + 1 - place.core).wait_recv()
+
+    return pl.pallas_call(
+        kernel,
+        in_specs=[ANY] * 4,
+        out_specs=[ANY] * 4,
+        out_shape=[
+            jax.ShapeDtypeStruct((rows_n, cols_n) + bundle.shape, bundle.dtype),
+            jax.ShapeDtypeStruct((cols_n,) + cotangent.shape, cotangent.dtype),
+            jax.ShapeDtypeStruct((cols_n,) + routes_t.shape, routes_t.dtype),
+            jax.ShapeDtypeStruct((rows_n,) + shared.shape, shared.dtype),
+        ],
+        scratch_shapes=gather_sems(cols_n) * 3
+        + [
+            pltpu.SemaphoreType.DMA((cols_n, rows_n)),
+            pltpu.SemaphoreType.DMA((rows_n, cols_n)),
+            pltpu.SemaphoreType.DMA((rows_n, cols_n)),
+            pltpu.SemaphoreType.DMA((rows_n,)),
+            pltpu.SemaphoreType.DMA((rows_n,)),
+            pltpu.SemaphoreType.DMA,
+        ],
+        compiler_params=pltpu.CompilerParams(collective_id=collective_id, has_side_effects=True),
+        name="first_gather",
+    )(bundle, cotangent, routes_t, shared)
+
+
+def line_sum_loop(place, mine, recv, send_sems, recv_sems, parts, ready):
+    chips, here = place.chips, place.chip
+    rows = mine.shape[1] // parts
+    items = (chips - 1) * parts
+
+    def copy(chip, part, way):
+        span = pl.ds(part * rows, rows)
+        goal = here + way
+        land = chip if way > 0 else jnp.where(chip == goal, chips, chip)
+        return remote(
+            mine.at[chip, span],
+            recv.at[land, span],
+            send_sems.at[chip, part],
+            recv_sems.at[land, part],
+            (place.row, place.col + 2 * way),
+        )
+
+    def incoming(land, part):
+        span = pl.ds(part * rows, rows)
+        return remote(
+            mine.at[0, span], recv.at[land, span], send_sems.at[0, part],
+            recv_sems.at[land, part], (place.row, place.other),
+        )
+
+    def handle(chip, part, way):
+        @pl.when(part == 0)
+        def _():
+            ready(chip)
+
+        span = pl.ds(part * rows, rows)
+        comes = here > 0 if way > 0 else here < chips - 1
+
+        @pl.when(comes)
+        def _():
+            incoming(chip, part).wait_recv()
+            total = mine[chip, span].astype(F32) + recv[chip, span].astype(F32)
+            mine[chip, span] = total.astype(mine.dtype)
+
+        copy(chip, part, way).start()
+
+    lag = 2 * (chips - 2 - here)
+
+    @pl.loop(0, items + 2 * (chips - 2))
+    def _(at):
+        up = jnp.minimum(at, items - 1)
+        up_chip = chips - 1 - lax.div(up, parts)
+
+        @pl.when((at < items) & (up_chip > here))
+        def _():
+            handle(up_chip, lax.rem(up, parts), 1)
+
+        down = at - jnp.maximum(lag, 0)
+        safe = jnp.clip(down, 0, items - 1)
+        down_chip = lax.div(safe, parts)
+
+        @pl.when((down >= 0) & (down < items) & (down_chip < here))
+        def _():
+            handle(down_chip, lax.rem(safe, parts), -1)
+
+    ready(here)
+
+    def result(part, store):
+        span = pl.ds(part * rows, rows)
+        total = mine[here, span].astype(F32)
+
+        @pl.when((here > 0) & (here < chips - 1))
+        def _():
+            incoming(here, part).wait_recv()
+            incoming(chips, part).wait_recv()
+            store(span, total + recv[here, span].astype(F32) + recv[chips, span].astype(F32))
+
+        @pl.when((here > 0) & (here == chips - 1))
+        def _():
+            incoming(here, part).wait_recv()
+            store(span, total + recv[here, span].astype(F32))
+
+        @pl.when((here == 0) & (here < chips - 1))
+        def _():
+            incoming(chips, part).wait_recv()
+            store(span, total + recv[chips, span].astype(F32))
+
+    def drain():
+        @pl.loop(0, chips)
+        def _(chip):
+            for part in range(parts):
+
+                @pl.when(chip > here)
+                def _():
+                    copy(chip, part, 1).wait_send()
+
+                @pl.when(chip < here)
+                def _():
+                    copy(chip, part, -1).wait_send()
+
+    return result, drain
+
+
+LINE_PARTS = 4
+
+
+def line_sum(parts_all, collective_id, rows_n, cols_n):
+    chips = cols_n // 2
+    block = parts_all.shape[2:]
+
+    def kernel(
+        in_ref, out_ref, mine, extra, recv, load_sems, core_send, core_recv, send_sems, recv_sems
+    ):
+        place = Place(rows_n, cols_n)
+
+        def load(chip):
+            return pltpu.make_async_copy(
+                in_ref.at[place.core, chip], mine.at[chip], load_sems.at[chip]
+            )
+
+        def swap(chip):
+            return remote(
+                in_ref.at[1 - place.core, chip], extra.at[chip], core_send.at[chip],
+                core_recv.at[chip], (place.row, place.other),
+            )
+
+        order = []
+        for i in range((chips + 1) // 2):
+            order += [chips - 1 - i, i] if chips - 1 - i != i else [i]
+        for chip in order:
+            load(chip).start()
+        place.greet(False)
+        for chip in order:
+            swap(chip).start()
+
+        def ready(chip):
+            load(chip).wait()
+            swap(chip).wait_recv()
+            rows = block[0] // LINE_PARTS
+            for part in range(LINE_PARTS):
+                span = pl.ds(part * rows, rows)
+                mine[chip, span] = (
+                    mine[chip, span].astype(F32) + extra[chip, span].astype(F32)
+                ).astype(mine.dtype)
+
+        result, drain = line_sum_loop(
+            place, mine, recv, send_sems, recv_sems, LINE_PARTS, ready
+        )
+
+        def store(span, value):
+            out_ref[span] = value
+
+        for part in range(LINE_PARTS):
+            result(part, store)
+        drain()
+        for chip in range(chips):
+            swap(chip).wait_send()
+
+    return pl.pallas_call(
+        kernel,
+        in_specs=[ANY],
+        out_specs=pl.BlockSpec(memory_space=pltpu.VMEM),
+        out_shape=jax.ShapeDtypeStruct(block, F32),
+        scratch_shapes=[
+            pltpu.VMEM((chips,) + block, BF),
+            pltpu.VMEM((chips,) + block, BF),
+            pltpu.VMEM((chips + 1,) + block, BF),
+            pltpu.SemaphoreType.DMA((chips,)),
+            pltpu.SemaphoreType.DMA((chips,)),
+            pltpu.SemaphoreType.DMA((chips,)),
+            pltpu.SemaphoreType.DMA((chips, LINE_PARTS)),
+            pltpu.SemaphoreType.DMA((chips + 1, LINE_PARTS)),
+        ],
+        compiler_params=pltpu.CompilerParams(
+            collective_id=collective_id, has_side_effects=True,
+            vmem_limit_bytes=58 * 1024 * 1024,
+        ),
+        name="line_sum",
+    )(parts_all)
+
+
+def dense_sum(grads, shared, collective_id, rows_n, cols_n):
+    chips = cols_n // 2
+    block = grads.shape[3:]
+
+    def kernel(
+        in_ref, sh_ref, out_ref, sh_out, mine, extra, rows_in, recv, sh_in,
+        load_sem, core_send, core_recv, row_send, row_recv, send_sems, recv_sems,
+        sh_send, sh_recv, sh_local,
+    ):
+        place = Place(rows_n, cols_n)
+        row, col = place.row, place.col
+        load = pltpu.make_async_copy(in_ref.at[place.core], mine, load_sem)
+        load.start()
+        shared_here = pltpu.make_async_copy(sh_ref.at[row], sh_in.at[row], sh_local)
+        shared_here.start()
+        place.greet(True)
+        swap = remote(
+            in_ref.at[1 - place.core], extra, core_send, core_recv, (row, place.other)
+        )
+        swap.start()
+
+        def shared_to(step):
+            goal = place.peer_row(step)
+            return remote(
+                sh_ref.at[goal], sh_in.at[row], sh_send.at[step], sh_recv.at[row], (goal, col)
+            )
+
+        def shared_from(step):
+            source = place.peer_row(step)
+            return remote(
+                sh_ref.at[source], sh_in.at[source], sh_send.at[0], sh_recv.at[source],
+                (source, col),
+            )
+
+        def to_row(step, chip):
+            goal = place.peer_row(step)
+            return remote(
+                mine.at[goal, chip], rows_in.at[row, chip], row_send.at[step, chip],
+                row_recv.at[row, chip], (goal, col),
+            )
+
+        def from_row(step, chip):
+            source = place.peer_row(step)
+            return remote(
+                mine.at[source, chip], rows_in.at[source, chip], row_send.at[0, chip],
+                row_recv.at[source, chip], (source, col),
+            )
+
+        load.wait()
+        swap.wait_recv()
+        order = []
+        for i in range((chips + 1) // 2):
+            order += [chips - 1 - i, i] if chips - 1 - i != i else [i]
+        for chip in order:
+            for step in range(1, rows_n):
+                goal = place.peer_row(step)
+                mine[goal, chip] = (
+                    mine[goal, chip].astype(F32) + extra[goal, chip].astype(F32)
+                ).astype(mine.dtype)
+                to_row(step, chip).start()
+        for step in range(1, rows_n):
+            shared_to(step).start()
+
+        def ready(chip):
+            total = mine[row, chip].astype(F32) + extra[row, chip].astype(F32)
+            for step in range(1, rows_n):
+                from_row(step, chip).wait_recv()
+                total = total + rows_in[place.peer_row(step), chip].astype(F32)
+            mine[row, chip] = total.astype(mine.dtype)
+
+        result, drain = line_sum_loop(
+            place, mine.at[row], recv, send_sems, recv_sems, 1, ready
+        )
+
+        def store(span, value):
+            out_ref[span] = value
+
+        result(0, store)
+        shared_here.wait()
+        for step in range(1, rows_n):
+            shared_from(step).wait_recv()
+        total = sh_in[0].astype(F32)
+        for other in range(1, rows_n):
+            total = total + sh_in[other].astype(F32)
+        sh_out[...] = total
+        drain()
+        swap.wait_send()
+        for step in range(1, rows_n):
+            shared_to(step).wait_send()
+            for chip in range(chips):
+                to_row(step, chip).wait_send()
+
+    vmem = pl.BlockSpec(memory_space=pltpu.VMEM)
+    return pl.pallas_call(
+        kernel,
+        in_specs=[ANY, ANY],
+        out_specs=[vmem, vmem],
+        out_shape=[
+            jax.ShapeDtypeStruct(block, F32),
+            jax.ShapeDtypeStruct(shared.shape[1:], F32),
+        ],
+        scratch_shapes=[
+            pltpu.VMEM((rows_n, chips) + block, BF),
+            pltpu.VMEM((rows_n, chips) + block, BF),
+            pltpu.VMEM((rows_n, chips) + block, BF),
+            pltpu.VMEM((chips + 1,) + block, BF),
+            pltpu.VMEM(shared.shape, BF),
+            pltpu.SemaphoreType.DMA,
+            pltpu.SemaphoreType.DMA,
+            pltpu.SemaphoreType.DMA,
+            pltpu.SemaphoreType.DMA((rows_n, chips)),
+            pltpu.SemaphoreType.DMA((rows_n, chips)),
+            pltpu.SemaphoreType.DMA((chips, 1)),
+            pltpu.SemaphoreType.DMA((chips + 1, 1)),
+            pltpu.SemaphoreType.DMA((rows_n,)),
+            pltpu.SemaphoreType.DMA((rows_n,)),
+            pltpu.SemaphoreType.DMA,
+        ],
+        compiler_params=pltpu.CompilerParams(
+            collective_id=collective_id, has_side_effects=True,
+            vmem_limit_bytes=58 * 1024 * 1024,
+        ),
+        name="dense_sum",
+    )(grads, shared)
+
+
+def routed_kernel(
+    x_ref, dy_ref, routes_ref, gates_ref, rank_ref, rank_t_ref, eg_ref, eu_ref, ed_ref,
+    sgu_ref, sd_ref,
+    out_hbm, gx_hbm, xs_hbm, dys_hbm, hid_ref, gg_ref, gu_ref, ggw_ref, shared_ref,
+    xs, dys, pick, wide_out, wide_gx, slot_gate, slot_ggw, stage, slot_sems, stage_sems,
+):
+    unit = pl.program_id(0)
+    units_n = pl.num_programs(0)
+    total = x_ref.shape[1]
+    cap = xs.shape[1] // 2
+    hidden_units = sd_ref.shape[0]
+    first = lax.axis_index("col") * EXP_DEV
+    slots = pl.ds(unit * 2 * cap, 2 * cap)
+    spans = [slice(at, at + 512) for at in range(0, x_ref.shape[2], 512)]
+
+    def slot_copy(which):
+        src, dst = ((xs, xs_hbm), (dys, dys_hbm))[which]
+        return pltpu.make_async_copy(src, dst.at[:, slots], slot_sems.at[which])
+
+    def stage_copy(which, core):
+        dst = (out_hbm, gx_hbm)[which]
+        return pltpu.make_async_copy(
+            stage.at[which], dst.at[core, unit], stage_sems.at[which]
+        )
+
+    @pl.when(unit > 0)
+    def _():
+        slot_copy(0).wait()
+        slot_copy(1).wait()
+
+    for core in range(2):
+        gate_rows = gates_ref[core]
+        route_rows = routes_ref[core]
+        for e in range(EXP_DEV):
+            at = lax.broadcasted_iota(jnp.int32, (cap, total), 0)
+            here = at == rank_ref[core, e : e + 1, :]
+            gate_row = jnp.sum(
+                jnp.where(route_rows == first + e, gate_rows, 0.0), axis=0, keepdims=True
+            )
+            slot_gate[e, core * cap : (core + 1) * cap, :] = jnp.sum(
+                jnp.where(here, gate_row, 0.0), axis=1, keepdims=True
+            )
+            pick[core, e * cap : (e + 1) * cap, :] = jnp.where(here, 1.0, 0.0).astype(BF)
+        for src, dst in ((x_ref, xs), (dy_ref, dys)):
+            for cols in spans:
+                got = mm(pick[core], src[core, :, cols]).astype(BF)
+                for e in range(EXP_DEV):
+                    dst[e, core * cap : (core + 1) * cap, cols] = got[e * cap : (e + 1) * cap]
+    slot_copy(0).start()
+    slot_copy(1).start()
+
+    @pl.loop(0, EXP_DEV)
+    def _(e):
+        rows_x = xs[e]
+        gate_part = mm(rows_x, eg_ref[e])
+        up_part = mm(rows_x, eu_ref[e])
+        act, slope = silu_parts(gate_part)
+        grad_hidden = mm_nt(dys[e], ed_ref[e])
+        hidden = (act * up_part).astype(BF).astype(F32)
+        weight = slot_gate[e]
+        gated = (hidden * weight).astype(BF)
+        hid_ref[e] = gated
+        slot_ggw[e] = jnp.sum(hidden * grad_hidden, axis=1, keepdims=True)
+        grad_hidden = grad_hidden * weight
+        geg = (grad_hidden * up_part * slope).astype(BF)
+        geu = (grad_hidden * act).astype(BF)
+        gg_ref[e] = geg
+        gu_ref[e] = geu
+        rows = pl.ds(pl.multiple_of(e * cap, cap), cap)
+        for cols in spans:
+            made = mm(gated, ed_ref[e, :, cols]).astype(BF)
+            back = (mm_nt(geg, eg_ref[e, cols, :]) + mm_nt(geu, eu_ref[e, cols, :])).astype(BF)
+            for core in range(2):
+                wide_out[core, rows, cols] = made[core * cap : (core + 1) * cap]
+                wide_gx[core, rows, cols] = back[core * cap : (core + 1) * cap]
+
+    ggw_ref[...] = jnp.zeros_like(ggw_ref)
+    for core in range(2):
+        for e in range(EXP_DEV):
+            here = pick[core, e * cap : (e + 1) * cap, :].astype(F32)
+            ggw_ref[core, e : e + 1, :] = jnp.sum(
+                here * slot_ggw[e, core * cap : (core + 1) * cap, :], axis=0, keepdims=True
+            )
+        at = lax.broadcasted_iota(jnp.int32, (total, cap), 1)
+        back_pick = jnp.concatenate(
+            [
+                jnp.where(at == rank_t_ref[core, :, e : e + 1], 1.0, 0.0).astype(BF)
+                for e in range(EXP_DEV)
+            ],
+            axis=1,
+        )
+        both = mm(x_ref[core], sgu_ref[...])
+        s_act, s_slope = silu_parts(both[:, :hidden_units])
+        s_up = both[:, hidden_units:]
+        s_hidden = (s_act * s_up).astype(BF)
+        grad_shared = mm_nt(dy_ref[core], sd_ref[...])
+        grad_both = jnp.concatenate(
+            [(grad_shared * s_up * s_slope).astype(BF), (grad_shared * s_act).astype(BF)],
+            axis=1,
+        )
+        for which in range(2):
+            if core == 0:
+
+                @pl.when(unit > 0)
+                def _():
+                    stage_copy(which, 1).wait()
+
+            else:
+                stage_copy(which, 0).wait()
+            for cols in spans:
+                if which == 0:
+                    value = mm(back_pick, wide_out[core, :, cols])
+                    value = value + mm(s_hidden, sd_ref[:, cols])
+                else:
+                    value = mm(back_pick, wide_gx[core, :, cols])
+                    value = value + mm_nt(grad_both, sgu_ref[cols, :])
+                stage[which, :, cols] = value.astype(BF)
+            stage_copy(which, core).start()
+        if core == 0:
+
+            @pl.when(unit == 0)
+            def _():
+                shared_ref[...] = jnp.zeros_like(shared_ref)
+
+        for cols in spans:
+            shared_ref[cols, : 2 * hidden_units] += mm_tn(x_ref[core, :, cols], grad_both)
+            shared_ref[cols, 2 * hidden_units :] += mm_tn(dy_ref[core, :, cols], s_hidden)
+
+    @pl.when(unit == units_n - 1)
+    def _():
+        slot_copy(0).wait()
+        slot_copy(1).wait()
+        stage_copy(0, 1).wait()
+        stage_copy(1, 1).wait()
+
+
+def routed(x_all, dy_all, routes_all, gates_all, rank, egate, eup, edown, sgu, sdown):
+    cols_n, total, width = x_all.shape
+    chips = cols_n // 2
+    cap = 4 * total * TOP // (3 * EXP_DEV * cols_n)
+    slots = 2 * cap
+    ffn = egate.shape[2]
+    hidden_units = sdown.shape[0]
+    rank_t = jnp.swapaxes(rank, 1, 2)
+
+    def per_unit(*shape):
+        return pl.BlockSpec(shape, lambda q: (q,) + (0,) * (len(shape) - 1))
+
+    def whole(a):
+        return pl.BlockSpec(
+            a.shape, lambda q: (0,) * a.ndim, pipeline_mode=pl.Buffered(1)
+        )
+
+    slot_block = pl.BlockSpec(
+        (EXP_DEV, slots, ffn), lambda q: (0, q, 0), pipeline_mode=pl.Buffered(1)
+    )
+    small = per_unit(2, 8, total)
+    return pl.pallas_call(
+        routed_kernel,
+        grid=(chips,),
+        in_specs=[
+            per_unit(2, total, width), per_unit(2, total, width), small, small, small,
+            per_unit(2, total, 8), whole(egate), whole(eup), whole(edown), whole(sgu),
+            whole(sdown),
+        ],
+        out_specs=[
+            ANY, ANY, ANY, ANY, slot_block, slot_block, slot_block, small,
+            pl.BlockSpec(
+                (width, 3 * hidden_units), lambda q: (0, 0), pipeline_mode=pl.Buffered(1)
+            ),
+        ],
+        out_shape=[
+            jax.ShapeDtypeStruct((2, chips, total, width), BF),
+            jax.ShapeDtypeStruct((2, chips, total, width), BF),
+            jax.ShapeDtypeStruct((EXP_DEV, cols_n * cap, width), BF),
+            jax.ShapeDtypeStruct((EXP_DEV, cols_n * cap, width), BF),
+            jax.ShapeDtypeStruct((EXP_DEV, cols_n * cap, ffn), BF),
+            jax.ShapeDtypeStruct((EXP_DEV, cols_n * cap, ffn), BF),
+            jax.ShapeDtypeStruct((EXP_DEV, cols_n * cap, ffn), BF),
+            jax.ShapeDtypeStruct((cols_n, 8, total), F32),
+            jax.ShapeDtypeStruct((width, 3 * hidden_units), F32),
+        ],
+        scratch_shapes=[
+            pltpu.VMEM((EXP_DEV, slots, width), BF),
+            pltpu.VMEM((EXP_DEV, slots, width), BF),
+            pltpu.VMEM((2, EXP_DEV * cap, total), BF),
+            pltpu.VMEM((2, EXP_DEV * cap, width), BF),
+            pltpu.VMEM((2, EXP_DEV * cap, width), BF),
+            pltpu.VMEM((EXP_DEV, slots, 1), F32),
+            pltpu.VMEM((EXP_DEV, slots, 1), F32),
+            pltpu.VMEM((2, total, width), BF),
+            pltpu.SemaphoreType.DMA((2,)),
+            pltpu.SemaphoreType.DMA((2,)),
+        ],
+        compiler_params=pltpu.CompilerParams(vmem_limit_bytes=60 * 1024 * 1024),
+        name="routed",
+    )(x_all, dy_all, routes_all, gates_all, rank, rank_t, egate, eup, edown, sgu, sdown)
+
+
+def expert_grads_kernel(xs_ref, dys_ref, hid_ref, gg_ref, gu_ref, og_ref, ou_ref, od_ref):
+    rows = xs_ref[0]
+    og_ref[0] = mm_tn(rows, gg_ref[0]).astype(BF)
+    ou_ref[0] = mm_tn(rows, gu_ref[0]).astype(BF)
+    od_ref[0] = mm_tn(hid_ref[0], dys_ref[0]).astype(BF)
+
+
+def expert_grads(xs, dys, hid, gg, gu):
+    _, slots, width = xs.shape
+    ffn = hid.shape[2]
+
+    def each(rows, cols):
+        return pl.BlockSpec((1, rows, cols), lambda e: (e, 0, 0))
+
+    return pl.pallas_call(
+        expert_grads_kernel,
+        grid=(EXP_DEV,),
+        in_specs=[each(slots, width)] * 2 + [each(slots, ffn)] * 3,
+        out_specs=[each(width, ffn), each(width, ffn), each(ffn, width)],
+        out_shape=[
+            jax.ShapeDtypeStruct((EXP_DEV, width, ffn), BF),
+            jax.ShapeDtypeStruct((EXP_DEV, width, ffn), BF),
+            jax.ShapeDtypeStruct((EXP_DEV, ffn, width), BF),
+        ],
+        compiler_params=pltpu.CompilerParams(vmem_limit_bytes=60 * 1024 * 1024),
+        name="expert_grads",
+    )(xs, dys, hid, gg, gu)
 
 
 def on_device(
@@ -177,13 +990,23 @@
     total = tokens.shape[0]
     width = MODEL_WIDTH
     experts = EXP_DEV * cols_n
-    cap = 4 * total * TOP // (3 * experts)
 
     q_w, k_w = w_query.shape[1], key_projection.shape[1]
-    bundle = jnp.concatenate([w_query.T, key_projection.T, value_projection.T, w_out.T], axis=0)
-    full = lax.all_gather(bundle, both, axis=0).reshape(
-        (rows_n, cols_n) + bundle.shape
+    inner = w_query.shape[0]
+    gains = jnp.stack([g_attn, g_moe])
+    gains = jnp.pad(gains, ((0, 0), (0, inner - gains.shape[1])))
+    tail = jnp.concatenate([w_router.T, gains], axis=0)
+    tail = jnp.pad(tail, ((0, 16 - tail.shape[0]), (0, 0)))
+    bundle = jnp.concatenate(
+        [w_query.T, key_projection.T, value_projection.T, w_out.T, tail], axis=0
     )
+    routes_t = jnp.pad(routes.T, ((0, 8 - TOP), (0, 0)), constant_values=-1)
+    units = s_gate.shape[1]
+    shared = jnp.concatenate([s_gate, s_up], axis=1)
+    full, dy_all, routes_all, sgu = first_gather(
+        bundle, cotangent, routes_t, shared, 0, rows_n, cols_n
+    )
+    sgu = sgu.reshape(width, 2 * units)
 
     def piece(lo, extent):
         part = full[:, :, lo : lo + extent]
@@ -193,25 +1016,25 @@
     wk_t = piece(q_w, k_w)
     wv_t = piece(q_w + k_w, k_w)
     wo_t = piece(q_w + 2 * k_w, q_w)
-    gain_attn = lax.all_gather(g_attn, both, axis=0, tiled=True).astype(F32)
-    gain_moe = lax.all_gather(g_moe, both, axis=0, tiled=True).astype(F32)
-    router = lax.all_gather(
-        lax.all_gather(w_router, "col", axis=1, tiled=True), "row", axis=0, tiled=True
-    )
+    t_at = 2 * q_w + 2 * k_w
+    router_t = piece(t_at, EXP_DEV)
+    n_gain = g_attn.shape[0]
+    gain_attn = full[:, :, t_at + EXP_DEV, :n_gain].reshape(width).astype(F32)
+    gain_moe = full[:, :, t_at + EXP_DEV + 1, :n_gain].reshape(width).astype(F32)
     egate = lax.all_gather(e_gate, "row", axis=1, tiled=True)
     eup = lax.all_gather(e_up, "row", axis=1, tiled=True)
     edown = lax.all_gather(e_down, "row", axis=2, tiled=True)
-    sgate = lax.all_gather(s_gate, "row", axis=0, tiled=True)
-    sup = lax.all_gather(s_up, "row", axis=0, tiled=True)
-    units = s_gate.shape[1]
     per_row = s_down.shape[0] // units
     sdown_cols = lax.all_gather(s_down, "col", axis=1, tiled=True)
     sdown_mine = lax.dynamic_slice_in_dim(sdown_cols, (col_here % per_row) * units, units, 0)
     sdown = lax.dynamic_index_in_dim(
         lax.all_gather(sdown_mine, "row", axis=0), col_here // per_row, 0, keepdims=False
     )
-    dy_all = lax.all_gather(cotangent, "col", axis=0)
-    routes_all = lax.all_gather(routes, "col", axis=0)
+
+    mine = col_here * EXP_DEV + jnp.arange(EXP_DEV, dtype=jnp.int32)
+    hit = jnp.any(routes_all[:, None, :TOP, :] == mine[None, :, None, None], axis=2)
+    rank = jnp.where(hit, jnp.cumsum(hit.astype(jnp.int32), axis=2) - 1, -1)
+    rank = jnp.pad(rank, ((0, 0), (0, 8 - EXP_DEV), (0, 0)), constant_values=-1)
 
     own_lens = lengths[deal.reshape(-1) * cols_n + col_here, row_here]
     seq_ends = jnp.cumsum(own_lens)
@@ -230,7 +1053,7 @@
     scale_two = rms_scale(after_attn)
     unit_two = after_attn * scale_two
     normed_two = (unit_two * gain_moe).astype(BF)
-    logits = mm(normed_two, router)
+    logits = mm_nt(normed_two, router_t)
     route_picks = (
         routes[:, :, None] == jnp.arange(experts, dtype=jnp.int32)[None, None, :]
     ).astype(F32)
@@ -238,55 +1061,15 @@
     gate_raw = jnp.exp(chosen - jnp.max(chosen, axis=-1, keepdims=True))
     gate_weights = gate_raw / jnp.sum(gate_raw, axis=-1, keepdims=True)
 
-    x_all = lax.all_gather(normed_two, "col", axis=0)
-    gates_all = lax.all_gather(gate_weights, "col", axis=0)
-    mine = col_here * EXP_DEV + jnp.arange(EXP_DEV, dtype=jnp.int32)
-    hits = routes_all[:, :, :, None] == mine
-    hit = jnp.any(hits, axis=2)
-    gate = jnp.sum(jnp.where(hits, gates_all[:, :, :, None], 0.0), axis=2)
-    rank = jnp.where(hit, jnp.cumsum(hit.astype(jnp.int32), axis=1) - 1, -1)
-    rank = rank.transpose(0, 2, 1)
-    gate = gate.transpose(0, 2, 1)
-    pick = rank[:, :, None, :] == jnp.arange(cap, dtype=jnp.int32)[None, None, :, None]
-    slot_gate = jnp.sum(jnp.where(pick, gate[:, :, None, :], 0.0), axis=-1)
-    pick_b = pick.astype(BF)
-    xs = ein("sept,std->sepd", pick_b, x_all).astype(BF)
-    dys = ein("sept,std->sepd", pick_b, dy_all).astype(BF)
-    gate_part = ein("sepd,edf->sepf", xs, egate)
-    up_part = ein("sepd,edf->sepf", xs, eup)
-    act, slope = silu_parts(gate_part)
-    hidden_f = (act * up_part).astype(BF).astype(F32)
-    gated_hidden = (hidden_f * slot_gate[..., None]).astype(BF)
-    weighted = ein("sepf,efd->sepd", gated_hidden, edown).astype(BF)
-    out_part = ein("sept,sepd->std", pick_b, weighted)
-    grad_hidden = ein("sepd,efd->sepf", dys, edown)
-    slot_ggw = jnp.sum(hidden_f * grad_hidden, axis=-1)
-    ggw = jnp.sum(jnp.where(pick, slot_ggw[..., None], 0.0), axis=2)
-    grad_hidden = grad_hidden * slot_gate[..., None]
-    geg = (grad_hidden * up_part * slope).astype(BF)
-    geu = (grad_hidden * act).astype(BF)
-    grad_edown = ein("sepf,sepd->efd", gated_hidden, dys)
-    grad_egate = ein("sepd,sepf->edf", xs, geg)
-    grad_eup = ein("sepd,sepf->edf", xs, geu)
-    grad_in = (ein("sepf,edf->sepd", geg, egate) + ein("sepf,edf->sepd", geu, eup)).astype(BF)
-    gx_part = ein("sept,sepd->std", pick_b, grad_in)
-    x_flat = x_all.reshape(cols_n * total, width)
-    dy_flat = dy_all.reshape(cols_n * total, width)
-    s_act, s_slope = silu_parts(mm(x_flat, sgate))
-    s_upv = mm(x_flat, sup)
-    s_hidden = (s_act * s_upv).astype(BF)
-    gsh = mm_nt(dy_flat, sdown)
-    gsg = (gsh * s_upv * s_slope).astype(BF)
-    gsu = (gsh * s_act).astype(BF)
-    out_part = out_part + mm(s_hidden, sdown).reshape(out_part.shape)
-    gx_part = gx_part + (mm_nt(gsg, sgate) + mm_nt(gsu, sup)).reshape(gx_part.shape)
-    grad_sgate = mm_tn(x_flat, gsg)
-    grad_sup = mm_tn(x_flat, gsu)
-    grad_sdown = mm_tn(s_hidden, dy_flat)
-
-    gx = lax.psum_scatter(gx_part.astype(BF), "col", scatter_dimension=0)
-    moe = lax.psum_scatter(out_part.astype(BF), "col", scatter_dimension=0)
-    output = (after_attn + moe.astype(F32)).astype(BF)
+    gates_t = jnp.pad(gate_weights.T, ((0, 8 - TOP), (0, 0)))
+    x_all, gates_all = line_gather([normed_two, gates_t], 1, rows_n, cols_n)
+    out_part, gx_part, xs, dys, hid, gg, gu, ggw, grad_sh = routed(
+        x_all, dy_all, routes_all, gates_all, rank, egate, eup, edown, sgu, sdown
+    )
+    grad_egate, grad_eup, grad_edown = expert_grads(xs, dys, hid, gg, gu)
+    ggw = ggw[:, :EXP_DEV]
+
+    gx = line_sum(gx_part, 2, rows_n, cols_n)
     ggw_home = lax.all_to_all(ggw, "col", split_axis=0, concat_axis=0, tiled=True)
     ggw_home = ggw_home.reshape(experts, total).T
 
@@ -295,8 +1078,8 @@
         grad_gates - jnp.sum(gate_weights * grad_gates, axis=-1, keepdims=True)
     )
     grad_logits = jnp.sum(route_picks * grad_chosen[:, :, None], axis=1).astype(BF)
-    grad_router = mm_tn(normed_two, grad_logits)
-    grad_normed_two = gx.astype(F32) + mm_nt(grad_logits, router)
+    grad_router = mm_tn(grad_logits, normed_two)
+    grad_normed_two = gx + mm(grad_logits, router_t)
     grad_two, grad_gain_moe = norm_back(grad_normed_two, unit_two, scale_two, gain_moe)
     grad_after = cotangent.astype(F32) + grad_two
     grad_attn_b = grad_after.astype(BF)
@@ -310,28 +1093,49 @@
     grad_one, grad_gain_attn = norm_back(grad_normed_one, unit_one, scale_one, gain_attn)
     grad_tokens = grad_after + grad_one
 
+    moe = line_sum(out_part, 3, rows_n, cols_n)
+    output = (after_attn + moe).astype(BF)
+
     def cut(grad):
-        part = grad.reshape(cols_n, grad.shape[0] // cols_n, rows_n, width // rows_n)
-        return part.transpose(2, 0, 1, 3)
-
-    grads = jnp.concatenate(
-        [cut(grad_wq), cut(grad_wk), cut(grad_wv), cut(grad_wout)], axis=2
-    ).astype(BF)
-    grads = lax.psum_scatter(
-        grads.reshape((rows_n * cols_n,) + bundle.shape), both, scatter_dimension=0
-    ).astype(F32)
-    out_wq = grads[:q_w].T
-    out_wk = grads[q_w : q_w + k_w].T
-    out_wv = grads[q_w + k_w : q_w + 2 * k_w].T
-    out_wo = grads[q_w + 2 * k_w :].T
-    out_g_attn = lax.psum_scatter(grad_gain_attn, both, scatter_dimension=0, tiled=True)
-    out_g_moe = lax.psum_scatter(grad_gain_moe, both, scatter_dimension=0, tiled=True)
-    out_router = lax.psum_scatter(
-        lax.psum_scatter(grad_router, "col", scatter_dimension=1, tiled=True),
-        "row",
-        scatter_dimension=0,
-        tiled=True,
-    )
+        extent = grad.shape[0] // cols_n
+        part = grad.astype(BF).reshape(cols_n // 2, 2, extent, rows_n, inner)
+        return part.transpose(1, 3, 0, 2, 4)
+
+    def cut_gain(grad):
+        part = grad.astype(BF).reshape(rows_n, cols_n // 2, 2, 1, n_gain)
+        part = jnp.pad(part, ((0, 0),) * 4 + ((0, inner - n_gain),))
+        return part.transpose(2, 0, 1, 3, 4)
+
+    grads = [cut(grad_wq), cut(grad_wk), cut(grad_wv), cut(grad_wout), cut(grad_router)]
+    grads += [cut_gain(grad_gain_attn), cut_gain(grad_gain_moe)]
+    blank = 16 - EXP_DEV - 2
+    grads.append(jnp.zeros((2, rows_n, cols_n // 2, blank, inner), BF))
+    grads = jnp.concatenate(grads, axis=3)
+    grads_sh = grad_sh.astype(BF).reshape(rows_n, inner, 3 * units)
+    dense, dense_sh = dense_sum(grads, grads_sh, 4, rows_n, cols_n)
+    out_wq = dense[:q_w].T
+    out_wk = dense[q_w : q_w + k_w].T
+    out_wv = dense[q_w + k_w : q_w + 2 * k_w].T
+    out_wo = dense[q_w + 2 * k_w : t_at].T
+    out_router = dense[t_at : t_at + EXP_DEV].T
+    out_g_attn = dense[t_at + EXP_DEV, :n_gain]
+    out_g_moe = dense[t_at + EXP_DEV + 1, :n_gain]
+    out_sg = dense_sh[:, :units]
+    out_su = dense_sh[:, units : 2 * units]
+    sd_rows = dense_sh[:, 2 * units :].astype(BF).reshape(per_row, inner // per_row, units)
+    lands = []
+    for turn in range(per_row):
+        moves = [
+            (rr * cols_n + cc, (cc // per_row) * cols_n + per_row * rr + (cc + turn) % per_row)
+            for rr in range(rows_n)
+            for cc in range(cols_n)
+        ]
+        part = lax.dynamic_index_in_dim(sd_rows, (col_here + turn) % per_row, 0, keepdims=False)
+        lands.append(lax.ppermute(part, ("row", "col"), moves))
+    lands = jnp.stack(lands)
+    turns = (col_here - jnp.arange(per_row, dtype=jnp.int32)) % per_row
+    out_sd = jnp.take(lands, turns, axis=0).transpose(0, 2, 1)
+    out_sd = out_sd.reshape(per_row * units, inner // per_row).astype(F32)
 
     def row_sum(grad, dim):
         return lax.psum_scatter(
@@ -341,13 +1145,6 @@
     out_eg = row_sum(grad_egate, 1)
     out_eu = row_sum(grad_eup, 1)
     out_ed = row_sum(grad_edown, 2)
-    out_sg = row_sum(grad_sgate, 0)
-    out_su = row_sum(grad_sup, 0)
-    sd_sum = lax.psum(grad_sdown.astype(BF), "row")
-    sd_parts = sd_sum.reshape(units, cols_n, width // cols_n).transpose(1, 0, 2)
-    sd_home = lax.all_to_all(sd_parts, "col", split_axis=0, concat_axis=0, tiled=True)
-    out_sd = lax.dynamic_slice_in_dim(sd_home, row_here * per_row, per_row, 0)
-    out_sd = out_sd.reshape(per_row * units, width // cols_n).astype(F32)
     return (
         output,
         grad_tokens,

time: 1560 us -> 1070 us (0.69)
  waiting for transfers between devices: 822 us -> 3.16 us
  Pallas kernels: 21.4 us -> 735 us
  matrix products: 328 us -> 45.2 us
  blocking collectives: 178 us -> 16 us
  local copies, waits for them, and re-layouts: 114 us -> 192 us
  other arithmetic: 67 us -> 28.6 us
    pallas_call x0 -> x7, Pallas kernels: none -> 714 us  [the longest x2 220 us: line_sum(): pl.pallas_call(kernel, in_specs=[ANY], out_specs=pl.BlockSpec(memory_spac...]
    reduce_scatter x3 -> x0, waiting for transfers between devices: 261 us -> none  [the longest x1 125 us: on_device(): moe = lax.psum_scatter(out_part.astype(BF), 'col', scatter_dimension=0)]
    dot_general x13 -> x0, matrix products: 195 us -> none  [ein(): return jnp.einsum(spec, a, b, preferred_element_type=F32)]
    reduce_scatter x4 -> x2, waiting for transfers between devices: 159 us -> 0.01 us  [row_sum(): lax.psum_scatter(grad.astype(BF), 'row', scatter_dimension=dim, tiled=True)]
    all_gather x3 -> x0, waiting for transfers between devices: 157 us -> none  [the longest x1 87.8 us: on_device(): x_all = lax.all_gather(normed_two, 'col', axis=0)]
    unnamed x2 -> x0, blocking collectives: 84 us -> none
    all_gather x6 -> x0, blocking collectives: 77.7 us -> none  [the longest x1 15.4 us: on_device(): gates_all = lax.all_gather(gate_weights, 'col', axis=0)]
    unnamed x21 -> x8, waiting for transfers between devices: 73.4 us -> 3.14 us
  transfers between devices with their start and end apart: 20 -> 10, of which waited for: 14 -> 0; matrix products, arithmetic and copies ran while one was open for 30% -> 23% of each run, Pallas kernels for 1% -> 56%
where the time goes in v2:
time: 1070 us; the launch traced here: 1060 us
  Pallas kernels  735 us (69%)
  local copies, waits for them, and re-layouts  192 us (18%)
  matrix products  45.2 us (4%)
  other arithmetic  28.6 us (3%)
  starting transfers between devices  19.9 us (2%)
  blocking collectives  16 us (1%)
  between operations  15.6 us (1%)
    pallas_call x2, Pallas kernels, line_sum(): pl.pallas_call(kernel, in_specs=[ANY], out_specs=pl.BlockSpec(memory_spac...  220 us
    pallas_call x1, Pallas kernels, first_gather(): pl.pallas_call(kernel, in_specs=[ANY] * 4, out_specs=[ANY] * 4, out_shape...  142 us
    pallas_call x1, Pallas kernels, routed(): pl.pallas_call(routed_kernel, grid=(chips,), in_specs=[per_unit(2, total,...  115 us
    pallas_call x1, Pallas kernels, line_gather(): pl.pallas_call(kernel, in_specs=[ANY] * n, out_specs=[ANY] * n, out_shape...  111 us
    pallas_call x1, Pallas kernels, dense_sum(): pl.pallas_call(kernel, in_specs=[ANY, ANY], out_specs=[vmem, vmem], out_s...  100 us
    concatenate x1, local copies, waits for them, and re-layouts, on_device(): grads = jnp.concatenate(grads, axis=3)  69.9 us
    unnamed x120, local copies, waits for them, and re-layouts  37 us
    reshape x6, local copies, waits for them, and re-layouts, cut(): part = grad.astype(BF).reshape(cols_n // 2, 2, extent, rows_n, inner)  26.6 us
  transfers between devices with their start and end apart: 10, of which 0 were waited for; matrix products, arithmetic and copies ran while one was open for 23% of the time, Pallas kernels for 56%

profile of v2, /device:TPU:2, one launch (start us, length us, event | category | flops | bytes accessed | tf_op | source)
XLA Modules:
  0.0 1055.4 jit_solution(2205735713172973519)
XLA Ops:
  7.3 16.0 %all_gather.21 = bf16[256,1536]{0,1:T(8,128)(2,1)S(1)} all-gather(bf16[256,192]{0,1:T(8,128)(2,1)} %param.31), channel_id=1, replica_groups=mesh['row'=4,'col'=8] {'col'}, dimensions={1}, use_global_device_ids=true | all-gather | bytes 884736 | tf_op jit(solution)/shard_map/all_gather | solution.py:1028
  27.9 141.7 %first_gather.1 = (bf16[4,8,528,384]{3,2,1,0:T(8,128)(2,1)}, bf16[8,512,1536]{2,1,0:T(8,128)(2,1)}, s32[8,8,512]{2,1,0:T(8,128)}, bf16[4,384,256]{2,1,0:T(8,128)(2,1)}) custom-call(bf16[528,384]{1,0:T(8,128)(2,1)} %copy-done.24, bf16[512,1536]{1,0:T(8,128)(2,1)} %dy_ref.1, s32[8,512]{1,0:T(8,128)} %pad.30.rt_ref, bf16[384,256]{1,0:T(8,128)(2,1)} %pad_maximum_fusion.sh_ref), custom_call_target="tpu_custom_call" | custom-call | tf_op jit(solution)/shard_map/first_gather/pallas_call | solution.py:412
  170.7 2.2 slice_bitcast_fusion.2
  172.9 1.2 copy.119
  174.2 1.4 copy.146
  175.6 1.2 copy.118
  176.8 1.4 copy.145
  178.2 7.1 slice_bitcast_fusion
  185.3 3.6 copy.117
  189.0 3.2 copy.144
  193.2 6.5 copy.121
  199.8 3.0 copy.147
  204.3 2.6 convolution_convert_fusion.7.v_ref
  207.9 5.2 convolution_convert_fusion.5.q_ref
  213.1 7.3 attend_forward.1
  220.5 2.7 multiply_reduce_fusion.2
  225.7 111.0 %line_gather.1 = (bf16[8,512,1536]{2,1,0:T(8,128)(2,1)}, f32[8,8,512]{2,1,0:T(8,128)}) custom-call(bf16[512,1536]{1,0:T(8,128)(2,1)} %copy-done.11, f32[8,512]{1,0:T(8,128)} %pad.31.refs_1_), custom_call_target="tpu_custom_call" | custom-call | tf_op jit(solution)/shard_map/line_gather/pallas_call | solution.py:320
  336.9 1.4 copy.128
  338.3 4.7 reduce-window.19
  343.4 2.0 copy.127
  345.4 2.0 bitcast_select_fusion
  347.4 1.2 copy.156
  348.6 1.5 pad.32.clone.rank_ref
  350.1 1.5 pad_bitcast_fusion.2.rank_t_ref
  351.6 1.7 copy.140
  354.1 115.3 %routed.1 = (bf16[2,4,512,1536]{3,2,1,0:T(8,128)(2,1)}, bf16[2,4,512,1536]{3,2,1,0:T(8,128)(2,1)}, bf16[4,1024,1536]{2,1,0:T(8,128)(2,1)}, bf16[4,1024,1536]{2,1...) custom-call(bf16[8,512,1536]{2,1,0:T(8,128)(2,1)} %get-tuple-element, ...), custom_call_target="tpu_custom_call" | custom-call | tf_op jit(solution)/shard_map/routed/pallas_call | solution.py:894
  469.5 25.9 %expert_grads.1 = (bf16[4,1536,512]{2,1,0:T(8,128)(2,1)}, bf16[4,1536,512]{2,1,0:T(8,128)(2,1)}, bf16[4,512,1536]{2,1,0:T(8,128)(2,1)}) custom-call(bf16[4,1024,1536]{2,1,0:T(8,128)(2,1)} %get-tuple-element.56.xs_ref, bf16[4,1024,1536]{2,1,0:T(8,128)(2,1)} %get-tuple-element.57.dys_ref, bf16[4,1024,512]{2,1,0:T(8,128)(2,1)} %get-tuple-element.58.hid_ref, ...), custom_call_target="tpu_custom_call" | custom-call | tf_op jit(solution)/shard_map/expert_grads/pallas_call | solution.py:950
  495.4 11.2 %copy.141 = bf16[4,512,1536]{1,0,2:T(4,128)(2,1)} copy(bf16[4,512,1536]{2,1,0:T(8,128)(2,1)} %get-tuple-element.63) | data formatting | bytes 12582912
  506.6 8.1 copy.149
  516.8 3.4 all-to-all-start
  521.4 109.6 %line_sum.3 = f32[512,1536]{1,0:T(8,128)} custom-call(bf16[2,4,512,1536]{3,2,1,0:T(8,128)(2,1)} %get-tuple-element.48.in_ref), custom_call_target="tpu_custom_call" | custom-call | tf_op jit(solution)/shard_map/line_sum/pallas_call | solution.py:588
  631.0 110.2 %line_sum.2 = f32[512,1536]{1,0:T(8,128)} custom-call(bf16[2,4,512,1536]{3,2,1,0:T(8,128)(2,1)} %get-tuple-element.47.in_ref), custom_call_target="tpu_custom_call" | custom-call | tf_op jit(solution)/shard_map/line_sum/pallas_call | solution.py:588
  741.2 1.2 convert_element_type.163
  742.7 4.0 multiply_reduce_fusion
  747.8 2.1 multiply_add_fusion
  750.0 3.8 convolution_convert_fusion.4.gm_ref
  753.8 14.1 %attend_backward.1 = (bf16[512,1536]{1,0:T(8,128)(2,1)S(1)}, bf16[512,512]{1,0:T(8,128)(2,1)S(1)}, bf16[512,512]{1,0:T(8,128)(2,1)S(1)}) custom-call(bf16[512,1536]{1,0:T(8,128)(2,1)} %copy-done.2, bf16[512,512]{1,0:T(8,128)(2,1)S(1)} %convolution_convert_fusion.8.k_ref, bf16[512,512]{1,0:T(8,128)(2,1)S(1)} %convolution_convert_fusion.7.v_ref, ...), custom_call_target="tpu_custom_call" | custom-call | tf_op jit(solution)/shard_map/attend_backward/pallas_call | solution.py:137
  768.0 2.6 fusion.40
  772.5 3.0 fusion.9
  775.7 1.8 convolution_convert_fusion.6
  777.6 3.7 convolution_convert_fusion.3
  781.3 4.3 reshape.326
  785.5 2.3 convolution_convert_fusion.2
  787.8 4.0 reshape.327
  791.9 4.7 convolution_convert_fusion.1
  796.5 9.2 reshape.325
  805.7 6.3 convolution_convert_fusion
  812.0 9.0 reshape.328
  821.1 3.8 copy_bitcast_fusion.2
  824.9 7.9 copy_bitcast_fusion
  833.6 69.9 %concatenate.19.in_ref = bf16[2,4,4,528,384]{4,3,2,1,0:T(8,128)(2,1)} concatenate(bf16[2,4,4,192,384]{4,3,2,1,0:T(8,128)(2,1)} %get-tuple-element.92, bf16[2,4,4,64,384]{4,3,2,1,0:T(8,128)(2,1)} %get-tuple-element.94, bf16[2,4,4,64,384]{4,3,2,1,0:T(8,128)(2,1)S(1)} %get-tuple-element.93, bf16[2,4,4,192,384]{4,3,2,1,0:T(8,128)(2,1)} %get-tuple-element.91, ...), dimensions={3} | concatenate | bytes 25952256 | tf_op jit(solution)/shard_map/concatenate | solution.py:1113
  903.5 100.1 %dense_sum.1 = (f32[528,384]{1,0:T(8,128)}, f32[384,384]{1,0:T(8,128)}) custom-call(bf16[2,4,4,528,384]{4,3,2,1,0:T(8,128)(2,1)} %concatenate.19.in_ref, bf16[4,384,384]{2,1,0:T(8,128)(2,1)} %bitcast.145), custom_call_target="tpu_custom_call" | custom-call | tf_op jit(solution)/shard_map/dense_sum/pallas_call | solution.py:704
  1004.6 16.3 %collective-permute-start = (bf16[192,128]{1,0:T(8,128)(2,1)S(1)}, bf16[192,128]{1,0:T(8,128)(2,1)S(1)}, u32[]{:S(2)}, u32[]{:S(2)}) collective-permute-start(bf16[192,128]{1,0:T(8,128)(2,1)S(1)} %get-tuple-element.85), channel_id=1, source_target_pairs={{0,0},{1,1},{2,8},{3,9},{4,16},{5,17},{6,24},{7,25},{8,2},{9,3},{1... | collective-permute-start | bytes 147464 | tf_op jit(solution)/shard_map/ppermute | solution.py:1134
  1021.0 1.3 slice_bitcast_fusion.9
  1022.3 1.6 slice_bitcast_fusion.6
  1023.9 1.8 fusion.38
  1025.7 1.9 slice_bitcast_fusion.4
  1027.6 4.4 fusion.8
  1032.0 1.3 slice_bitcast_fusion.10
  1034.7 2.9 reshape.352
  1037.6 1.6 copy.142
  1039.2 1.9 convert_element_type.166
  1041.1 3.5 convert_element_type.164
  1044.6 3.5 convert_element_type.165
  (202 shorter events, 23.0 us)
Async XLA Ops:
  7.2 185.0 %copy-start = (s32[32,4]{0,1:T(4,128)S(1)}, s32[32,4]{0,1:T(4,128)}, u32[]{:S(2)}) copy-start(s32[32,4]{0,1:T(4,128)} %param.34) | copy-start | bytes 1540
  7.2 344.4 %all-gather.12.cloned.1.call-start = ((), (), s32[]{:S(2)}) async-start(), calls=%async_computation.9 | async-start | bytes 1966080 | tf_op jit(solution)/shard_map/all_gather | solution.py:1031
  23.3 3.0 copy-start.26
  23.3 3.6 copy-start.44
  23.3 3.6 copy-start.45
  23.3 3.6 copy-start.27
  23.3 3.6 copy-start.33
  23.3 3.7 copy-start.34
  23.3 3.7 copy-start.28
  24.1 2.9 copy-start.42
  24.1 3.0 copy-start.29
  24.1 3.0 copy-start.30
  24.1 330.0 %all-gather.10.cloned.1.call-start = ((), (), s32[]{:S(2)}) async-start(), calls=%async_computation.6 | async-start | bytes 7864320 | tf_op jit(solution)/shard_map/all_gather | solution.py:1026
  24.9 329.3 %all-gather.6.cloned.1.call-start = ((), (), s32[]{:S(2)}) async-start(), calls=%async_computation.4 | async-start | bytes 7864320 | tf_op jit(solution)/shard_map/all_gather | solution.py:1024
  25.6 328.5 %all-gather.8.cloned.1.call-start = ((), (), s32[]{:S(2)}) async-start(), calls=%async_computation.5 | async-start | bytes 7864320 | tf_op jit(solution)/shard_map/all_gather | solution.py:1025
  26.2 1008.6 %reduce-scatter.10.cloned.1.call-start = ((), (), s32[]{:S(2)}) async-start(), calls=%async_computation.10 | async-start | bytes 7864320
  27.1 0.8 copy-start.24
  170.7 37.2 %copy-start.31 = (f32[1536]{0:T(1024)}, f32[1536]{0:T(1024)S(1)}, u32[]{:S(2)}) copy-start(f32[1536]{0:T(1024)S(1)} %reshape.332) | copy-start | bytes 18436
  188.9 3.2 copy-start.46
  199.8 4.1 copy-start.13
  204.2 2.6 copy-start.20
  204.3 3.6 copy-start.40
  206.8 13.6 %slice-start.2 = ((s8[4718592]{0:T(1024)(128)(4,1)}), s8[4194304]{0:T(1024)(128)(4,1)S(1)}, s32[]{:S(2)}) async-start(s8[4718592]{0:T(1024)(128)(4,1)} %bitcast.150), calls=%async_computation.13 | async-start | bytes 8388608
  207.9 12.6 %slice-start.3 = ((s8[4718592]{0:T(1024)(128)(4,1)}), s8[524288]{0:T(1024)(128)(4,1)S(1)}, s32[]{:S(2)}) async-start(s8[4718592]{0:T(1024)(128)(4,1)} %bitcast.150), calls=%async_computation.14 | async-start | bytes 1048576
  213.1 10.1 copy-start.2
  220.4 2.8 copy-start.3
  220.4 2.8 copy-start.5
  223.2 1.7 copy-start.9
  223.3 0.8 copy-start.35
  223.3 113.4 %copy-start.25 = (s32[8,8,512]{2,1,0:T(8,128)S(1)}, s32[8,8,512]{2,1,0:T(8,128)}, u32[]{:S(2)}) copy-start(s32[8,8,512]{2,1,0:T(8,128)} %get-tuple-element.44.routes_ref) | copy-start | bytes 393220
  223.6 2.1 copy-start.11
  225.0 111.6 %copy-start.37 = (f32[512]{0:T(512)}, f32[512]{0:T(512)S(1)}, u32[]{:S(2)}) copy-start(f32[512]{0:T(512)S(1)} %fusion.18) | copy-start | bytes 6148
  514.7 526.4 %reduce-scatter.6.cloned.1.call-start = ((), (), s32[]{:S(2)}) async-start(), calls=%async_computation.7 | async-start | bytes 7864320 | tf_op jit(solution)/shard_map/reduce_scatter | solution.py:1141
  515.2 529.3 %reduce-scatter.8.cloned.1.call-start = ((), (), s32[]{:S(2)}) async-start(), calls=%async_computation.8 | async-start | bytes 7864320 | tf_op jit(solution)/shard_map/reduce_scatter | solution.py:1141
  515.3 0.9 copy-start.39
  516.8 225.6 %all-to-all-start = ((f32[8,4,512]{2,1,0:T(4,128)}), f32[8,4,512]{2,1,0:T(4,128)S(1)}, u32[]{:S(2)}, u32[]{:S(2)}) async-start(f32[8,4,512]{2,1,0:T(4,128)} %slice.74), calls=%async_computation | async-start | bytes 131072 | tf_op jit(solution)/shard_map/all_to_all | solution.py:1073
  631.0 110.2 %copy-start.23 = (f32[1536,384]{1,0:T(8,128)S(1)}, f32[1536,384]{1,0:T(8,128)}, u32[]{:S(2)}) copy-start(f32[1536,384]{1,0:T(8,128)} %get-tuple-element.54) | copy-start | bytes 7077892
  741.2 1.3 copy-start.38
  741.2 1.4 copy-start.36
  742.7 4.1 copy-start.10
  742.7 4.7 copy-start.18
  742.7 5.1 copy-start.22
  742.7 7.2 slice-start.4
  747.8 2.2 slice-start.5
  747.8 20.1 %slice-start = ((s8[4718592]{0:T(1024)(128)(4,1)}), s8[524288]{0:T(1024)(128)(4,1)S(1)}, s32[]{:S(2)}) async-start(s8[4718592]{0:T(1024)(128)(4,1)} %bitcast.147), calls=%async_computation.11 | async-start | bytes 1048576
  749.9 3.8 copy-start.17
  749.9 3.8 copy-start.4
  750.0 18.0 %slice-start.1 = ((s8[4718592]{0:T(1024)(128)(4,1)}), s8[4194304]{0:T(1024)(128)(4,1)S(1)}, s32[]{:S(2)}) async-start(s8[4718592]{0:T(1024)(128)(4,1)} %bitcast.147), calls=%async_computation.12 | async-start | bytes 8388608
  767.9 2.7 copy-start.7
  768.0 2.6 copy-start.21
  770.6 1.4 copy-start.14
  770.6 1.9 copy-start.19
  770.6 1.9 copy-start.32
  770.6 1.9 copy-start.41
  781.3 4.3 copy-start.15
  787.8 4.1 copy-start.8
  796.5 9.2 copy-start.6
  821.1 3.8 copy-start.12
  903.5 124.1 %copy-start.16 = (f32[512,1536]{1,0:T(8,128)S(1)}, f32[512,1536]{1,0:T(8,128)}, u32[]{:S(2)}) copy-start(f32[512,1536]{1,0:T(8,128)} %get-tuple-element.90) | copy-start | bytes 9437188
  1004.6 28.6 %collective-permute-start = (bf16[192,128]{1,0:T(8,128)(2,1)S(1)}, bf16[192,128]{1,0:T(8,128)(2,1)S(1)}, u32[]{:S(2)}, u32[]{:S(2)}) collective-permute-start(bf16[192,128]{1,0:T(8,128)(2,1)S(1)} %get-tuple-element.85), channel_id=1, source_target_pairs={{0,0},{1,1},{2,8},{3,9},{4,16},{5,17},{6,24},{7,25},{8,2},{9,3},{1... | collective-permute-start | bytes 147464 | tf_op jit(solution)/shard_map/ppermute | solution.py:1134
  1020.9 12.4 %collective-permute-start.1 = (bf16[192,128]{1,0:T(8,128)(2,1)S(1)}, bf16[192,128]{1,0:T(8,128)(2,1)S(1)}, u32[]{:S(2)}, u32[]{:S(2)}) collective-permute-start(bf16[192,128]{1,0:T(8,128)(2,1)S(1)} %get-tuple-element.86), channel_id=1, source_target_pairs={{0,1},{1,0},{2,9},{3,8},{4,17},{5,16},{6,25},{7,24},{8,3},{9,2},{1... | collective-permute-start | bytes 147464 | tf_op jit(solution)/shard_map/ppermute | solution.py:1134
  1027.6 6.4 copy-start.43
  1041.1 7.0 copy-start.1
Sparse Core Ops, SparseCore 0:
  24.2 54.1 all-gather.11
  80.2 100.7 all-gather.9
  182.9 70.1 all-gather.5
  254.8 70.1 all-gather.7
  514.8 68.9 reduce-scatter.9
  586.6 70.2 reduce-scatter.5
  659.8 70.2 reduce-scatter.7

commit v3 on v2

--- a/solution.py
+++ b/solution.py
@@ -173,7 +173,7 @@
     def peer_row(self, step):
         return lax.rem(self.row + step, self.rows_n)
 
-    def greet(self, with_rows, with_downs=0):
+    def greet(self, with_rows, per_row=0, downs_back=0):
         barrier = pltpu.get_barrier_semaphore()
 
         def hello(row, col):
@@ -200,7 +200,62 @@
             for step in range(1, self.rows_n):
                 hello(self.peer_row(step), self.col)
             count = count + (self.rows_n - 1)
+        if per_row:
+            source = lax.div(self.col, per_row)
+            for col in range(2 * self.chips):
+
+                @pl.when(jnp.logical_not((source == self.row) & (self.col == col)))
+                def _():
+                    hello(source, jnp.int32(col))
+
+            count = count + self.rows_n * per_row - (source == self.row).astype(jnp.int32)
+        if downs_back:
+            goal = lax.div(self.col, downs_back)
+            for turn in range(downs_back):
+                goal_col = downs_back * self.row + turn
+
+                @pl.when(jnp.logical_not((goal == self.row) & (goal_col == self.col)))
+                def _():
+                    hello(goal, goal_col)
+
+            count = count + downs_back - (goal == self.row).astype(jnp.int32)
         pl.semaphore_wait(barrier, count)
+
+
+class Moves:
+    def __init__(self, place, up, down, from_below, from_above, send_sems, recv_sems):
+        self.place = place
+        self.copies = [
+            remote(
+                src, dst, send_sems.at[which], recv_sems.at[which],
+                (place.row, place.col + way),
+            )
+            for which, (src, dst, way) in enumerate(
+                ((up, from_below, 2), (down, from_above, -2))
+            )
+        ]
+        self.ends = (place.chip < place.chips - 1, place.chip > 0)
+
+    def start(self):
+        for which in range(2):
+
+            @pl.when(self.ends[which])
+            def _():
+                self.copies[which].start()
+
+    def wait_send(self):
+        for which in range(2):
+
+            @pl.when(self.ends[which])
+            def _():
+                self.copies[which].wait_send()
+
+    def wait_recv(self):
+        for which in range(2):
+
+            @pl.when(self.ends[1 - which])
+            def _():
+                self.copies[which].wait_recv()
 
 
 class LineGather:
@@ -328,16 +383,19 @@
     )(*arrays)
 
 
-def first_gather(bundle, cotangent, routes_t, shared, collective_id, rows_n, cols_n):
+def first_gather(bundle, cotangent, routes_t, shared, downs, collective_id, rows_n, cols_n):
+    per_row = downs.shape[0]
+
     def kernel(
-        bundle_ref, dy_ref, rt_ref, sh_ref, full_ref, dy_all, rt_all, sh_all, *sems
+        bundle_ref, dy_ref, rt_ref, sh_ref, sd_ref,
+        full_ref, dy_all, rt_all, sh_all, sd_all, *sems
     ):
         place = Place(rows_n, cols_n)
         b_sems, sems = sems[:4], sems[4:]
         d_sems, sems = sems[:4], sems[4:]
         r_sems, sems = sems[:4], sems[4:]
-        row_send, row_core, row_recv, sh_send, sh_recv, sh_local = sems
-        place.greet(True)
+        row_send, row_core, row_recv, sh_send, sh_recv, sh_local, sd_send, sd_recv = sems
+        place.greet(True, per_row)
         row, col = place.row, place.col
         weights = LineGather(place, bundle_ref, full_ref.at[row], *b_sems)
         grads = LineGather(place, dy_ref, dy_all, *d_sems)
@@ -366,6 +424,33 @@
                 sh_ref, sh_all.at[row], sh_send.at[step], sh_recv.at[row],
                 (place.peer_row(step), col),
             )
+
+        down_row = lax.div(col, per_row)
+
+        def downs_to(act_far, act_here):
+            for step in range(rows_n):
+                for turn in range(per_row):
+                    goal_row, goal_col = place.peer_row(step), per_row * row + turn
+                    here = (goal_col == col) if step == 0 else None
+                    far = remote(
+                        sd_ref.at[turn], sd_all.at[col], sd_send.at[step, turn],
+                        sd_recv.at[col], (goal_row, goal_col),
+                    )
+                    if here is None:
+                        act_far(far)
+                        continue
+
+                    @pl.when(here)
+                    def _():
+                        act_here(
+                            pltpu.make_async_copy(
+                                sd_ref.at[turn], sd_all.at[col], sd_recv.at[col]
+                            )
+                        )
+
+                    @pl.when(jnp.logical_not(here))
+                    def _():
+                        act_far(far)
 
         weights.start()
         push(col, bundle_ref)
@@ -375,6 +460,7 @@
             shared_to(step).start()
         for dist in range(1, place.chips):
             weights.step(dist, push)
+        downs_to(lambda far: far.start(), lambda here: here.start())
         grads.start()
         picks.start()
         for dist in range(1, place.chips - 1):
@@ -395,6 +481,17 @@
         grads.finish()
         picks.finish()
         shared_here.wait()
+        downs_to(lambda far: far.wait_send(), lambda here: here.wait())
+
+        @pl.loop(0, cols_n)
+        def _(source):
+            @pl.when(jnp.logical_not((source == col) & (down_row == row)))
+            def _():
+                remote(
+                    sd_ref.at[0], sd_all.at[source], sd_send.at[0, 0], sd_recv.at[source],
+                    (row, place.other),
+                ).wait_recv()
+
         for step in range(1, rows_n):
             other_row = place.peer_row(step)
             shared_to(step).wait_send()
@@ -411,13 +508,14 @@
 
     return pl.pallas_call(
         kernel,
-        in_specs=[ANY] * 4,
-        out_specs=[ANY] * 4,
+        in_specs=[ANY] * 5,
+        out_specs=[ANY] * 5,
         out_shape=[
             jax.ShapeDtypeStruct((rows_n, cols_n) + bundle.shape, bundle.dtype),
             jax.ShapeDtypeStruct((cols_n,) + cotangent.shape, cotangent.dtype),
             jax.ShapeDtypeStruct((cols_n,) + routes_t.shape, routes_t.dtype),
             jax.ShapeDtypeStruct((rows_n,) + shared.shape, shared.dtype),
+            jax.ShapeDtypeStruct((cols_n,) + downs.shape[1:], downs.dtype),
         ],
         scratch_shapes=gather_sems(cols_n) * 3
         + [
@@ -427,10 +525,12 @@
             pltpu.SemaphoreType.DMA((rows_n,)),
             pltpu.SemaphoreType.DMA((rows_n,)),
             pltpu.SemaphoreType.DMA,
+            pltpu.SemaphoreType.DMA((rows_n, per_row)),
+            pltpu.SemaphoreType.DMA((cols_n,)),
         ],
         compiler_params=pltpu.CompilerParams(collective_id=collective_id, has_side_effects=True),
         name="first_gather",
-    )(bundle, cotangent, routes_t, shared)
+    )(bundle, cotangent, routes_t, shared, downs)
 
 
 def line_sum_loop(place, mine, recv, send_sems, recv_sems, parts, ready):
@@ -530,104 +630,109 @@
     return result, drain
 
 
-LINE_PARTS = 4
-
-
-def line_sum(parts_all, collective_id, rows_n, cols_n):
+def dense_sum(lefts, rights, tails, shared, rounds, collective_id, rows_n, cols_n):
+    n_rounds = len(rounds)
+    moved = rounds[0][0]
     chips = cols_n // 2
-    block = parts_all.shape[2:]
-
-    def kernel(
-        in_ref, out_ref, mine, extra, recv, load_sems, core_send, core_recv, send_sems, recv_sems
-    ):
-        place = Place(rows_n, cols_n)
-
-        def load(chip):
-            return pltpu.make_async_copy(
-                in_ref.at[place.core, chip], mine.at[chip], load_sems.at[chip]
-            )
-
-        def swap(chip):
-            return remote(
-                in_ref.at[1 - place.core, chip], extra.at[chip], core_send.at[chip],
-                core_recv.at[chip], (place.row, place.other),
-            )
-
-        order = []
-        for i in range((chips + 1) // 2):
-            order += [chips - 1 - i, i] if chips - 1 - i != i else [i]
-        for chip in order:
-            load(chip).start()
-        place.greet(False)
-        for chip in order:
-            swap(chip).start()
-
-        def ready(chip):
-            load(chip).wait()
-            swap(chip).wait_recv()
-            rows = block[0] // LINE_PARTS
-            for part in range(LINE_PARTS):
-                span = pl.ds(part * rows, rows)
-                mine[chip, span] = (
-                    mine[chip, span].astype(F32) + extra[chip, span].astype(F32)
-                ).astype(mine.dtype)
-
-        result, drain = line_sum_loop(
-            place, mine, recv, send_sems, recv_sems, LINE_PARTS, ready
-        )
-
-        def store(span, value):
-            out_ref[span] = value
-
-        for part in range(LINE_PARTS):
-            result(part, store)
-        drain()
-        for chip in range(chips):
-            swap(chip).wait_send()
-
-    return pl.pallas_call(
-        kernel,
-        in_specs=[ANY],
-        out_specs=pl.BlockSpec(memory_space=pltpu.VMEM),
-        out_shape=jax.ShapeDtypeStruct(block, F32),
-        scratch_shapes=[
-            pltpu.VMEM((chips,) + block, BF),
-            pltpu.VMEM((chips,) + block, BF),
-            pltpu.VMEM((chips + 1,) + block, BF),
-            pltpu.SemaphoreType.DMA((chips,)),
-            pltpu.SemaphoreType.DMA((chips,)),
-            pltpu.SemaphoreType.DMA((chips,)),
-            pltpu.SemaphoreType.DMA((chips, LINE_PARTS)),
-            pltpu.SemaphoreType.DMA((chips + 1, LINE_PARTS)),
-        ],
-        compiler_params=pltpu.CompilerParams(
-            collective_id=collective_id, has_side_effects=True,
-            vmem_limit_bytes=58 * 1024 * 1024,
-        ),
-        name="line_sum",
-    )(parts_all)
-
-
-def dense_sum(grads, shared, collective_id, rows_n, cols_n):
-    chips = cols_n // 2
-    block = grads.shape[3:]
-
-    def kernel(
-        in_ref, sh_ref, out_ref, sh_out, mine, extra, rows_in, recv, sh_in,
-        load_sem, core_send, core_recv, row_send, row_recv, send_sems, recv_sems,
-        sh_send, sh_recv, sh_local,
-    ):
+    inner = shared.shape[1]
+    units = shared.shape[2] // 3
+    per_row = cols_n // rows_n
+    extents = [left.shape[1] // cols_n for left in lefts]
+    block = (sum(extents), inner)
+    n = len(lefts)
+
+    def kernel(*refs):
+        left_refs, right_refs = refs[:n], refs[n : 2 * n]
+        (
+            tail_ref, sh_ref, *round_refs
+        ) = refs[2 * n : 2 * n + 2 + 2 * n_rounds]
+        (
+            out_ref, sh_out, sd_out, arrivals,
+            both, extra, rows_in, recv, sh_in, sd_cut, held, came, held_sems, came_sems,
+            core_send, core_recv, row_send, row_recv, send_sems, recv_sems,
+            sh_send, sh_recv, sh_local, move_send, move_recv, sd_send, sd_recv,
+        ) = refs[2 * n + 2 + 2 * n_rounds :]
         place = Place(rows_n, cols_n)
         row, col = place.row, place.col
-        load = pltpu.make_async_copy(in_ref.at[place.core], mine, load_sem)
-        load.start()
+        mine = both.at[place.core]
         shared_here = pltpu.make_async_copy(sh_ref.at[row], sh_in.at[row], sh_local)
         shared_here.start()
-        place.greet(True)
-        swap = remote(
-            in_ref.at[1 - place.core], extra, core_send, core_recv, (row, place.other)
-        )
-        swap.start()
+        down_row = lax.div(col, per_row)
+        place.greet(True, downs_back=per_row)
+
+        def moves(turn):
+            pair = round_refs[:2] if turn == 0 else (held.at[0], held.at[1])
+            return Moves(
+                place, *pair, arrivals.at[turn, 0], arrivals.at[turn, 1], move_send.at[turn],
+                move_recv.at[turn],
+            )
+
+        def hold(turn):
+            return [
+                pltpu.make_async_copy(
+                    round_refs[2 * turn + which], held.at[which], held_sems.at[which]
+                )
+                for which in range(2)
+            ]
+
+        def next_round(turn):
+            moves(turn - 1).wait_send()
+            copies = hold(turn)
+            for copy in copies:
+                copy.start()
+            moves(turn - 1).wait_recv()
+            for which, comes in ((0, place.chip > 0), (1, place.chip < chips - 1)):
+                bring = pltpu.make_async_copy(
+                    arrivals.at[turn - 1, which], came.at[which], came_sems.at[which]
+                )
+
+                @pl.when(comes)
+                def _():
+                    bring.start()
+
+                copies[which].wait()
+
+                @pl.when(comes)
+                def _():
+                    bring.wait()
+                    part = came.shape[1] // 4
+                    for at in range(0, came.shape[1], part):
+                        span = slice(at, at + part)
+                        held[which, span] = (
+                            held[which, span].astype(F32) + came[which, span].astype(F32)
+                        ).astype(BF)
+
+            moves(turn).start()
+
+        moves(0).start()
+
+        def downs_to(turn, act_far, act_here):
+            goal_col = per_row * row + turn
+            here = (goal_col == col) & (down_row == row)
+            source = lax.rem(col, per_row)
+
+            @pl.when(here)
+            def _():
+                act_here(
+                    pltpu.make_async_copy(
+                        sd_cut.at[turn], sd_out.at[source], sd_recv.at[source]
+                    )
+                )
+
+            @pl.when(jnp.logical_not(here))
+            def _():
+                act_far(
+                    remote(
+                        sd_cut.at[turn], sd_out.at[source], sd_send.at[turn],
+                        sd_recv.at[source], (down_row, goal_col),
+                    )
+                )
+
+        def swap(goal):
+            return remote(
+                both.at[1 - place.core, goal], extra.at[goal], core_send.at[goal],
+                core_recv.at[goal], (row, place.other),
+            )
 
         def shared_to(step):
             goal = place.peer_row(step)
@@ -642,10 +747,9 @@
                 (source, col),
             )
 
-        def to_row(step, chip):
-            goal = place.peer_row(step)
+        def to_row(goal, chip):
             return remote(
-                mine.at[goal, chip], rows_in.at[row, chip], row_send.at[step, chip],
+                mine.at[goal, chip], rows_in.at[row, chip], row_send.at[goal, chip],
                 row_recv.at[row, chip], (goal, col),
             )
 
@@ -656,68 +760,119 @@
                 row_recv.at[source, chip], (source, col),
             )
 
-        load.wait()
-        swap.wait_recv()
         order = []
         for i in range((chips + 1) // 2):
             order += [chips - 1 - i, i] if chips - 1 - i != i else [i]
-        for chip in order:
-            for step in range(1, rows_n):
-                goal = place.peer_row(step)
-                mine[goal, chip] = (
-                    mine[goal, chip].astype(F32) + extra[goal, chip].astype(F32)
-                ).astype(mine.dtype)
-                to_row(step, chip).start()
+
+        def push(goal):
+            swap(goal).wait_recv()
+
+            @pl.when(goal != row)
+            def _():
+                for chip in order:
+                    mine[goal, chip] = (
+                        mine[goal, chip].astype(F32) + extra[goal, chip].astype(F32)
+                    ).astype(BF)
+                    to_row(goal, chip).start()
+
         for step in range(1, rows_n):
             shared_to(step).start()
-
-        def ready(chip):
-            total = mine[row, chip].astype(F32) + extra[row, chip].astype(F32)
-            for step in range(1, rows_n):
-                from_row(step, chip).wait_recv()
-                total = total + rows_in[place.peer_row(step), chip].astype(F32)
-            mine[row, chip] = total.astype(mine.dtype)
-
-        result, drain = line_sum_loop(
-            place, mine.at[row], recv, send_sems, recv_sems, 1, ready
-        )
-
-        def store(span, value):
-            out_ref[span] = value
-
-        result(0, store)
+        for goal in range(rows_n):
+            cols = slice(goal * inner, (goal + 1) * inner)
+            at = 0
+            for i in range(n):
+                made = mm_tn(left_refs[i][...], right_refs[i][:, cols])
+                if i == n - 1:
+                    made = made + tail_ref[goal]
+                made = made.astype(BF)
+                for owner in range(cols_n):
+                    both[owner % 2, goal, owner // 2, at : at + extents[i], :] = made[
+                        owner * extents[i] : (owner + 1) * extents[i]
+                    ]
+                at += extents[i]
+            swap(goal).start()
+            if goal > 0:
+                push(goal - 1)
+        push(rows_n - 1)
+        for turn in range(1, n_rounds):
+            next_round(turn)
         shared_here.wait()
         for step in range(1, rows_n):
             shared_from(step).wait_recv()
         total = sh_in[0].astype(F32)
         for other in range(1, rows_n):
             total = total + sh_in[other].astype(F32)
-        sh_out[...] = total
+        sh_out[...] = total[:, : 2 * units]
+        cut = inner // per_row
+        for turn in range(per_row):
+            sd_cut[turn] = total[turn * cut : (turn + 1) * cut, 2 * units :]
+            downs_to(turn, lambda far: far.start(), lambda here: here.start())
+
+        def ready(chip):
+            total = mine[row, chip].astype(F32) + extra[row, chip].astype(F32)
+            for step in range(1, rows_n):
+                from_row(step, chip).wait_recv()
+                total = total + rows_in[place.peer_row(step), chip].astype(F32)
+            mine[row, chip] = total.astype(BF)
+
+        result, drain = line_sum_loop(
+            place, mine.at[row], recv, send_sems, recv_sems, 1, ready
+        )
+
+        def store(span, value):
+            out_ref[span] = value
+
+        result(0, store)
         drain()
-        swap.wait_send()
+
+        moves(n_rounds - 1).wait_send()
+        moves(n_rounds - 1).wait_recv()
+        for turn in range(per_row):
+            downs_to(turn, lambda far: far.wait_send(), lambda here: here.wait())
+            at_home = per_row * row + turn
+            mine_here = (at_home == col) & (down_row == row)
+
+            @pl.when(jnp.logical_not(mine_here))
+            def _():
+                remote(
+                    sd_cut.at[0], sd_out.at[turn], sd_send.at[turn], sd_recv.at[turn],
+                    (down_row, at_home),
+                ).wait_recv()
+
         for step in range(1, rows_n):
             shared_to(step).wait_send()
-            for chip in range(chips):
-                to_row(step, chip).wait_send()
+        for goal in range(rows_n):
+            swap(goal).wait_send()
+
+            @pl.when(goal != row)
+            def _():
+                for chip in range(chips):
+                    to_row(goal, chip).wait_send()
 
     vmem = pl.BlockSpec(memory_space=pltpu.VMEM)
     return pl.pallas_call(
         kernel,
-        in_specs=[ANY, ANY],
-        out_specs=[vmem, vmem],
+        in_specs=[vmem] * (2 * n + 1) + [ANY] * (1 + 2 * n_rounds),
+        out_specs=[vmem, vmem, vmem, ANY],
         out_shape=[
             jax.ShapeDtypeStruct(block, F32),
-            jax.ShapeDtypeStruct(shared.shape[1:], F32),
+            jax.ShapeDtypeStruct((inner, 2 * units), F32),
+            jax.ShapeDtypeStruct((per_row, inner // per_row, units), F32),
+            jax.ShapeDtypeStruct((n_rounds, 2) + moved.shape, moved.dtype),
         ],
         scratch_shapes=[
-            pltpu.VMEM((rows_n, chips) + block, BF),
+            pltpu.VMEM((2, rows_n, chips) + block, BF),
             pltpu.VMEM((rows_n, chips) + block, BF),
             pltpu.VMEM((rows_n, chips) + block, BF),
             pltpu.VMEM((chips + 1,) + block, BF),
             pltpu.VMEM(shared.shape, BF),
-            pltpu.SemaphoreType.DMA,
-            pltpu.SemaphoreType.DMA,
-            pltpu.SemaphoreType.DMA,
+            pltpu.VMEM((per_row, inner // per_row, units), F32),
+            pltpu.VMEM((2,) + moved.shape, BF),
+            pltpu.VMEM((2,) + moved.shape, BF),
+            pltpu.SemaphoreType.DMA((2,)),
+            pltpu.SemaphoreType.DMA((2,)),
+            pltpu.SemaphoreType.DMA((rows_n,)),
+            pltpu.SemaphoreType.DMA((rows_n,)),
             pltpu.SemaphoreType.DMA((rows_n, chips)),
             pltpu.SemaphoreType.DMA((rows_n, chips)),
             pltpu.SemaphoreType.DMA((chips, 1)),
@@ -725,241 +880,403 @@
             pltpu.SemaphoreType.DMA((rows_n,)),
             pltpu.SemaphoreType.DMA((rows_n,)),
             pltpu.SemaphoreType.DMA,
+            pltpu.SemaphoreType.DMA((n_rounds, 2)),
+            pltpu.SemaphoreType.DMA((n_rounds, 2)),
+            pltpu.SemaphoreType.DMA((per_row,)),
+            pltpu.SemaphoreType.DMA((per_row,)),
         ],
         compiler_params=pltpu.CompilerParams(
             collective_id=collective_id, has_side_effects=True,
-            vmem_limit_bytes=58 * 1024 * 1024,
+            vmem_limit_bytes=60 * 1024 * 1024,
+        ),
+        cost_estimate=pl.CostEstimate(
+            flops=2 * 512 * 1536 * 4096, bytes_accessed=350_000_000, transcendentals=0
         ),
         name="dense_sum",
-    )(grads, shared)
-
-
-def routed_kernel(
-    x_ref, dy_ref, routes_ref, gates_ref, rank_ref, rank_t_ref, eg_ref, eu_ref, ed_ref,
-    sgu_ref, sd_ref,
-    out_hbm, gx_hbm, xs_hbm, dys_hbm, hid_ref, gg_ref, gu_ref, ggw_ref, shared_ref,
-    xs, dys, pick, wide_out, wide_gx, slot_gate, slot_ggw, stage, slot_sems, stage_sems,
-):
-    unit = pl.program_id(0)
-    units_n = pl.num_programs(0)
+    )(*lefts, *rights, tails, shared, *[part for pair in rounds for part in pair])
+
+
+def round_tables(chips):
+    order, up, down = [], [], []
+    for here in range(chips):
+        due = {q: chips - 1 - q + here for q in range(here + 1, chips)}
+        due.update({q: q + chips - 1 - here for q in range(here)})
+        calls = sorted(due, key=lambda q: (due[q], -q)) + [here]
+        order.append(calls)
+        at = {q: i for i, q in enumerate(calls)}
+        up.append([at.get(chips - 1 - t + here, 0) for t in range(chips - 1)])
+        down.append([at.get(t - (chips - 1 - here), 0) for t in range(chips - 1)])
+    return order, up, down
+
+
+class LineRounds:
+    def __init__(self, cols_n):
+        self.chips = cols_n // 2
+        here = lax.axis_index("col") // 2
+        _, up, down = round_tables(self.chips)
+        self.up_call = jnp.array(up, jnp.int32)[here]
+        self.down_call = jnp.array(down, jnp.int32)[here]
+        self.not_first, self.not_last = here > 0, here < self.chips - 1
+        self.sums = []
+        self.below = self.above = None
+
+    def add(self, own, other):
+        self.sums.append((own, other))
+
+    def held(self, call):
+        total = None
+        for i, (own, other) in enumerate(self.sums):
+            value = own.astype(F32) + other.astype(F32)
+            total = value if i == 0 else jnp.where(call == i, value, total)
+        return total
+
+    def kept(self, turn):
+        return [self.held(call[turn]).astype(BF) for call in (self.up_call, self.down_call)]
+
+    def outgoing(self, turn):
+        ups, downs = self.held(self.up_call[turn]), self.held(self.down_call[turn])
+        if turn:
+            ups = ups + jnp.where(self.not_first, self.below.astype(F32), 0.0)
+            downs = downs + jnp.where(self.not_last, self.above.astype(F32), 0.0)
+        return ups.astype(BF), downs.astype(BF)
+
+    def arrived(self, below, above):
+        self.below, self.above = below, above
+
+    def result(self):
+        own, other = self.sums[-1]
+        total = own.astype(F32) + other.astype(F32)
+        total = total + jnp.where(self.not_first, self.below.astype(F32), 0.0)
+        return total + jnp.where(self.not_last, self.above.astype(F32), 0.0)
+
+
+def routed_kernel(call, rows_n, cols_n, n_moves, *refs):
+    (
+        x_hbm, dy_hbm, routes_hbm, routes_t_hbm, gates_hbm, eg_ref, eu_ref, ed_ref, sgu_ref, sd_ref
+    ) = refs[:10]
+    up_down, refs = refs[10 : 10 + n_moves], refs[10 + n_moves :]
+    (
+        own_hbm, other_hbm, xs_hbm, dys_hbm, hid_ref, gg_ref, gu_ref, ggw_ref, shared_ref
+    ) = refs[:9]
+    arrivals, refs = refs[9 : 9 + n_moves], refs[9 + n_moves :]
+    (
+        x_ref, dy_ref, routes_ref, routes_t_ref, gates_ref,
+        xs, dys, pick, back_pick, wide_out, wide_gx, slot_gate, stage,
+        load_sems, slot_sems, own_sems, core_send, core_recv, move_send, move_recv,
+    ) = refs
+    place = Place(rows_n, cols_n)
+    my_core = place.core
+    unit = jnp.int32(0)
+    for chip, calls in enumerate(round_tables(place.chips)[0]):
+        unit = unit + jnp.where(place.chip == chip, calls[call], 0)
+    pair = pl.ds(2 * unit, 2)
+    loads = [
+        pltpu.make_async_copy(src.at[pair], dst, load_sems.at[i])
+        for i, (src, dst) in enumerate(
+            (
+                (routes_hbm, routes_ref), (routes_t_hbm, routes_t_ref), (gates_hbm, gates_ref),
+                (x_hbm, x_ref), (dy_hbm, dy_ref),
+            )
+        )
+    ]
+    moves = None
+    if n_moves:
+        moves = Moves(place, *up_down, *arrivals, move_send, move_recv)
+    e = pl.program_id(0)
     total = x_ref.shape[1]
     cap = xs.shape[1] // 2
     hidden_units = sd_ref.shape[0]
-    first = lax.axis_index("col") * EXP_DEV
-    slots = pl.ds(unit * 2 * cap, 2 * cap)
+    first = place.col * EXP_DEV
     spans = [slice(at, at + 512) for at in range(0, x_ref.shape[2], 512)]
 
     def slot_copy(which):
         src, dst = ((xs, xs_hbm), (dys, dys_hbm))[which]
-        return pltpu.make_async_copy(src, dst.at[:, slots], slot_sems.at[which])
-
-    def stage_copy(which, core):
-        dst = (out_hbm, gx_hbm)[which]
+        return pltpu.make_async_copy(src, dst, slot_sems.at[which])
+
+    def own_copy(which):
         return pltpu.make_async_copy(
-            stage.at[which], dst.at[core, unit], stage_sems.at[which]
+            stage.at[which, my_core], own_hbm.at[which], own_sems.at[which]
         )
 
-    @pl.when(unit > 0)
+    def core_copy(which):
+        return remote(
+            stage.at[which, 1 - my_core], other_hbm.at[which], core_send.at[which],
+            core_recv.at[which], (place.row, place.other),
+        )
+
+    @pl.when(e == 0)
     def _():
+        for load in loads:
+            load.start()
+        place.greet(False)
+        if n_moves:
+            moves.start()
+        ggw_ref[...] = jnp.zeros_like(ggw_ref)
+        for load in loads:
+            load.wait()
+        row_at = lax.broadcasted_iota(jnp.int32, (total, total), 0)
+        col_at = lax.broadcasted_iota(jnp.int32, (total, total), 1)
+        upto = jnp.where(row_at <= col_at, 1.0, 0.0).astype(BF)
+        since = jnp.where(row_at >= col_at, 1.0, 0.0).astype(BF)
+        for core in range(2):
+            gate_rows = gates_ref[core]
+            route_rows = routes_ref[core]
+            route_cols = routes_t_ref[core]
+            hits = [
+                jnp.sum(jnp.where(route_rows == first + i, 1.0, 0.0), axis=0, keepdims=True)
+                for i in range(EXP_DEV)
+            ]
+            hits = jnp.concatenate(hits + [jnp.zeros((8 - EXP_DEV, total), F32)], axis=0)
+            rank = jnp.where(hits > 0.0, mm(hits.astype(BF), upto) - 1.0, -1.0)
+            hits_t = [
+                jnp.sum(jnp.where(route_cols == first + i, 1.0, 0.0), axis=1, keepdims=True)
+                for i in range(EXP_DEV)
+            ]
+            hits_t = jnp.concatenate(hits_t + [jnp.zeros((total, 8 - EXP_DEV), F32)], axis=1)
+            rank_t = jnp.where(hits_t > 0.0, mm(since, hits_t.astype(BF)) - 1.0, -1.0)
+            at = lax.broadcasted_iota(jnp.int32, (cap, total), 0).astype(F32)
+            at_t = lax.broadcasted_iota(jnp.int32, (total, cap), 1).astype(F32)
+            backs = []
+            for i in range(EXP_DEV):
+                here = at == rank[i : i + 1, :]
+                gate_row = jnp.sum(
+                    jnp.where(route_rows == first + i, gate_rows, 0.0), axis=0, keepdims=True
+                )
+                slot_gate[i, core * cap : (core + 1) * cap, :] = jnp.sum(
+                    jnp.where(here, gate_row, 0.0), axis=1, keepdims=True
+                )
+                pick[core, i * cap : (i + 1) * cap, :] = jnp.where(here, 1.0, 0.0).astype(BF)
+                backs.append(jnp.where(at_t == rank_t[:, i : i + 1], 1.0, 0.0).astype(BF))
+            back_pick[core] = jnp.concatenate(backs, axis=1)
+            for src, dst in ((x_ref, xs), (dy_ref, dys)):
+                for cols in spans:
+                    got = mm(pick[core], src[core, :, cols]).astype(BF)
+                    for i in range(EXP_DEV):
+                        dst[i, core * cap : (core + 1) * cap, cols] = got[
+                            i * cap : (i + 1) * cap
+                        ]
+        slot_copy(0).start()
+        slot_copy(1).start()
+
+    rows_x = xs[e]
+    gate_part = mm(rows_x, eg_ref[0])
+    up_part = mm(rows_x, eu_ref[0])
+    act, slope = silu_parts(gate_part)
+    grad_hidden = mm_nt(dys[e], ed_ref[0])
+    hidden = (act * up_part).astype(BF).astype(F32)
+    weight = slot_gate[e]
+    gated = (hidden * weight).astype(BF)
+    hid_ref[0] = gated
+    slot_ggw = jnp.sum(hidden * grad_hidden, axis=1, keepdims=True)
+    grad_hidden = grad_hidden * weight
+    geg = (grad_hidden * up_part * slope).astype(BF)
+    geu = (grad_hidden * act).astype(BF)
+    gg_ref[0] = geg
+    gu_ref[0] = geu
+    rows = pl.ds(pl.multiple_of(e * cap, cap), cap)
+    for cols in spans:
+        made = mm(gated, ed_ref[0, :, cols]).astype(BF)
+        back = (mm_nt(geg, eg_ref[0, cols, :]) + mm_nt(geu, eu_ref[0, cols, :])).astype(BF)
+        for core in range(2):
+            wide_out[core, rows, cols] = made[core * cap : (core + 1) * cap]
+            wide_gx[core, rows, cols] = back[core * cap : (core + 1) * cap]
+    sub = lax.broadcasted_iota(jnp.int32, (8, total), 0)
+    for core in range(2):
+        back = jnp.sum(
+            pick[core, rows, :].astype(F32) * slot_ggw[core * cap : (core + 1) * cap],
+            axis=0,
+            keepdims=True,
+        )
+        ggw_ref[core] = jnp.where(sub == e, back, ggw_ref[core])
+
+    @pl.when(e == EXP_DEV - 1)
+    def _():
+        for core in range(2):
+            both = mm(x_ref[core], sgu_ref[...])
+            s_act, s_slope = silu_parts(both[:, :hidden_units])
+            s_up = both[:, hidden_units:]
+            s_hidden = (s_act * s_up).astype(BF)
+            grad_shared = mm_nt(dy_ref[core], sd_ref[...])
+            grad_both = jnp.concatenate(
+                [(grad_shared * s_up * s_slope).astype(BF), (grad_shared * s_act).astype(BF)],
+                axis=1,
+            )
+            for cols in spans:
+                value = mm(back_pick[core], wide_gx[core, :, cols])
+                value = value + mm_nt(grad_both, sgu_ref[cols, :])
+                stage[1, core, :, cols] = value.astype(BF)
+                value = mm(back_pick[core], wide_out[core, :, cols])
+                value = value + mm(s_hidden, sd_ref[:, cols])
+                stage[0, core, :, cols] = value.astype(BF)
+                made = mm_tn(x_ref[core, :, cols], grad_both)
+                made_d = mm_tn(dy_ref[core, :, cols], s_hidden)
+                if core == 0:
+                    shared_ref[cols, : 2 * hidden_units] = made
+                    shared_ref[cols, 2 * hidden_units :] = made_d
+                else:
+                    shared_ref[cols, : 2 * hidden_units] += made
+                    shared_ref[cols, 2 * hidden_units :] += made_d
+        for which in (1, 0):
+            core_copy(which).start()
+            own_copy(which).start()
         slot_copy(0).wait()
         slot_copy(1).wait()
-
-    for core in range(2):
-        gate_rows = gates_ref[core]
-        route_rows = routes_ref[core]
-        for e in range(EXP_DEV):
-            at = lax.broadcasted_iota(jnp.int32, (cap, total), 0)
-            here = at == rank_ref[core, e : e + 1, :]
-            gate_row = jnp.sum(
-                jnp.where(route_rows == first + e, gate_rows, 0.0), axis=0, keepdims=True
-            )
-            slot_gate[e, core * cap : (core + 1) * cap, :] = jnp.sum(
-                jnp.where(here, gate_row, 0.0), axis=1, keepdims=True
-            )
-            pick[core, e * cap : (e + 1) * cap, :] = jnp.where(here, 1.0, 0.0).astype(BF)
-        for src, dst in ((x_ref, xs), (dy_ref, dys)):
-            for cols in spans:
-                got = mm(pick[core], src[core, :, cols]).astype(BF)
-                for e in range(EXP_DEV):
-                    dst[e, core * cap : (core + 1) * cap, cols] = got[e * cap : (e + 1) * cap]
-    slot_copy(0).start()
-    slot_copy(1).start()
-
-    @pl.loop(0, EXP_DEV)
-    def _(e):
-        rows_x = xs[e]
-        gate_part = mm(rows_x, eg_ref[e])
-        up_part = mm(rows_x, eu_ref[e])
-        act, slope = silu_parts(gate_part)
-        grad_hidden = mm_nt(dys[e], ed_ref[e])
-        hidden = (act * up_part).astype(BF).astype(F32)
-        weight = slot_gate[e]
-        gated = (hidden * weight).astype(BF)
-        hid_ref[e] = gated
-        slot_ggw[e] = jnp.sum(hidden * grad_hidden, axis=1, keepdims=True)
-        grad_hidden = grad_hidden * weight
-        geg = (grad_hidden * up_part * slope).astype(BF)
-        geu = (grad_hidden * act).astype(BF)
-        gg_ref[e] = geg
-        gu_ref[e] = geu
-        rows = pl.ds(pl.multiple_of(e * cap, cap), cap)
-        for cols in spans:
-            made = mm(gated, ed_ref[e, :, cols]).astype(BF)
-            back = (mm_nt(geg, eg_ref[e, cols, :]) + mm_nt(geu, eu_ref[e, cols, :])).astype(BF)
-            for core in range(2):
-                wide_out[core, rows, cols] = made[core * cap : (core + 1) * cap]
-                wide_gx[core, rows, cols] = back[core * cap : (core + 1) * cap]
-
-    ggw_ref[...] = jnp.zeros_like(ggw_ref)
-    for core in range(2):
-        for e in range(EXP_DEV):
-            here = pick[core, e * cap : (e + 1) * cap, :].astype(F32)
-            ggw_ref[core, e : e + 1, :] = jnp.sum(
-                here * slot_ggw[e, core * cap : (core + 1) * cap, :], axis=0, keepdims=True
-            )
-        at = lax.broadcasted_iota(jnp.int32, (total, cap), 1)
-        back_pick = jnp.concatenate(
-            [
-                jnp.where(at == rank_t_ref[core, :, e : e + 1], 1.0, 0.0).astype(BF)
-                for e in range(EXP_DEV)
-            ],
-            axis=1,
-        )
-        both = mm(x_ref[core], sgu_ref[...])
-        s_act, s_slope = silu_parts(both[:, :hidden_units])
-        s_up = both[:, hidden_units:]
-        s_hidden = (s_act * s_up).astype(BF)
-        grad_shared = mm_nt(dy_ref[core], sd_ref[...])
-        grad_both = jnp.concatenate(
-            [(grad_shared * s_up * s_slope).astype(BF), (grad_shared * s_act).astype(BF)],
-            axis=1,
-        )
-        for which in range(2):
-            if core == 0:
-
-                @pl.when(unit > 0)
-                def _():
-                    stage_copy(which, 1).wait()
-
-            else:
-                stage_copy(which, 0).wait()
-            for cols in spans:
-                if which == 0:
-                    value = mm(back_pick, wide_out[core, :, cols])
-                    value = value + mm(s_hidden, sd_ref[:, cols])
-                else:
-                    value = mm(back_pick, wide_gx[core, :, cols])
-                    value = value + mm_nt(grad_both, sgu_ref[cols, :])
-                stage[which, :, cols] = value.astype(BF)
-            stage_copy(which, core).start()
-        if core == 0:
-
-            @pl.when(unit == 0)
-            def _():
-                shared_ref[...] = jnp.zeros_like(shared_ref)
-
-        for cols in spans:
-            shared_ref[cols, : 2 * hidden_units] += mm_tn(x_ref[core, :, cols], grad_both)
-            shared_ref[cols, 2 * hidden_units :] += mm_tn(dy_ref[core, :, cols], s_hidden)
-
-    @pl.when(unit == units_n - 1)
-    def _():
-        slot_copy(0).wait()
-        slot_copy(1).wait()
-        stage_copy(0, 1).wait()
-        stage_copy(1, 1).wait()
-
-
-def routed(x_all, dy_all, routes_all, gates_all, rank, egate, eup, edown, sgu, sdown):
+        if n_moves:
+            moves.wait_send()
+            moves.wait_recv()
+        for which in (1, 0):
+            own_copy(which).wait()
+            core_copy(which).wait_send()
+            core_copy(which).wait_recv()
+
+
+def routed(call, rows_n, x_all, dy_all, routes, routes_t, gates, egate, eup, edown, sgu, sdown, moves):
     cols_n, total, width = x_all.shape
-    chips = cols_n // 2
     cap = 4 * total * TOP // (3 * EXP_DEV * cols_n)
     slots = 2 * cap
     ffn = egate.shape[2]
     hidden_units = sdown.shape[0]
-    rank_t = jnp.swapaxes(rank, 1, 2)
-
-    def per_unit(*shape):
-        return pl.BlockSpec(shape, lambda q: (q,) + (0,) * (len(shape) - 1))
-
-    def whole(a):
+
+    def each(*shape):
+        return pl.BlockSpec((1,) + shape, lambda e: (e,) + (0,) * len(shape))
+
+    def whole(*shape):
         return pl.BlockSpec(
-            a.shape, lambda q: (0,) * a.ndim, pipeline_mode=pl.Buffered(1)
+            shape, lambda e: (0,) * len(shape), pipeline_mode=pl.Buffered(1)
         )
 
-    slot_block = pl.BlockSpec(
-        (EXP_DEV, slots, ffn), lambda q: (0, q, 0), pipeline_mode=pl.Buffered(1)
-    )
-    small = per_unit(2, 8, total)
+    slot_block = each(slots, ffn)
     return pl.pallas_call(
-        routed_kernel,
-        grid=(chips,),
-        in_specs=[
-            per_unit(2, total, width), per_unit(2, total, width), small, small, small,
-            per_unit(2, total, 8), whole(egate), whole(eup), whole(edown), whole(sgu),
-            whole(sdown),
-        ],
+        functools.partial(routed_kernel, call, rows_n, cols_n, len(moves)),
+        grid=(EXP_DEV,),
+        in_specs=[ANY] * 5
+        + [
+            each(width, ffn), each(width, ffn), each(ffn, width), whole(*sgu.shape),
+            whole(*sdown.shape),
+        ]
+        + [ANY] * len(moves),
         out_specs=[
-            ANY, ANY, ANY, ANY, slot_block, slot_block, slot_block, small,
-            pl.BlockSpec(
-                (width, 3 * hidden_units), lambda q: (0, 0), pipeline_mode=pl.Buffered(1)
-            ),
-        ],
+            ANY, ANY, ANY, ANY, slot_block, slot_block, slot_block,
+            whole(2, 8, total), whole(width, 3 * hidden_units),
+        ]
+        + [ANY] * len(moves),
         out_shape=[
-            jax.ShapeDtypeStruct((2, chips, total, width), BF),
-            jax.ShapeDtypeStruct((2, chips, total, width), BF),
-            jax.ShapeDtypeStruct((EXP_DEV, cols_n * cap, width), BF),
-            jax.ShapeDtypeStruct((EXP_DEV, cols_n * cap, width), BF),
-            jax.ShapeDtypeStruct((EXP_DEV, cols_n * cap, ffn), BF),
-            jax.ShapeDtypeStruct((EXP_DEV, cols_n * cap, ffn), BF),
-            jax.ShapeDtypeStruct((EXP_DEV, cols_n * cap, ffn), BF),
-            jax.ShapeDtypeStruct((cols_n, 8, total), F32),
+            jax.ShapeDtypeStruct((2, total, width), BF),
+            jax.ShapeDtypeStruct((2, total, width), BF),
+            jax.ShapeDtypeStruct((EXP_DEV, slots, width), BF),
+            jax.ShapeDtypeStruct((EXP_DEV, slots, width), BF),
+            jax.ShapeDtypeStruct((EXP_DEV, slots, ffn), BF),
+            jax.ShapeDtypeStruct((EXP_DEV, slots, ffn), BF),
+            jax.ShapeDtypeStruct((EXP_DEV, slots, ffn), BF),
+            jax.ShapeDtypeStruct((2, 8, total), F32),
             jax.ShapeDtypeStruct((width, 3 * hidden_units), F32),
-        ],
+        ]
+        + [jax.ShapeDtypeStruct(a.shape, a.dtype) for a in moves],
         scratch_shapes=[
+            pltpu.VMEM((2, total, width), BF),
+            pltpu.VMEM((2, total, width), BF),
+            pltpu.VMEM((2, 8, total), jnp.int32),
+            pltpu.VMEM((2, total, 8), jnp.int32),
+            pltpu.VMEM((2, 8, total), F32),
             pltpu.VMEM((EXP_DEV, slots, width), BF),
             pltpu.VMEM((EXP_DEV, slots, width), BF),
             pltpu.VMEM((2, EXP_DEV * cap, total), BF),
+            pltpu.VMEM((2, total, EXP_DEV * cap), BF),
             pltpu.VMEM((2, EXP_DEV * cap, width), BF),
             pltpu.VMEM((2, EXP_DEV * cap, width), BF),
             pltpu.VMEM((EXP_DEV, slots, 1), F32),
-            pltpu.VMEM((EXP_DEV, slots, 1), F32),
-            pltpu.VMEM((2, total, width), BF),
+            pltpu.VMEM((2, 2, total, width), BF),
+            pltpu.SemaphoreType.DMA((5,)),
+            pltpu.SemaphoreType.DMA((2,)),
+            pltpu.SemaphoreType.DMA((2,)),
+            pltpu.SemaphoreType.DMA((2,)),
+            pltpu.SemaphoreType.DMA((2,)),
             pltpu.SemaphoreType.DMA((2,)),
             pltpu.SemaphoreType.DMA((2,)),
         ],
-        compiler_params=pltpu.CompilerParams(vmem_limit_bytes=60 * 1024 * 1024),
+        compiler_params=pltpu.CompilerParams(
+            collective_id=4 + call, has_side_effects=True, vmem_limit_bytes=60 * 1024 * 1024
+        ),
+        cost_estimate=pl.CostEstimate(
+            flops=24_000_000_000, bytes_accessed=100_000_000, transcendentals=0
+        ),
         name="routed",
-    )(x_all, dy_all, routes_all, gates_all, rank, rank_t, egate, eup, edown, sgu, sdown)
-
-
-def expert_grads_kernel(xs_ref, dys_ref, hid_ref, gg_ref, gu_ref, og_ref, ou_ref, od_ref):
-    rows = xs_ref[0]
-    og_ref[0] = mm_tn(rows, gg_ref[0]).astype(BF)
-    ou_ref[0] = mm_tn(rows, gu_ref[0]).astype(BF)
-    od_ref[0] = mm_tn(hid_ref[0], dys_ref[0]).astype(BF)
-
-
-def expert_grads(xs, dys, hid, gg, gu):
-    _, slots, width = xs.shape
-    ffn = hid.shape[2]
-
-    def each(rows, cols):
-        return pl.BlockSpec((1, rows, cols), lambda e: (e, 0, 0))
+    )(
+        x_all, dy_all, routes, routes_t, gates, egate, eup, edown, sgu, sdown, *moves
+    )
+
+
+def expert_grads_kernel(units_n, place_of, *refs):
+    xs, dys, hid, gg, gu = (refs[i * units_n : (i + 1) * units_n] for i in range(5))
+    up, down, og_ref, ou_ref, od_ref, from_below, from_above, send_sems, recv_sems = refs[
+        5 * units_n :
+    ]
+    place = place_of()
+    moves = Moves(place, up, down, from_below, from_above, send_sems, recv_sems)
+
+    @pl.when(pl.program_id(0) == 0)
+    def _():
+        place.greet(False)
+        moves.start()
+
+    rows_n = og_ref.shape[0]
+    inner = og_ref.shape[2]
+
+    def joined(parts, cols=slice(None)):
+        return jnp.concatenate([part[0, :, cols] for part in parts], axis=0)
+
+    all_gg, all_gu, all_hid = joined(gg), joined(gu), joined(hid)
+    for row in range(rows_n):
+        cols = slice(row * inner, (row + 1) * inner)
+        rows = joined(xs, cols)
+        og_ref[row, 0] = mm_tn(rows, all_gg).astype(BF)
+        ou_ref[row, 0] = mm_tn(rows, all_gu).astype(BF)
+        od_ref[row, 0] = mm_tn(all_hid, joined(dys, cols)).astype(BF)
+
+    @pl.when(pl.program_id(0) == EXP_DEV - 1)
+    def _():
+        moves.wait_send()
+        moves.wait_recv()
+
+
+def expert_grads(xs, dys, hid, gg, gu, rows_n, cols_n, moves, collective_id):
+    _, slots, width = xs[0].shape
+    ffn = hid[0].shape[2]
+    inner = width // rows_n
+    units_n = len(xs)
+
+    def each(cols):
+        return pl.BlockSpec((1, slots, cols), lambda e: (e, 0, 0))
 
     return pl.pallas_call(
-        expert_grads_kernel,
+        functools.partial(expert_grads_kernel, units_n, lambda: Place(rows_n, cols_n)),
         grid=(EXP_DEV,),
-        in_specs=[each(slots, width)] * 2 + [each(slots, ffn)] * 3,
-        out_specs=[each(width, ffn), each(width, ffn), each(ffn, width)],
+        in_specs=[each(width)] * (2 * units_n)
+        + [each(ffn)] * (3 * units_n)
+        + [ANY] * 2,
+        out_specs=[
+            pl.BlockSpec((rows_n, 1, inner, ffn), lambda e: (0, e, 0, 0)),
+            pl.BlockSpec((rows_n, 1, inner, ffn), lambda e: (0, e, 0, 0)),
+            pl.BlockSpec((rows_n, 1, ffn, inner), lambda e: (0, e, 0, 0)),
+            ANY,
+            ANY,
+        ],
         out_shape=[
-            jax.ShapeDtypeStruct((EXP_DEV, width, ffn), BF),
-            jax.ShapeDtypeStruct((EXP_DEV, width, ffn), BF),
-            jax.ShapeDtypeStruct((EXP_DEV, ffn, width), BF),
+            jax.ShapeDtypeStruct((rows_n, EXP_DEV, inner, ffn), BF),
+            jax.ShapeDtypeStruct((rows_n, EXP_DEV, inner, ffn), BF),
+            jax.ShapeDtypeStruct((rows_n, EXP_DEV, ffn, inner), BF),
+            jax.ShapeDtypeStruct(moves[0].shape, moves[0].dtype),
+            jax.ShapeDtypeStruct(moves[1].shape, moves[1].dtype),
         ],
-        compiler_params=pltpu.CompilerParams(vmem_limit_bytes=60 * 1024 * 1024),
+        scratch_shapes=[pltpu.SemaphoreType.DMA((2,)), pltpu.SemaphoreType.DMA((2,))],
+        compiler_params=pltpu.CompilerParams(
+            collective_id=collective_id, has_side_effects=True, vmem_limit_bytes=60 * 1024 * 1024
+        ),
+        cost_estimate=pl.CostEstimate(
+            flops=20_000_000_000, bytes_accessed=100_000_000, transcendentals=0
+        ),
         name="expert_grads",
-    )(xs, dys, hid, gg, gu)
+    )(*xs, *dys, *hid, *gg, *gu, *moves)
 
 
 def on_device(
@@ -1003,9 +1320,12 @@
     routes_t = jnp.pad(routes.T, ((0, 8 - TOP), (0, 0)), constant_values=-1)
     units = s_gate.shape[1]
     shared = jnp.concatenate([s_gate, s_up], axis=1)
-    full, dy_all, routes_all, sgu = first_gather(
-        bundle, cotangent, routes_t, shared, 0, rows_n, cols_n
+    per_row = s_down.shape[0] // units
+    downs = s_down.reshape(per_row, units, s_down.shape[1])
+    full, dy_all, routes_all, sgu, sdown = first_gather(
+        bundle, cotangent, routes_t, shared, downs, 0, rows_n, cols_n
     )
+    sdown = jnp.swapaxes(sdown, 0, 1).reshape(units, width)
     sgu = sgu.reshape(width, 2 * units)
 
     def piece(lo, extent):
@@ -1024,18 +1344,6 @@
     egate = lax.all_gather(e_gate, "row", axis=1, tiled=True)
     eup = lax.all_gather(e_up, "row", axis=1, tiled=True)
     edown = lax.all_gather(e_down, "row", axis=2, tiled=True)
-    per_row = s_down.shape[0] // units
-    sdown_cols = lax.all_gather(s_down, "col", axis=1, tiled=True)
-    sdown_mine = lax.dynamic_slice_in_dim(sdown_cols, (col_here % per_row) * units, units, 0)
-    sdown = lax.dynamic_index_in_dim(
-        lax.all_gather(sdown_mine, "row", axis=0), col_here // per_row, 0, keepdims=False
-    )
-
-    mine = col_here * EXP_DEV + jnp.arange(EXP_DEV, dtype=jnp.int32)
-    hit = jnp.any(routes_all[:, None, :TOP, :] == mine[None, :, None, None], axis=2)
-    rank = jnp.where(hit, jnp.cumsum(hit.astype(jnp.int32), axis=2) - 1, -1)
-    rank = jnp.pad(rank, ((0, 0), (0, 8 - EXP_DEV), (0, 0)), constant_values=-1)
-
     own_lens = lengths[deal.reshape(-1) * cols_n + col_here, row_here]
     seq_ends = jnp.cumsum(own_lens)
     places = jnp.arange(total, dtype=jnp.int32)
@@ -1063,13 +1371,33 @@
 
     gates_t = jnp.pad(gate_weights.T, ((0, 8 - TOP), (0, 0)))
     x_all, gates_all = line_gather([normed_two, gates_t], 1, rows_n, cols_n)
-    out_part, gx_part, xs, dys, hid, gg, gu, ggw, grad_sh = routed(
-        x_all, dy_all, routes_all, gates_all, rank, egate, eup, edown, sgu, sdown
+    chips = cols_n // 2
+    my_order = jnp.array(round_tables(chips)[0], jnp.int32)[col_here // 2]
+    routes_rows = jnp.swapaxes(routes_all, 1, 2)
+    gx_sum, moe_sum = LineRounds(cols_n), LineRounds(cols_n)
+    saved, ggw, grad_sh = [], 0.0, 0.0
+    for call in range(chips):
+        moves = gx_sum.outgoing(call - 1) if call else ()
+        own, other, *keep = routed(
+            call, rows_n, x_all, dy_all, routes_all, routes_rows, gates_all, egate, eup, edown,
+            sgu, sdown, moves,
+        )
+        saved.append(keep[:5])
+        ggw_part, sh_part, *arrivals = keep[5:]
+        if call:
+            gx_sum.arrived(*arrivals)
+        grad_sh = grad_sh + sh_part
+        is_unit = jnp.arange(chips, dtype=jnp.int32)[:, None, None, None] == my_order[call]
+        ggw = ggw + jnp.where(is_unit, ggw_part[None], 0.0)
+        gx_sum.add(own[1], other[1])
+        moe_sum.add(own[0], other[0])
+    gx = gx_sum.result()
+    grad_egate, grad_eup, grad_edown, below, above = expert_grads(
+        *zip(*saved), rows_n, cols_n, moe_sum.outgoing(0), 3
     )
-    grad_egate, grad_eup, grad_edown = expert_grads(xs, dys, hid, gg, gu)
-    ggw = ggw[:, :EXP_DEV]
-
-    gx = line_sum(gx_part, 2, rows_n, cols_n)
+    moe_sum.arrived(below, above)
+    ggw = ggw.reshape(cols_n, 8, total)[:, :EXP_DEV]
+
     ggw_home = lax.all_to_all(ggw, "col", split_axis=0, concat_axis=0, tiled=True)
     ggw_home = ggw_home.reshape(experts, total).T
 
@@ -1078,41 +1406,35 @@
         grad_gates - jnp.sum(gate_weights * grad_gates, axis=-1, keepdims=True)
     )
     grad_logits = jnp.sum(route_picks * grad_chosen[:, :, None], axis=1).astype(BF)
-    grad_router = mm_tn(grad_logits, normed_two)
     grad_normed_two = gx + mm(grad_logits, router_t)
     grad_two, grad_gain_moe = norm_back(grad_normed_two, unit_two, scale_two, gain_moe)
     grad_after = cotangent.astype(F32) + grad_two
     grad_attn_b = grad_after.astype(BF)
-    grad_wout = mm_tn(grad_attn_b, mixed)
     grad_mixed = mm(grad_attn_b, wo_t).astype(BF)
     gq, gk, gv = attend_backward(queries, keys, values, grad_mixed, segment, log_totals)
-    grad_wq = mm_tn(gq, normed_one)
-    grad_wk = mm_tn(gk, normed_one)
-    grad_wv = mm_tn(gv, normed_one)
     grad_normed_one = mm(gq, wq_t) + mm(gk, wk_t) + mm(gv, wv_t)
     grad_one, grad_gain_attn = norm_back(grad_normed_one, unit_one, scale_one, gain_attn)
     grad_tokens = grad_after + grad_one
 
-    moe = line_sum(out_part, 3, rows_n, cols_n)
-    output = (after_attn + moe).astype(BF)
-
-    def cut(grad):
-        extent = grad.shape[0] // cols_n
-        part = grad.astype(BF).reshape(cols_n // 2, 2, extent, rows_n, inner)
-        return part.transpose(1, 3, 0, 2, 4)
-
-    def cut_gain(grad):
-        part = grad.astype(BF).reshape(rows_n, cols_n // 2, 2, 1, n_gain)
-        part = jnp.pad(part, ((0, 0),) * 4 + ((0, inner - n_gain),))
-        return part.transpose(2, 0, 1, 3, 4)
-
-    grads = [cut(grad_wq), cut(grad_wk), cut(grad_wv), cut(grad_wout), cut(grad_router)]
-    grads += [cut_gain(grad_gain_attn), cut_gain(grad_gain_moe)]
-    blank = 16 - EXP_DEV - 2
-    grads.append(jnp.zeros((2, rows_n, cols_n // 2, blank, inner), BF))
-    grads = jnp.concatenate(grads, axis=3)
+    rounds = [moe_sum.outgoing(1)] + [moe_sum.kept(turn) for turn in range(2, chips - 1)]
+
+    def gain_rows(grad):
+        part = grad.reshape(rows_n, cols_n, 1, n_gain)
+        return jnp.pad(part, ((0, 0),) * 3 + ((0, inner - n_gain),))
+
+    tails = jnp.concatenate([gain_rows(grad_gain_attn), gain_rows(grad_gain_moe)], axis=2)
+    tails = jnp.pad(tails, ((0, 0), (0, 0), (EXP_DEV, 16 - EXP_DEV - 2), (0, 0)))
+    tails = tails.reshape(rows_n, cols_n * 16, inner)
+    logits_left = grad_logits.reshape(total, cols_n, EXP_DEV)
+    logits_left = jnp.pad(logits_left, ((0, 0), (0, 0), (0, 16 - EXP_DEV)))
     grads_sh = grad_sh.astype(BF).reshape(rows_n, inner, 3 * units)
-    dense, dense_sh = dense_sum(grads, grads_sh, 4, rows_n, cols_n)
+    dense, dense_sh, sd_parts, arrivals = dense_sum(
+        [gq, gk, gv, grad_attn_b, logits_left.reshape(total, cols_n * 16)],
+        [normed_one, normed_one, normed_one, mixed, normed_two],
+        tails, grads_sh, rounds, 2, rows_n, cols_n,
+    )
+    moe_sum.arrived(arrivals[-1, 0], arrivals[-1, 1])
+    output = (after_attn + moe_sum.result()).astype(BF)
     out_wq = dense[:q_w].T
     out_wk = dense[q_w : q_w + k_w].T
     out_wv = dense[q_w + k_w : q_w + 2 * k_w].T
@@ -1121,30 +1443,15 @@
     out_g_attn = dense[t_at + EXP_DEV, :n_gain]
     out_g_moe = dense[t_at + EXP_DEV + 1, :n_gain]
     out_sg = dense_sh[:, :units]
-    out_su = dense_sh[:, units : 2 * units]
-    sd_rows = dense_sh[:, 2 * units :].astype(BF).reshape(per_row, inner // per_row, units)
-    lands = []
-    for turn in range(per_row):
-        moves = [
-            (rr * cols_n + cc, (cc // per_row) * cols_n + per_row * rr + (cc + turn) % per_row)
-            for rr in range(rows_n)
-            for cc in range(cols_n)
-        ]
-        part = lax.dynamic_index_in_dim(sd_rows, (col_here + turn) % per_row, 0, keepdims=False)
-        lands.append(lax.ppermute(part, ("row", "col"), moves))
-    lands = jnp.stack(lands)
-    turns = (col_here - jnp.arange(per_row, dtype=jnp.int32)) % per_row
-    out_sd = jnp.take(lands, turns, axis=0).transpose(0, 2, 1)
-    out_sd = out_sd.reshape(per_row * units, inner // per_row).astype(F32)
-
-    def row_sum(grad, dim):
-        return lax.psum_scatter(
-            grad.astype(BF), "row", scatter_dimension=dim, tiled=True
-        ).astype(F32)
-
-    out_eg = row_sum(grad_egate, 1)
-    out_eu = row_sum(grad_eup, 1)
-    out_ed = row_sum(grad_edown, 2)
+    out_su = dense_sh[:, units:]
+    out_sd = sd_parts.transpose(0, 2, 1).reshape(per_row * units, inner // per_row)
+
+    def row_sum(grad):
+        return lax.psum_scatter(grad, "row", scatter_dimension=0).astype(F32)
+
+    out_eg = row_sum(grad_egate)
+    out_eu = row_sum(grad_eup)
+    out_ed = row_sum(grad_edown)
     return (
         output,
         grad_tokens,

time: 1070 us -> 932 us (0.87)
  local copies, waits for them, and re-layouts: 192 us -> 67.1 us
  Pallas kernels: 735 us -> 649 us
  waiting for transfers between devices: 3.16 us -> 58 us
  other arithmetic: 28.6 us -> 82.8 us
  starting transfers between devices: 19.9 us -> 3.77 us
  blocking collectives: 16 us -> 0 us
  matrix products: 45.2 us -> 32.3 us
  between operations: 15.6 us -> 27.6 us
    pallas_call x6 -> x7, Pallas kernels: 603 us -> 514 us  [the longest x4 163 us: routed(): pl.pallas_call(functools.partial(routed_kernel, call, rows_n, cols_n, len...]
    concatenate x1 -> x0, local copies, waits for them, and re-layouts: 69.9 us -> none  [on_device(): grads = jnp.concatenate(grads, axis=3)]
    convert_element_type x5 -> x15, other arithmetic: 9.67 us -> 66.6 us  [the longest x8 42.1 us: outgoing(): return (ups.astype(BF), downs.astype(BF))]
    unnamed x8 -> x9, waiting for transfers between devices: 3.14 us -> 57.9 us
    reshape x6 -> x5, local copies, waits for them, and re-layouts: 26.6 us -> 3.5 us  [the longest x1 1.62 us: on_device(): sd_parts.transpose(0, 2, 1).reshape(per_row * units, inner // per_row)]
    dot_general x5 -> x0, matrix products: 18.7 us -> none  [mm_tn(): lax.dot_general(left, right, (((0,), (0,)), ((), ())), preferred_element_...]
    ppermute x2 -> x0, starting transfers between devices: 16.3 us -> none  [on_device(): lands.append(lax.ppermute(part, ('row', 'col'), moves))]
    all_gather x1 -> x0, blocking collectives: 16 us -> none  [on_device(): sdown_cols = lax.all_gather(s_down, 'col', axis=1, tiled=True)]
  transfers between devices with their start and end apart: 10 -> 7, of which waited for: 0 -> 1; matrix products, arithmetic and copies ran while one was open for 23% -> 15% of each run, Pallas kernels for 56% -> 48%
where the time goes in v3:
time: 932 us; the launch traced here: 920 us
  Pallas kernels  649 us (70%)
  other arithmetic  82.8 us (9%)
  local copies, waits for them, and re-layouts  67.1 us (7%)
  waiting for transfers between devices  58 us (6%)
  matrix products  32.3 us (3%)
  between operations  27.6 us (3%)
    pallas_call x4, Pallas kernels, routed(): pl.pallas_call(functools.partial(routed_kernel, call, rows_n, cols_n, len...  163 us
    pallas_call x1, Pallas kernels, first_gather(): pl.pallas_call(kernel, in_specs=[ANY] * 5, out_specs=[ANY] * 5, out_shape...  156 us
    pallas_call x1, Pallas kernels, dense_sum(): pl.pallas_call(kernel, in_specs=[vmem] * (2 * n + 1) + [ANY] * (1 + 2 * n...  152 us
    pallas_call x1, Pallas kernels, line_gather(): pl.pallas_call(kernel, in_specs=[ANY] * n, out_specs=[ANY] * n, out_shape...  113 us
    unnamed x9, waiting for transfers between devices  57.9 us
    pallas_call x1, Pallas kernels, expert_grads(): pl.pallas_call(functools.partial(expert_grads_kernel, units_n, lambda: Pl...  42.1 us
    convert_element_type x8, other arithmetic, outgoing(): return (ups.astype(BF), downs.astype(BF))  42.1 us
    transpose x8, local copies, waits for them, and re-layouts, piece(): return part.transpose(1, 2, 0, 3).reshape(cols_n * extent, width)  23 us
  transfers between devices with their start and end apart: 7, of which 1 were waited for; matrix products, arithmetic and copies ran while one was open for 15% of the time, Pallas kernels for 48%

profile of v3, /device:TPU:2, one launch (start us, length us, event | category | flops | bytes accessed | tf_op | source)
XLA Modules:
  0.0 920.2 jit_solution(3678197505364871004)
XLA Ops:
  20.5 156.2 %first_gather.1 = (bf16[4,8,528,384]{3,2,1,0:T(8,128)(2,1)}, bf16[8,512,1536]{2,1,0:T(8,128)(2,1)}, s32[8,8,512]{2,1,0:T(8,128)}, bf16[4,384,256]{2,1,0:T(8,128)(2,1)}, bf16[8,128,192]{2,1,0:T(8,128)(2,1)}) custom-call(bf16[528,384]{1,0:T(8,128)(2,1)} %copy-done.45, bf16[512,1536]{1,0:T(8,128)(2,1)} %dy_ref.1, s32[8,512]{1,0:T(8,128)} %pad.34.rt_ref, ...), custom_call_target="tpu_custom_call" | custom-call | tf_op jit(solution)/shard_map/first_gather/pallas_call | solution.py:509
  176.8 1.0 convert_reduce_fusion
  177.9 2.2 slice_bitcast_fusion.2
  180.1 1.2 copy.91
  181.3 1.4 copy.107
  182.7 1.2 copy.90
  183.9 1.4 copy.106
  185.3 7.1 slice_bitcast_fusion
  192.4 3.6 copy.89
  196.0 2.9 copy.105
  200.1 6.6 copy.93
  206.7 3.0 copy.108
  209.8 1.0 slice_bitcast_fusion.8
  211.9 3.5 convolution_convert_fusion.2.v_ref
  215.4 1.0 convolution_convert_fusion.3.k_ref
  216.5 2.6 convolution_convert_fusion.1.q_ref
  219.2 7.3 attend_forward.1
  226.5 5.3 multiply_reduce_fusion.2
  234.8 113.4 %line_gather.1 = (bf16[8,512,1536]{2,1,0:T(8,128)(2,1)}, f32[8,8,512]{2,1,0:T(8,128)}) custom-call(bf16[512,1536]{1,0:T(8,128)(2,1)} %copy-done.33, f32[8,512]{1,0:T(8,128)} %pad.35.refs_1_), custom_call_target="tpu_custom_call" | custom-call | tf_op jit(solution)/shard_map/line_gather/pallas_call | solution.py:375
  348.3 2.8 copy.95
  351.4 0.9 copy.100.refs_9_
  353.7 38.0 %routed.4 = (bf16[2,512,1536]{2,1,0:T(8,128)(2,1)}, bf16[2,512,1536]{2,1,0:T(8,128)(2,1)}, bf16[4,256,1536]{2,1,0:T(8,128)(2,1)}, bf16[4,256,1536]{2,1,0:T(8,128...) custom-call(bf16[8,512,1536]{2,1,0:T(8,128)(2,1)} %get-tuple-element, ...), custom_call_target="tpu_custom_call" | custom-call | flops 24000000000 | bytes 100000000 | tf_op jit(solution)/shard_map/routed/pallas_call | solution.py:1149
  391.7 3.4 fusion.27.refs_10_.refs_11_
  395.1 42.2 %routed.5 = (bf16[2,512,1536]{2,1,0:T(8,128)(2,1)}, bf16[2,512,1536]{2,1,0:T(8,128)(2,1)}, bf16[4,256,1536]{2,1,0:T(8,128)(2,1)}, bf16[4,256,1536]{2,1,0:T(8,128...) custom-call(bf16[8,512,1536]{2,1,0:T(8,128)(2,1)} %get-tuple-element, ...), custom_call_target="tpu_custom_call" | custom-call | flops 24000000000 | bytes 100000000 | tf_op jit(solution)/shard_map/routed/pallas_call | solution.py:1149
  437.3 5.6 fusion.24
  442.9 41.4 %routed.6 = (bf16[2,512,1536]{2,1,0:T(8,128)(2,1)}, bf16[2,512,1536]{2,1,0:T(8,128)(2,1)}, bf16[4,256,1536]{2,1,0:T(8,128)(2,1)}, bf16[4,256,1536]{2,1,0:T(8,128...) custom-call(bf16[8,512,1536]{2,1,0:T(8,128)(2,1)} %get-tuple-element, ...), custom_call_target="tpu_custom_call" | custom-call | flops 24000000000 | bytes 100000000 | tf_op jit(solution)/shard_map/routed/pallas_call | solution.py:1149
  484.4 6.0 fusion.22.refs_11_
  491.0 0.9 copy-done.19
  491.9 0.9 copy-done.22
  492.8 4.0 fusion.23.refs_10_
  496.8 41.9 %routed.7 = (bf16[2,512,1536]{2,1,0:T(8,128)(2,1)}, bf16[2,512,1536]{2,1,0:T(8,128)(2,1)}, bf16[4,256,1536]{2,1,0:T(8,128)(2,1)}, bf16[4,256,1536]{2,1,0:T(8,128...) custom-call(bf16[8,512,1536]{2,1,0:T(8,128)(2,1)} %get-tuple-element, ...), custom_call_target="tpu_custom_call" | custom-call | flops 24000000000 | bytes 100000000 | tf_op jit(solution)/shard_map/routed/pallas_call | solution.py:1149
  538.7 6.6 fusion.17.refs_21_
  545.6 1.1 copy-done.20
  546.6 0.9 copy-done.23
  547.5 4.5 fusion.18.refs_20_
  552.0 42.1 %expert_grads.1 = (bf16[4,4,384,512]{3,2,1,0:T(8,128)(2,1)}, bf16[4,4,384,512]{3,2,1,0:T(8,128)(2,1)}, bf16[4,4,512,384]{3,2,1,0:T(8,128)(2,1)}, bf16[512,1536]{1,0:T(8,128)(2,1)}, bf16[512,1536]{1,0:T(8,128)(2,1)}) custom-call(bf16[4,256,1536]{2,1,0:T(8,128)(2,1)} %get-tuple-element.112.refs_0_, bf16[4,256,1536]{2,1,0:T(8,128)(2,1)} %get-tuple-element.113.refs_1_, ...), custom_call_target="tpu_custom_call" | custom-call | flops 20000000000 | bytes 100000000 | tf_op jit(solution)/shard_map/expert_grads/pallas_call | solution.py:1251
  603.2 6.4 fusion.13.refs_15_
  609.7 6.5 fusion.14.refs_14_
  617.1 3.5 all-to-all-start
  620.7 7.1 fusion.16.refs_13_
  628.5 0.9 copy-done.21
  630.3 1.1 copy-done.25
  631.5 5.0 fusion.20.refs_12_
  636.5 1.0 copy-done.41
  637.5 1.5 add_convert_fusion
  639.3 4.9 multiply_reduce_fusion
  645.9 7.7 convolution_convert_fusion.gm_ref
  653.7 14.3 %attend_backward.1 = (bf16[512,1536]{1,0:T(8,128)(2,1)S(1)}, bf16[512,512]{1,0:T(8,128)(2,1)S(1)}, bf16[512,512]{1,0:T(8,128)(2,1)S(1)}) custom-call(bf16[512,1536]{1,0:T(8,128)(2,1)} %copy-done.2, bf16[512,512]{1,0:T(8,128)(2,1)S(1)} %copy-done.6, bf16[512,512]{1,0:T(8,128)(2,1)S(1)} %copy-done.4, bf16[512,1536]{1,0:T(8,128)(2,1)} %convolution_convert_fusion.gm_ref, ...), custom_call_target="tpu_custom_call" | custom-call | tf_op jit(solution)/shard_map/attend_backward/pallas_call | solution.py:137
  668.1 2.6 fusion.52
  670.8 1.0 convolution_add_fusion.2
  672.6 3.0 fusion.6
  675.9 1.0 pad.39
  677.7 151.8 %dense_sum.1 = (f32[528,384]{1,0:T(8,128)}, f32[384,256]{1,0:T(8,128)}, f32[2,192,128]{2,1,0:T(8,128)}, bf16[2,2,512,1536]{3,2,1,0:T(8,128)(2,1)}) custom-call(bf16[512,1536]{1,0:T(8,128)(2,1)} %copy-done.12, bf16[512,512]{1,0:T(8,128)(2,1)} %copy-done.7, bf16[512,512]{1,0:T(8,128)(2,1)} %copy-done.8, bf16[512,1536]{1,0:T(8,128)(2,1)} %copy-done.43, ...), custom_call_target="tpu_custom_call" | custom-call | flops 6442450944 | bytes 350000000 | tf_op jit(solution)/shard_map/dense_sum/pallas_call | solution.py:853
  829.5 1.3 slice_bitcast_fusion.10
  830.8 1.3 slice_bitcast_fusion.9
  832.1 1.6 slice_bitcast_fusion.6
  833.8 1.6 copy_bitcast_fusion
  835.4 1.8 fusion.47
  837.2 1.9 slice_bitcast_fusion.4
  839.1 8.2 fusion.9
  847.3 3.3 bitcast_convert_fusion
  850.6 3.5 bitcast_convert_fusion.1
  854.1 55.3 %reduce-scatter.10.cloned.1.call-done = bf16[1,4,384,512]{3,2,1,0:T(8,128)(2,1)} async-done(((bf16[4,4,384,512]{3,2,1,0:T(8,128)(2,1)}), bf16[1,4,384,512]{3,2,1,0:T(8,128)(2,1)}) %reduce-scatter.10.cloned.1.call-update) | async-done | bytes 1572880
  909.4 3.5 bitcast_convert_fusion.2
  (247 shorter events, 24.6 us)
Async XLA Ops:
  7.2 191.8 %copy-start = (s32[32,4]{0,1:T(4,128)S(1)}, s32[32,4]{0,1:T(4,128)}, u32[]{:S(2)}) copy-start(s32[32,4]{0,1:T(4,128)} %param.39) | copy-start | bytes 1540
  7.2 10.9 %copy-start.59 = (bf16[256,192]{0,1:T(8,128)(2,1)S(1)}, bf16[256,192]{0,1:T(8,128)(2,1)}, u32[]{:S(2)}) copy-start(bf16[256,192]{0,1:T(8,128)(2,1)} %param.36) | copy-start | bytes 294916
  7.2 11.7 %copy-start.51 = (s32[512,6]{0,1:T(8,128)S(1)}, s32[512,6]{0,1:T(8,128)}, u32[]{:S(2)}) copy-start(s32[512,6]{0,1:T(8,128)} %param.37) | copy-start | bytes 36868
  7.2 12.3 %copy-start.78 = (bf16[48]{0:T(256)(128)(2,1)S(1)}, bf16[48]{0:T(256)(128)(2,1)}, u32[]{:S(2)}) copy-start(bf16[48]{0:T(256)(128)(2,1)} %param.24) | copy-start | bytes 292
  7.2 12.3 %copy-start.77 = (bf16[48]{0:T(256)(128)(2,1)S(1)}, bf16[48]{0:T(256)(128)(2,1)}, u32[]{:S(2)}) copy-start(bf16[48]{0:T(256)(128)(2,1)} %param.29) | copy-start | bytes 292
  7.2 12.3 %copy-start.53 = (bf16[384,192]{0,1:T(8,128)(2,1)S(1)}, bf16[384,192]{0,1:T(8,128)(2,1)}, u32[]{:S(2)}) copy-start(bf16[384,192]{0,1:T(8,128)(2,1)} %param.25) | copy-start | bytes 442372
  7.3 12.3 %copy-start.64 = (bf16[384,64]{0,1:T(8,128)(2,1)S(1)}, bf16[384,64]{0,1:T(8,128)(2,1)}, u32[]{:S(2)}) copy-start(bf16[384,64]{0,1:T(8,128)(2,1)} %param.26) | copy-start | bytes 147460
  7.3 12.3 %copy-start.65 = (bf16[384,64]{0,1:T(8,128)(2,1)S(1)}, bf16[384,64]{0,1:T(8,128)(2,1)}, u32[]{:S(2)}) copy-start(bf16[384,64]{0,1:T(8,128)(2,1)} %param.27) | copy-start | bytes 147460
  7.3 12.3 %copy-start.54 = (bf16[384,192]{0,1:T(8,128)(2,1)S(1)}, bf16[384,192]{0,1:T(8,128)(2,1)}, u32[]{:S(2)}) copy-start(bf16[384,192]{0,1:T(8,128)(2,1)} %param.28) | copy-start | bytes 442372
  7.3 12.4 %copy-start.76 = (bf16[384,4]{0,1:T(4,128)(2,1)S(1)}, bf16[384,4]{0,1:T(4,128)(2,1)}, u32[]{:S(2)}) copy-start(bf16[384,4]{0,1:T(4,128)(2,1)} %param.30) | copy-start | bytes 9220
  7.3 12.4 %copy-start.61 = (bf16[384,128]{1,0:T(8,128)(2,1)S(1)}, bf16[384,128]{1,0:T(8,128)(2,1)}, u32[]{:S(2)}) copy-start(bf16[384,128]{1,0:T(8,128)(2,1)} %param.34) | copy-start | bytes 294916
  7.3 12.4 %copy-start.60 = (bf16[384,128]{1,0:T(8,128)(2,1)S(1)}, bf16[384,128]{1,0:T(8,128)(2,1)}, u32[]{:S(2)}) copy-start(bf16[384,128]{1,0:T(8,128)(2,1)} %param.35) | copy-start | bytes 294916
  7.3 346.3 %all-gather.4.cloned.1.call-start = ((), (), s32[]{:S(2)}) async-start(), calls=%async_computation.4 | async-start | bytes 7864320 | tf_op jit(solution)/shard_map/all_gather | solution.py:1344
  8.0 345.6 %all-gather.6.cloned.1.call-start = ((), (), s32[]{:S(2)}) async-start(), calls=%async_computation.5 | async-start | bytes 7864320 | tf_op jit(solution)/shard_map/all_gather | solution.py:1345
  8.8 344.9 %all-gather.8.cloned.1.call-start = ((), (), s32[]{:S(2)}) async-start(), calls=%async_computation.6 | async-start | bytes 7864320 | tf_op jit(solution)/shard_map/all_gather | solution.py:1346
  9.5 837.8 %reduce-scatter.14.cloned.1.call-start = ((), (), s32[]{:S(2)}) async-start(), calls=%async_computation.9 | async-start | bytes 7864320
  177.9 33.4 %copy-start.55 = (f32[1536]{0:T(1024)}, f32[1536]{0:T(1024)S(1)}, u32[]{:S(2)}) copy-start(f32[1536]{0:T(1024)S(1)} %reshape.423) | copy-start | bytes 18436
  199.9 19.2 %copy-start.9 = (s32[512]{0:T(512)}, s32[512]{0:T(512)S(1)}, u32[]{:S(2)}) copy-start(s32[512]{0:T(512)S(1)} %convert_reduce_fusion.2) | copy-start | bytes 6148
  209.8 22.1 %copy-start.57 = (f32[1536]{0:T(1024)}, f32[1536]{0:T(1024)S(1)}, u32[]{:S(2)}) copy-start(f32[1536]{0:T(1024)S(1)} %reshape.424) | copy-start | bytes 18436
  210.9 21.4 %copy-start.49 = (bf16[4,8,4,384]{3,1,2,0:T(8,128)(2,1)}, bf16[4,8,4,384]{3,1,2,0:T(8,128)(2,1)S(1)}, u32[]{:S(2)}) copy-start(bf16[4,8,4,384]{3,1,2,0:T(8,128)(2,1)S(1)} %copy.109) | copy-start | bytes 294916
  210.9 5.6 slice-start
  211.9 4.6 copy-start.44
  211.9 4.6 slice-start.1
  219.1 12.7 %copy-start.2 = (bf16[512,1536]{1,0:T(8,128)(2,1)}, bf16[512,1536]{1,0:T(8,128)(2,1)S(1)}, u32[]{:S(2)}) copy-start(bf16[512,1536]{1,0:T(8,128)(2,1)S(1)} %convolution_convert_fusion.1.q_ref) | copy-start | bytes 4718596
  226.5 5.3 copy-start.11
  232.2 118.9 %copy-start.48 = (bf16[8,128,192]{2,1,0:T(8,128)(2,1)S(1)}, bf16[8,128,192]{2,1,0:T(8,128)(2,1)}, u32[]{:S(2)}) copy-start(bf16[8,128,192]{2,1,0:T(8,128)(2,1)} %get-tuple-element.85) | copy-start | bytes 1179652
  233.6 158.1 %copy-start.46 = (f32[512,6]{0,1:T(8,128)}, f32[512,6]{0,1:T(8,128)S(1)}, u32[]{:S(2)}) copy-start(f32[512,6]{0,1:T(8,128)S(1)} %select_reduce_fusion.2) | copy-start | bytes 36868
  233.6 158.1 %copy-start.62 = (f32[512]{0:T(512)}, f32[512]{0:T(512)S(1)}, u32[]{:S(2)}) copy-start(f32[512]{0:T(512)S(1)} %reduce_max.9) | copy-start | bytes 6148
  484.3 6.0 copy-start.13
  484.3 6.6 copy-start.16
  484.3 7.5 copy-start.19
  484.4 8.4 copy-start.22
  538.6 6.6 copy-start.14
  538.7 6.9 copy-start.17
  538.7 8.0 copy-start.20
  538.7 8.9 copy-start.23
  594.1 256.5 %reduce-scatter.12.cloned.1.call-start = ((), (), s32[]{:S(2)}) async-start(), calls=%async_computation.8 | async-start | bytes 7864320
  594.7 314.7 %reduce-scatter.10.cloned.1.call-start = ((), (), s32[]{:S(2)}) async-start(), calls=%async_computation.7 | async-start | bytes 7864320
  609.6 6.6 copy-start.73
  609.6 6.6 copy-start.72
  609.6 6.6 copy-start.71
  609.7 6.6 copy-start.70
  609.7 18.1 %copy-start.42 = (bf16[512,1536]{1,0:T(8,128)(2,1)S(1)}, bf16[512,1536]{1,0:T(8,128)(2,1)}, u32[]{:S(2)}) copy-start(bf16[512,1536]{1,0:T(8,128)(2,1)} %get-tuple-element.132) | copy-start | bytes 4718596
  617.1 21.9 %all-to-all-start = ((f32[8,4,512]{2,1,0:T(4,128)}), f32[8,4,512]{2,1,0:T(4,128)S(1)}, u32[]{:S(2)}, u32[]{:S(2)}) async-start(f32[8,4,512]{2,1,0:T(4,128)} %fusion.29), calls=%async_computation | async-start | bytes 131072 | tf_op jit(solution)/shard_map/all_to_all | solution.py:1401
  620.6 7.1 copy-start.15
  620.6 7.9 copy-start.18
  620.6 8.8 copy-start.21
  620.6 9.7 %copy-start.24 = (bf16[2,512,1536]{2,1,0:T(8,128)(2,1)S(1)}, bf16[2,512,1536]{2,1,0:T(8,128)(2,1)}, u32[]{:S(2)}) copy-start(bf16[2,512,1536]{2,1,0:T(8,128)(2,1)} %get-tuple-element.89) | copy-start | bytes 9437188
  620.7 10.8 %copy-start.25 = (bf16[2,512,1536]{2,1,0:T(8,128)(2,1)S(1)}, bf16[2,512,1536]{2,1,0:T(8,128)(2,1)}, u32[]{:S(2)}) copy-start(bf16[2,512,1536]{2,1,0:T(8,128)(2,1)} %get-tuple-element.92) | copy-start | bytes 9437188
  631.4 5.0 copy-start.38
  631.4 5.0 copy-start.39
  631.4 5.1 copy-start.40
  631.4 6.0 copy-start.41
  639.3 5.0 copy-start.28
  639.3 5.3 copy-start.32
  644.6 23.5 %slice-start.2 = ((s8[4718592]{0:T(1024)(128)(4,1)}), s8[4194304]{0:T(1024)(128)(4,1)S(1)}, s32[]{:S(2)}) async-start(s8[4718592]{0:T(1024)(128)(4,1)} %bitcast.218), calls=%async_computation.12 | async-start | bytes 8388608
  645.9 7.8 copy-start.43
  645.9 7.8 copy-start.4
  645.9 7.8 copy-start.6
  645.9 7.8 copy-start.10
  645.9 22.2 %slice-start.3 = ((s8[4718592]{0:T(1024)(128)(4,1)}), s8[524288]{0:T(1024)(128)(4,1)S(1)}, s32[]{:S(2)}) async-start(s8[4718592]{0:T(1024)(128)(4,1)} %bitcast.218), calls=%async_computation.13 | async-start | bytes 1048576
  677.7 161.4 %copy-start.26 = (bf16[2,512,1536]{2,1,0:T(8,128)(2,1)S(1)}, bf16[2,512,1536]{2,1,0:T(8,128)(2,1)}, u32[]{:S(2)}) copy-start(bf16[2,512,1536]{2,1,0:T(8,128)(2,1)} %get-tuple-element.96) | copy-start | bytes 9437188
  829.5 9.6 %copy-start.31 = (bf16[512,1536]{1,0:T(8,128)(2,1)S(1)}, bf16[512,1536]{1,0:T(8,128)(2,1)}, u32[]{:S(2)}) copy-start(bf16[512,1536]{1,0:T(8,128)(2,1)} %param.23) | copy-start | bytes 4718596
  850.6 62.3 %copy-start.1 = (s32[32,4]{0,1:T(4,128)S(1)}, s32[32,4]{0,1:T(4,128)}, u32[]{:S(2)}) copy-start(s32[32,4]{0,1:T(4,128)} %param.39) | copy-start | bytes 1540
  (27 other events, 57.2 us)
Sparse Core Ops, SparseCore 0:
  10.0 147.0 all-gather.3
  158.9 76.0 all-gather.5
  236.8 69.9 all-gather.7
  594.3 87.7 reduce-scatter.13
  684.9 150.4 reduce-scatter.11
  838.2 71.1 reduce-scatter.9

commit v4 on v3

--- a/solution.py
+++ b/solution.py
@@ -61,12 +61,13 @@
     return (seg_col == seg_row) & (k_at <= q_at)
 
 
-def attend_forward_kernel(q_ref, k_ref, v_ref, segc_ref, segr_ref, mixed_ref, lse_ref):
-    allowed = allowed_mask(segc_ref[...], segr_ref[...])
-    keys = k_ref[...]
-    values = v_ref[...]
+def attend_forward_group(h, q_ref, k_ref, v_ref, allowed, mixed_ref, lse_ref):
+    here = pl.ds(pl.multiple_of(h * HEAD_SIZE, HEAD_SIZE), HEAD_SIZE)
+    keys = k_ref[:, here]
+    values = v_ref[:, here]
     for g in range(GROUP):
-        cols = slice(g * HEAD_SIZE, (g + 1) * HEAD_SIZE)
+        at = pl.multiple_of((h * GROUP + g) * HEAD_SIZE, HEAD_SIZE)
+        cols = pl.ds(at, HEAD_SIZE)
         scores = mm_nt(q_ref[:, cols], keys) * HEAD_SIZE ** (-0.5)
         scores = jnp.where(allowed, scores, masked_score)
         peak = jnp.max(scores, axis=-1, keepdims=True)
@@ -74,79 +75,302 @@
         total = jnp.sum(raw, axis=-1, keepdims=True)
         probs = (raw * (1.0 / total)).astype(BF)
         mixed_ref[:, cols] = mm(probs, values).astype(BF)
-        lse_ref[0, :, g : g + 1] = peak + jnp.log(total)
-
-
-def attend_backward_kernel(
-    q_ref, k_ref, v_ref, gm_ref, segc_ref, segr_ref, lse_ref, gq_ref, gk_ref, gv_ref
-):
-    allowed = allowed_mask(segc_ref[...], segr_ref[...])
-    keys = k_ref[...]
-    values = v_ref[...]
+        lse_ref[h, :, g : g + 1] = peak + jnp.log(total)
+
+
+def attend_backward_group(h, q_ref, k_ref, v_ref, gm_ref, allowed, lse_ref, gq_ref, gk_ref, gv_ref):
+    here = pl.ds(pl.multiple_of(h * HEAD_SIZE, HEAD_SIZE), HEAD_SIZE)
+    keys = k_ref[:, here]
+    values = v_ref[:, here]
     scale = HEAD_SIZE ** (-0.5)
-    grad_key = None
+    grad_key = grad_value = None
     for g in range(GROUP):
-        cols = slice(g * HEAD_SIZE, (g + 1) * HEAD_SIZE)
+        at = pl.multiple_of((h * GROUP + g) * HEAD_SIZE, HEAD_SIZE)
+        cols = pl.ds(at, HEAD_SIZE)
         query = q_ref[:, cols]
         grad_mixed = gm_ref[:, cols]
         scores = mm_nt(query, keys) * scale
-        probs = jnp.where(allowed, jnp.exp(scores - lse_ref[0, :, g : g + 1]), 0.0)
+        probs = jnp.where(allowed, jnp.exp(scores - lse_ref[h, :, g : g + 1]), 0.0)
         grad_probs = mm_nt(grad_mixed, values)
         inner = jnp.sum(probs * grad_probs, axis=-1, keepdims=True)
         grad_scores = (probs * (grad_probs - inner)).astype(BF)
         gq_ref[:, cols] = (mm(grad_scores, keys) * scale).astype(BF)
         part_key = mm_tn(grad_scores, query)
         part_value = mm_tn(probs.astype(BF), grad_mixed)
-        if grad_key is None:
-            grad_key, grad_value = part_key, part_value
-        else:
-            grad_key, grad_value = grad_key + part_key, grad_value + part_value
-    gk_ref[...] = (grad_key * scale).astype(BF)
-    gv_ref[...] = grad_value.astype(BF)
-
-
-def attention_specs(total):
-    wide = pl.BlockSpec((total, GROUP * HEAD_SIZE), lambda h: (0, h))
-    narrow = pl.BlockSpec((total, HEAD_SIZE), lambda h: (0, h))
-    seg_col = pl.BlockSpec((total, 1), lambda h: (0, 0))
-    seg_row = pl.BlockSpec((1, total), lambda h: (0, 0))
-    lse = pl.BlockSpec((1, total, GROUP), lambda h: (h, 0, 0))
-    return wide, narrow, seg_col, seg_row, lse
-
-
-def attend_forward(queries, keys, values, segment):
-    total = queries.shape[0]
-    wide, narrow, seg_col, seg_row, lse = attention_specs(total)
+        grad_key = part_key if g == 0 else grad_key + part_key
+        grad_value = part_value if g == 0 else grad_value + part_value
+    gk_ref[:, here] = (grad_key * scale).astype(BF)
+    gv_ref[:, here] = grad_value.astype(BF)
+
+
+class DenseWeights:
+    def __init__(self, full, extents):
+        self.rows_n, self.cols_n, _, self.inner = full.shape
+        self.extents = extents
+        self.width = self.rows_n * self.inner
+        self.cut = self.inner % 128 == 0
+        self.operands = [full]
+        if not self.cut:
+            self.operands = []
+            at = 0
+            for extent in extents:
+                part = full[:, :, at : at + extent].transpose(1, 2, 0, 3)
+                self.operands.append(part.reshape(self.cols_n, extent, self.width))
+                at += extent
+        self.count = len(self.operands)
+        self.scratch = [
+            pltpu.VMEM((self.cols_n, extent, self.width), BF) for extent in extents
+        ] + [pltpu.SemaphoreType.DMA((len(extents), self.rows_n))]
+
+    def copies(self, sources, held, sems):
+        made = []
+        at = 0
+        for part, extent in enumerate(self.extents):
+            if self.cut:
+                made.append(
+                    [
+                        pltpu.make_async_copy(
+                            sources[0].at[r, :, pl.ds(at, extent), :],
+                            held[part].at[:, :, pl.ds(r * self.inner, self.inner)],
+                            sems.at[part, r],
+                        )
+                        for r in range(self.rows_n)
+                    ]
+                )
+            else:
+                made.append(
+                    [pltpu.make_async_copy(sources[part], held[part], sems.at[part, 0])]
+                )
+            at += extent
+        return made
+
+
+ROW_STEP = 64
+
+
+def flat(value):
+    return value.reshape(value.shape[0] * value.shape[1], value.shape[2])
+
+
+def route_columns(routes):
+    return lax.div(routes, EXP_DEV) * 16 + lax.rem(routes, EXP_DEV)
+
+
+def column_spans(width, count=KEY_VALUE_HEADS):
+    step = width // count
+    return [slice(at, at + step) for at in range(0, width, step)]
+
+
+def block_start(tokens, full, extents, gains, segment, routes):
+    total, width = tokens.shape
+    weights = DenseWeights(full, extents)
+    n = weights.count
+    per_group = weights.cols_n // KEY_VALUE_HEADS
+
+    def kernel(*refs):
+        sources = refs[:n]
+        (
+            tok_ref, gain_ref, segc_ref, segr_ref, routes_ref,
+            n1_ref, q_ref, k_ref, v_ref, mixed_ref, lse_ref, after_ref, n2_ref, s1_ref, s2_ref,
+            gates_ref, gates_t_ref, *held, sems,
+        ) = refs[n:]
+        copies = weights.copies(sources, held, sems)
+        for part in copies:
+            for copy in part:
+                copy.start()
+
+        @pl.loop(0, total // ROW_STEP)
+        def _(step):
+            rows = pl.ds(pl.multiple_of(step * ROW_STEP, ROW_STEP), ROW_STEP)
+            x = tok_ref[rows].astype(F32)
+            scale = rms_scale(x)
+            n1_ref[rows] = (x * scale * gain_ref[0:1]).astype(BF)
+            s1_ref[rows] = scale
+
+        for part in copies:
+            for copy in part:
+                copy.wait()
+        normed = n1_ref[...]
+        for h, cols in enumerate(column_spans(width)):
+            mine = slice(h * per_group, (h + 1) * per_group)
+            q_ref[:, cols] = mm_nt(normed, flat(held[0][mine])).astype(BF)
+        k_ref[...] = mm_nt(normed, flat(held[1][...])).astype(BF)
+        v_ref[...] = mm_nt(normed, flat(held[2][...])).astype(BF)
+        allowed = allowed_mask(segc_ref[...], segr_ref[...])
+
+        @pl.loop(0, KEY_VALUE_HEADS)
+        def _(h):
+            attend_forward_group(h, q_ref, k_ref, v_ref, allowed, mixed_ref, lse_ref)
+
+        mixed = mixed_ref[...]
+        for h, cols in enumerate(column_spans(width)):
+            mine = slice(h * per_group, (h + 1) * per_group)
+            after_ref[:, cols] = tok_ref[:, cols].astype(F32) + mm_nt(mixed, flat(held[3][mine]))
+
+        @pl.loop(0, total // ROW_STEP)
+        def _(step):
+            rows = pl.ds(pl.multiple_of(step * ROW_STEP, ROW_STEP), ROW_STEP)
+            after = after_ref[rows]
+            scale = rms_scale(after)
+            n2_ref[rows] = (after * scale * gain_ref[1:2]).astype(BF)
+            s2_ref[rows] = scale
+
+        logits = mm_nt(n2_ref[...], flat(held[4][...]))
+        lane = lax.broadcasted_iota(jnp.int32, logits.shape, 1)
+        goal = route_columns(routes_ref[...])
+        chosen = [
+            jnp.sum(jnp.where(lane == goal[:, i : i + 1], logits, 0.0), axis=1, keepdims=True)
+            for i in range(TOP)
+        ]
+        peak = functools.reduce(jnp.maximum, chosen)
+        raw = [jnp.exp(value - peak) for value in chosen]
+        whole = functools.reduce(jnp.add, raw)
+        lane = lax.broadcasted_iota(jnp.int32, (total, 128), 1)
+        wide = jnp.zeros((total, 128), F32)
+        for i in range(TOP):
+            wide = jnp.where(lane == i, raw[i] / whole, wide)
+        gates_ref[...] = wide[:, :8]
+        gates_t_ref[...] = wide.T[:8]
+
+    vmem = pl.BlockSpec(memory_space=pltpu.VMEM)
+    kv = KEY_VALUE_HEADS * HEAD_SIZE
+    shapes = [
+        ((total, width), BF), ((total, width), BF), ((total, kv), BF), ((total, kv), BF),
+        ((total, width), BF), ((KEY_VALUE_HEADS, total, GROUP), F32), ((total, width), F32),
+        ((total, width), BF), ((total, 1), F32), ((total, 1), F32), ((total, 8), F32),
+        ((8, total), F32),
+    ]
     return pl.pallas_call(
-        attend_forward_kernel,
-        grid=(KEY_VALUE_HEADS,),
-        in_specs=[wide, narrow, narrow, seg_col, seg_row],
-        out_specs=[wide, lse],
-        out_shape=[
-            jax.ShapeDtypeStruct(queries.shape, BF),
-            jax.ShapeDtypeStruct((KEY_VALUE_HEADS, total, GROUP), F32),
-        ],
-        compiler_params=pltpu.CompilerParams(vmem_limit_bytes=48 * 1024 * 1024),
-        name="attend_forward",
-    )(queries, keys, values, segment[:, None], segment[None, :])
-
-
-def attend_backward(queries, keys, values, grad_mixed, segment, log_totals):
-    total = queries.shape[0]
-    wide, narrow, seg_col, seg_row, lse = attention_specs(total)
+        kernel,
+        in_specs=[pl.BlockSpec(memory_space=pl.ANY)] * n + [vmem] * 5,
+        out_specs=[vmem] * len(shapes),
+        out_shape=[jax.ShapeDtypeStruct(shape, kind) for shape, kind in shapes],
+        scratch_shapes=weights.scratch,
+        compiler_params=pltpu.CompilerParams(vmem_limit_bytes=60 * 1024 * 1024),
+        cost_estimate=pl.CostEstimate(
+            flops=10_000_000_000, bytes_accessed=30_000_000, transcendentals=0
+        ),
+        name="block_start",
+    )(*weights.operands, tokens, gains, segment[:, None], segment[None, :], routes)
+
+
+def block_end(
+    tokens, cotangent, full, extents, gains, segment, routes, gates, ggw, sums,
+    queries, keys, values, log_totals, after, scale_one, scale_two,
+):
+    total, width = tokens.shape
+    weights = DenseWeights(full, extents)
+    n = weights.count
+    chips = weights.cols_n // 2
+    experts = ggw.shape[0]
+
+    def kernel(*refs):
+        sources = refs[:n]
+        (
+            tok_ref, dy_ref, gain_ref, segc_ref, segr_ref, routes_ref, gates_ref, ggw_ref,
+            own_ref, other_ref, below_ref, above_ref, q_ref, k_ref, v_ref, lse_ref, after_ref,
+            s1_ref, s2_ref,
+            gtok_ref, gq_ref, gk_ref, gv_ref, gab_ref, glog_ref, ggain_ref,
+            acc, grad_mixed, *held, sems,
+        ) = refs[n:]
+        copies = weights.copies(sources, held, sems)
+        for part in (4, 3, 0, 1, 2):
+            for copy in copies[part]:
+                copy.start()
+        chip = lax.div(lax.axis_index("col"), 2)
+        not_first, not_last = chip > 0, chip < chips - 1
+
+        per_expert = jnp.pad(ggw_ref[...], ((0, 128 - experts), (0, 0))).T
+        lane = lax.broadcasted_iota(jnp.int32, (total, 128), 1)
+        goals = routes_ref[...]
+        weight = [gates_ref[:, i : i + 1] for i in range(TOP)]
+        grads = [
+            jnp.sum(jnp.where(lane == goals[:, i : i + 1], per_expert, 0.0), axis=1, keepdims=True)
+            for i in range(TOP)
+        ]
+        mean = functools.reduce(jnp.add, [w * g for w, g in zip(weight, grads)])
+        goals = route_columns(goals)
+        lane = lax.broadcasted_iota(jnp.int32, glog_ref.shape, 1)
+        spread = jnp.zeros(glog_ref.shape, F32)
+        for i in range(TOP):
+            spread = jnp.where(lane == goals[:, i : i + 1], weight[i] * (grads[i] - mean), spread)
+        glog = spread.astype(BF)
+        glog_ref[...] = glog
+        for copy in copies[4]:
+            copy.wait()
+        for cols in column_spans(width):
+            acc[:, cols] = mm(glog, flat(held[4][:, :, cols]))
+        ggain_ref[...] = jnp.zeros_like(ggain_ref)
+
+        @pl.loop(0, total // ROW_STEP)
+        def _(step):
+            rows = pl.ds(pl.multiple_of(step * ROW_STEP, ROW_STEP), ROW_STEP)
+            grad = acc[rows] + own_ref[rows].astype(F32) + other_ref[rows].astype(F32)
+            grad = grad + jnp.where(not_first, below_ref[rows].astype(F32), 0.0)
+            grad = grad + jnp.where(not_last, above_ref[rows].astype(F32), 0.0)
+            scale = s2_ref[rows]
+            unit = after_ref[rows] * scale
+            back, gain = norm_back(grad, unit, scale, gain_ref[1:2])
+            ggain_ref[1:2] += gain[None]
+            value = dy_ref[rows].astype(F32) + back
+            acc[rows] = value
+            gab_ref[rows] = value.astype(BF)
+
+        for copy in copies[3]:
+            copy.wait()
+        rounded = gab_ref[...]
+        for cols in column_spans(width):
+            grad_mixed[:, cols] = mm(rounded, flat(held[3][:, :, cols])).astype(BF)
+        allowed = allowed_mask(segc_ref[...], segr_ref[...])
+
+        @pl.loop(0, KEY_VALUE_HEADS)
+        def _(h):
+            attend_backward_group(
+                h, q_ref, k_ref, v_ref, grad_mixed, allowed, lse_ref, gq_ref, gk_ref, gv_ref
+            )
+
+        for part in range(3):
+            for copy in copies[part]:
+                copy.wait()
+        for cols in column_spans(width):
+            gtok_ref[:, cols] = (
+                mm(gq_ref[...], flat(held[0][:, :, cols]))
+                + mm(gk_ref[...], flat(held[1][:, :, cols]))
+                + mm(gv_ref[...], flat(held[2][:, :, cols]))
+            )
+
+        @pl.loop(0, total // ROW_STEP)
+        def _(step):
+            rows = pl.ds(pl.multiple_of(step * ROW_STEP, ROW_STEP), ROW_STEP)
+            scale = s1_ref[rows]
+            unit = tok_ref[rows].astype(F32) * scale
+            back, gain = norm_back(gtok_ref[rows], unit, scale, gain_ref[0:1])
+            ggain_ref[0:1] += gain[None]
+            gtok_ref[rows] = acc[rows] + back
+
+    vmem = pl.BlockSpec(memory_space=pltpu.VMEM)
+    kv = KEY_VALUE_HEADS * HEAD_SIZE
+    shapes = [
+        ((total, width), F32), ((total, width), BF), ((total, kv), BF), ((total, kv), BF),
+        ((total, width), BF), ((total, weights.cols_n * 16), BF), ((2, width), F32),
+    ]
+    args = (
+        tokens, cotangent, gains, segment[:, None], segment[None, :], routes, gates, ggw, *sums,
+        queries, keys, values, log_totals, after, scale_one, scale_two,
+    )
     return pl.pallas_call(
-        attend_backward_kernel,
-        grid=(KEY_VALUE_HEADS,),
-        in_specs=[wide, narrow, narrow, wide, seg_col, seg_row, lse],
-        out_specs=[wide, narrow, narrow],
-        out_shape=[
-            jax.ShapeDtypeStruct(queries.shape, BF),
-            jax.ShapeDtypeStruct(keys.shape, BF),
-            jax.ShapeDtypeStruct(keys.shape, BF),
-        ],
-        compiler_params=pltpu.CompilerParams(vmem_limit_bytes=48 * 1024 * 1024),
-        name="attend_backward",
-    )(queries, keys, values, grad_mixed, segment[:, None], segment[None, :], log_totals)
+        kernel,
+        in_specs=[pl.BlockSpec(memory_space=pl.ANY)] * n + [vmem] * len(args),
+        out_specs=[vmem] * len(shapes),
+        out_shape=[jax.ShapeDtypeStruct(shape, kind) for shape, kind in shapes],
+        scratch_shapes=[pltpu.VMEM((total, width), F32), pltpu.VMEM((total, width), BF)]
+        + weights.scratch,
+        compiler_params=pltpu.CompilerParams(vmem_limit_bytes=60 * 1024 * 1024),
+        cost_estimate=pl.CostEstimate(
+            flops=20_000_000_000, bytes_accessed=40_000_000, transcendentals=0
+        ),
+        name="block_end",
+    )(*weights.operands, *args)
 
 
 def remote(src, dst, send_sem, recv_sem, device):
@@ -1206,77 +1430,40 @@
     )
 
 
-def expert_grads_kernel(units_n, place_of, *refs):
-    xs, dys, hid, gg, gu = (refs[i * units_n : (i + 1) * units_n] for i in range(5))
-    up, down, og_ref, ou_ref, od_ref, from_below, from_above, send_sems, recv_sems = refs[
-        5 * units_n :
-    ]
-    place = place_of()
-    moves = Moves(place, up, down, from_below, from_above, send_sems, recv_sems)
-
-    @pl.when(pl.program_id(0) == 0)
-    def _():
-        place.greet(False)
-        moves.start()
-
-    rows_n = og_ref.shape[0]
-    inner = og_ref.shape[2]
+def expert_grads_kernel(units_n, rows_n, cut_left, *refs):
+    left, right, out_ref = refs[:units_n], refs[units_n : 2 * units_n], refs[-1]
+    inner = (left if cut_left else right)[0].shape[2] // rows_n
 
     def joined(parts, cols=slice(None)):
         return jnp.concatenate([part[0, :, cols] for part in parts], axis=0)
 
-    all_gg, all_gu, all_hid = joined(gg), joined(gu), joined(hid)
+    other = joined(right if cut_left else left)
     for row in range(rows_n):
-        cols = slice(row * inner, (row + 1) * inner)
-        rows = joined(xs, cols)
-        og_ref[row, 0] = mm_tn(rows, all_gg).astype(BF)
-        ou_ref[row, 0] = mm_tn(rows, all_gu).astype(BF)
-        od_ref[row, 0] = mm_tn(all_hid, joined(dys, cols)).astype(BF)
-
-    @pl.when(pl.program_id(0) == EXP_DEV - 1)
-    def _():
-        moves.wait_send()
-        moves.wait_recv()
-
-
-def expert_grads(xs, dys, hid, gg, gu, rows_n, cols_n, moves, collective_id):
-    _, slots, width = xs[0].shape
-    ffn = hid[0].shape[2]
-    inner = width // rows_n
-    units_n = len(xs)
-
-    def each(cols):
-        return pl.BlockSpec((1, slots, cols), lambda e: (e, 0, 0))
-
+        cut = joined(left if cut_left else right, slice(row * inner, (row + 1) * inner))
+        pair = (cut, other) if cut_left else (other, cut)
+        out_ref[row, 0] = mm_tn(*pair).astype(BF)
+
+
+def expert_grads(left, right, rows_n, cut_left):
+    slots = left[0].shape[1]
+    units_n = len(left)
+    sizes = [left[0].shape[2], right[0].shape[2]]
+    specs = [
+        pl.BlockSpec((1, slots, size), lambda e: (e, 0, 0)) for size in sizes for _ in left
+    ]
+    sizes[0 if cut_left else 1] //= rows_n
     return pl.pallas_call(
-        functools.partial(expert_grads_kernel, units_n, lambda: Place(rows_n, cols_n)),
+        functools.partial(expert_grads_kernel, units_n, rows_n, cut_left),
         grid=(EXP_DEV,),
-        in_specs=[each(width)] * (2 * units_n)
-        + [each(ffn)] * (3 * units_n)
-        + [ANY] * 2,
-        out_specs=[
-            pl.BlockSpec((rows_n, 1, inner, ffn), lambda e: (0, e, 0, 0)),
-            pl.BlockSpec((rows_n, 1, inner, ffn), lambda e: (0, e, 0, 0)),
-            pl.BlockSpec((rows_n, 1, ffn, inner), lambda e: (0, e, 0, 0)),
-            ANY,
-            ANY,
-        ],
-        out_shape=[
-            jax.ShapeDtypeStruct((rows_n, EXP_DEV, inner, ffn), BF),
-            jax.ShapeDtypeStruct((rows_n, EXP_DEV, inner, ffn), BF),
-            jax.ShapeDtypeStruct((rows_n, EXP_DEV, ffn, inner), BF),
-            jax.ShapeDtypeStruct(moves[0].shape, moves[0].dtype),
-            jax.ShapeDtypeStruct(moves[1].shape, moves[1].dtype),
-        ],
-        scratch_shapes=[pltpu.SemaphoreType.DMA((2,)), pltpu.SemaphoreType.DMA((2,))],
-        compiler_params=pltpu.CompilerParams(
-            collective_id=collective_id, has_side_effects=True, vmem_limit_bytes=60 * 1024 * 1024
-        ),
+        in_specs=specs,
+        out_specs=pl.BlockSpec((rows_n, 1) + tuple(sizes), lambda e: (0, e, 0, 0)),
+        out_shape=jax.ShapeDtypeStruct((rows_n, EXP_DEV) + tuple(sizes), BF),
+        compiler_params=pltpu.CompilerParams(vmem_limit_bytes=60 * 1024 * 1024),
         cost_estimate=pl.CostEstimate(
-            flops=20_000_000_000, bytes_accessed=100_000_000, transcendentals=0
+            flops=7_000_000_000, bytes_accessed=30_000_000, transcendentals=0
         ),
         name="expert_grads",
-    )(*xs, *dys, *hid, *gg, *gu, *moves)
+    )(*left, *right)
 
 
 def on_device(
@@ -1328,19 +1515,11 @@
     sdown = jnp.swapaxes(sdown, 0, 1).reshape(units, width)
     sgu = sgu.reshape(width, 2 * units)
 
-    def piece(lo, extent):
-        part = full[:, :, lo : lo + extent]
-        return part.transpose(1, 2, 0, 3).reshape(cols_n * extent, width)
-
-    wq_t = piece(0, q_w)
-    wk_t = piece(q_w, k_w)
-    wv_t = piece(q_w + k_w, k_w)
-    wo_t = piece(q_w + 2 * k_w, q_w)
     t_at = 2 * q_w + 2 * k_w
-    router_t = piece(t_at, EXP_DEV)
+    extents = [q_w, k_w, k_w, q_w, 16]
     n_gain = g_attn.shape[0]
-    gain_attn = full[:, :, t_at + EXP_DEV, :n_gain].reshape(width).astype(F32)
-    gain_moe = full[:, :, t_at + EXP_DEV + 1, :n_gain].reshape(width).astype(F32)
+    gains = full[:, :, t_at + EXP_DEV : t_at + EXP_DEV + 2, :n_gain].transpose(2, 0, 1, 3)
+    gains = gains.reshape(2, width).astype(F32)
     egate = lax.all_gather(e_gate, "row", axis=1, tiled=True)
     eup = lax.all_gather(e_up, "row", axis=1, tiled=True)
     edown = lax.all_gather(e_down, "row", axis=2, tiled=True)
@@ -1349,27 +1528,11 @@
     places = jnp.arange(total, dtype=jnp.int32)
     segment = jnp.sum((places[:, None] >= seq_ends[None, :]).astype(jnp.int32), axis=1)
 
-    tokens_f = tokens.astype(F32)
-    scale_one = rms_scale(tokens_f)
-    unit_one = tokens_f * scale_one
-    normed_one = (unit_one * gain_attn).astype(BF)
-    queries = mm_nt(normed_one, wq_t).astype(BF)
-    keys = mm_nt(normed_one, wk_t).astype(BF)
-    values = mm_nt(normed_one, wv_t).astype(BF)
-    mixed, log_totals = attend_forward(queries, keys, values, segment)
-    after_attn = tokens_f + mm_nt(mixed, wo_t)
-    scale_two = rms_scale(after_attn)
-    unit_two = after_attn * scale_two
-    normed_two = (unit_two * gain_moe).astype(BF)
-    logits = mm_nt(normed_two, router_t)
-    route_picks = (
-        routes[:, :, None] == jnp.arange(experts, dtype=jnp.int32)[None, None, :]
-    ).astype(F32)
-    chosen = jnp.sum(route_picks * logits[:, None, :], axis=-1)
-    gate_raw = jnp.exp(chosen - jnp.max(chosen, axis=-1, keepdims=True))
-    gate_weights = gate_raw / jnp.sum(gate_raw, axis=-1, keepdims=True)
-
-    gates_t = jnp.pad(gate_weights.T, ((0, 8 - TOP), (0, 0)))
+    (
+        normed_one, queries, keys, values, mixed, log_totals, after_attn, normed_two, scale_one,
+        scale_two, gates, gates_t,
+    ) = block_start(tokens, full, extents, gains, segment, routes)
+
     x_all, gates_all = line_gather([normed_two, gates_t], 1, rows_n, cols_n)
     chips = cols_n // 2
     my_order = jnp.array(round_tables(chips)[0], jnp.int32)[col_here // 2]
@@ -1391,45 +1554,32 @@
         ggw = ggw + jnp.where(is_unit, ggw_part[None], 0.0)
         gx_sum.add(own[1], other[1])
         moe_sum.add(own[0], other[0])
-    gx = gx_sum.result()
-    grad_egate, grad_eup, grad_edown, below, above = expert_grads(
-        *zip(*saved), rows_n, cols_n, moe_sum.outgoing(0), 3
+    xs, dys, hid, gg, gu = zip(*saved)
+    grad_edown = expert_grads(hid, dys, rows_n, False)
+    grad_egate = expert_grads(xs, gg, rows_n, True)
+    grad_eup = expert_grads(xs, gu, rows_n, True)
+    ggw = ggw.reshape(cols_n, 8, total)[:, :EXP_DEV]
+
+    ggw_home = lax.all_to_all(ggw, "col", split_axis=0, concat_axis=0, tiled=True)
+    grad_tokens, gq, gk, gv, grad_attn_b, logits_left, gain_grads = block_end(
+        tokens, cotangent, full, extents, gains, segment, routes, gates,
+        ggw_home.reshape(experts, total),
+        (gx_sum.sums[-1][0], gx_sum.sums[-1][1], gx_sum.below, gx_sum.above),
+        queries, keys, values, log_totals, after_attn, scale_one, scale_two,
     )
-    moe_sum.arrived(below, above)
-    ggw = ggw.reshape(cols_n, 8, total)[:, :EXP_DEV]
-
-    ggw_home = lax.all_to_all(ggw, "col", split_axis=0, concat_axis=0, tiled=True)
-    ggw_home = ggw_home.reshape(experts, total).T
-
-    grad_gates = jnp.sum(route_picks * ggw_home[:, None, :], axis=-1)
-    grad_chosen = gate_weights * (
-        grad_gates - jnp.sum(gate_weights * grad_gates, axis=-1, keepdims=True)
-    )
-    grad_logits = jnp.sum(route_picks * grad_chosen[:, :, None], axis=1).astype(BF)
-    grad_normed_two = gx + mm(grad_logits, router_t)
-    grad_two, grad_gain_moe = norm_back(grad_normed_two, unit_two, scale_two, gain_moe)
-    grad_after = cotangent.astype(F32) + grad_two
-    grad_attn_b = grad_after.astype(BF)
-    grad_mixed = mm(grad_attn_b, wo_t).astype(BF)
-    gq, gk, gv = attend_backward(queries, keys, values, grad_mixed, segment, log_totals)
-    grad_normed_one = mm(gq, wq_t) + mm(gk, wk_t) + mm(gv, wv_t)
-    grad_one, grad_gain_attn = norm_back(grad_normed_one, unit_one, scale_one, gain_attn)
-    grad_tokens = grad_after + grad_one
-
-    rounds = [moe_sum.outgoing(1)] + [moe_sum.kept(turn) for turn in range(2, chips - 1)]
+
+    rounds = [moe_sum.outgoing(0)] + [moe_sum.kept(turn) for turn in range(1, chips - 1)]
 
     def gain_rows(grad):
         part = grad.reshape(rows_n, cols_n, 1, n_gain)
         return jnp.pad(part, ((0, 0),) * 3 + ((0, inner - n_gain),))
 
-    tails = jnp.concatenate([gain_rows(grad_gain_attn), gain_rows(grad_gain_moe)], axis=2)
+    tails = jnp.concatenate([gain_rows(gain_grads[0]), gain_rows(gain_grads[1])], axis=2)
     tails = jnp.pad(tails, ((0, 0), (0, 0), (EXP_DEV, 16 - EXP_DEV - 2), (0, 0)))
     tails = tails.reshape(rows_n, cols_n * 16, inner)
-    logits_left = grad_logits.reshape(total, cols_n, EXP_DEV)
-    logits_left = jnp.pad(logits_left, ((0, 0), (0, 0), (0, 16 - EXP_DEV)))
     grads_sh = grad_sh.astype(BF).reshape(rows_n, inner, 3 * units)
     dense, dense_sh, sd_parts, arrivals = dense_sum(
-        [gq, gk, gv, grad_attn_b, logits_left.reshape(total, cols_n * 16)],
+        [gq, gk, gv, grad_attn_b, logits_left],
         [normed_one, normed_one, normed_one, mixed, normed_two],
         tails, grads_sh, rounds, 2, rows_n, cols_n,
     )

time: 932 us -> 858 us (0.921)
  Pallas kernels: 649 us -> 717 us
  waiting for transfers between devices: 58 us -> 2.17 us
  matrix products: 32.3 us -> 0 us
  local copies, waits for them, and re-layouts: 67.1 us -> 34.9 us
  other arithmetic: 82.8 us -> 64 us
    unnamed x9, waiting for transfers between devices: 57.9 us -> 2.11 us
    pallas_call x3 -> x5, Pallas kernels: 63.8 us -> 103 us  [the longest x1 39 us: block_end(): pl.pallas_call(kernel, in_specs=[pl.BlockSpec(memory_space=pl.ANY)] * n +...]
    dot_general x10 -> x0, matrix products: 32.3 us -> none  [the longest x5 19.3 us: mm(): return jnp.dot(left, right, preferred_element_type=F32)]
    pallas_call x1, Pallas kernels: 152 us -> 179 us  [dense_sum(): pl.pallas_call(kernel, in_specs=[vmem] * (2 * n + 1) + [ANY] * (1 + 2 * n...]
    transpose x8 -> x0, local copies, waits for them, and re-layouts: 23 us -> none  [piece(): return part.transpose(1, 2, 0, 3).reshape(cols_n * extent, width)]
    convert_element_type x8 -> x6, other arithmetic: 42.1 us -> 22.8 us  [outgoing(): return (ups.astype(BF), downs.astype(BF))]
    unnamed x178 -> x72, local copies, waits for them, and re-layouts: 22.4 us -> 7.03 us
  transfers between devices with their start and end apart: 7 -> 7, of which waited for: 1 -> 0; matrix products, arithmetic and copies ran while one was open for 15% -> 9% of each run, Pallas kernels for 48% -> 64%
where the time goes in v4:
time: 858 us; the launch traced here: 848 us
  Pallas kernels  717 us (84%)
  other arithmetic  64 us (7%)
  local copies, waits for them, and re-layouts  34.9 us (4%)
  between operations  26.7 us (3%)
    pallas_call x1, Pallas kernels, dense_sum(): pl.pallas_call(kernel, in_specs=[vmem] * (2 * n + 1) + [ANY] * (1 + 2 * n...  179 us
    pallas_call x4, Pallas kernels, routed(): pl.pallas_call(functools.partial(routed_kernel, call, rows_n, cols_n, len...  164 us
    pallas_call x1, Pallas kernels, first_gather(): pl.pallas_call(kernel, in_specs=[ANY] * 5, out_specs=[ANY] * 5, out_shape...  156 us
    pallas_call x1, Pallas kernels, line_gather(): pl.pallas_call(kernel, in_specs=[ANY] * n, out_specs=[ANY] * n, out_shape...  115 us
    pallas_call x1, Pallas kernels, block_end(): pl.pallas_call(kernel, in_specs=[pl.BlockSpec(memory_space=pl.ANY)] * n +...  39 us
    pallas_call x3, Pallas kernels, expert_grads(): pl.pallas_call(functools.partial(expert_grads_kernel, units_n, rows_n, cu...  36.9 us
    pallas_call x1, Pallas kernels, block_start(): pl.pallas_call(kernel, in_specs=[pl.BlockSpec(memory_space=pl.ANY)] * n +...  27.3 us
    convert_element_type x6, other arithmetic, outgoing(): return (ups.astype(BF), downs.astype(BF))  22.8 us
  transfers between devices with their start and end apart: 7, of which 0 were waited for; matrix products, arithmetic and copies ran while one was open for 9% of the time, Pallas kernels for 64%

profile of v4, /device:TPU:2, one launch (start us, length us, event | category | flops | bytes accessed | tf_op | source)
XLA Modules:
  0.0 847.9 jit_solution(4118476755278261097)
XLA Ops:
  7.4 0.7 all-gather.4.cloned.1.call-update
  8.1 0.7 all-gather.6.cloned.1.call-update
  8.9 0.7 all-gather.8.cloned.1.call-update
  9.6 0.7 constant_dynamic-slice_fusion.1
  12.2 0.7 fusion.31
  15.1 0.9 copy.78.refs_3_.refs_4_
  16.0 0.8 copy.76
  16.7 0.9 copy.79.refs_5_.refs_6_
  18.4 0.7 pad_maximum_fusion.sh_ref
  19.2 156.2 %first_gather.1 = (bf16[4,8,528,384]{3,2,1,0:T(8,128)(2,1)}, bf16[8,512,1536]{2,1,0:T(8,128)(2,1)}, s32[8,8,512]{2,1,0:T(8,128)}, bf16[4,384,256]{2,1,0:T(8,128)(2,1)}, bf16[8,128,192]{2,1,0:T(8,128)(2,1)}) custom-call(bf16[528,384]{1,0:T(8,128)(2,1)} %copy-done.15, bf16[512,1536]{1,0:T(8,128)(2,1)} %refs_2_.1, s32[8,512]{1,0:T(8,128)} %pad.26.rt_ref, ...), custom_call_target="tpu_custom_call" | custom-call | tf_op jit(solution)/shard_map/first_gather/pallas_call | solution.py:733
  175.5 0.9 convert_bitcast_fusion
  176.3 0.7 reshape.295.refs_2_.refs_3_
  177.0 2.8 copy.80
  179.9 1.3 copy.81
  181.2 0.9 copy.85.refs_9_
  183.4 27.3 %block_start.1 = (bf16[512,1536]{1,0:T(8,128)(2,1)}, bf16[512,1536]{1,0:T(8,128)(2,1)}, bf16[512,512]{1,0:T(8,128)(2,1)}, bf16[512,512]{1,0:T(8,128)(2,1)}, bf16...) custom-call(bf16[4,8,528,384]{3,2,1,0:T(8,128)(2,1)} %get-tuple-elem, ...), custom_call_target="tpu_custom_call" | custom-call | flops 10000000000 | bytes 30000000 | tf_op jit(solution)/shard_map/block_start/pallas_call | solution.py:243
  210.7 114.6 %line_gather.1 = (bf16[8,512,1536]{2,1,0:T(8,128)(2,1)}, f32[8,8,512]{2,1,0:T(8,128)}) custom-call(bf16[512,1536]{1,0:T(8,128)(2,1)} %get-tuple-element.89.refs_0_.refs_9_, f32[8,512]{1,0:T(8,128)} %get-tuple-element.90.refs_1_), custom_call_target="tpu_custom_call" | custom-call | tf_op jit(solution)/shard_map/line_gather/pallas_call | solution.py:599
  325.4 38.1 %routed.4 = (bf16[2,512,1536]{2,1,0:T(8,128)(2,1)}, bf16[2,512,1536]{2,1,0:T(8,128)(2,1)}, bf16[4,256,1536]{2,1,0:T(8,128)(2,1)}, bf16[4,256,1536]{2,1,0:T(8,128...) custom-call(bf16[8,512,1536]{2,1,0:T(8,128)(2,1)} %get-tuple-element, ...), custom_call_target="tpu_custom_call" | custom-call | flops 24000000000 | bytes 100000000 | tf_op jit(solution)/shard_map/routed/pallas_call | solution.py:1373
  363.5 3.4 fusion.13.refs_10_.refs_11_
  366.9 42.5 %routed.5 = (bf16[2,512,1536]{2,1,0:T(8,128)(2,1)}, bf16[2,512,1536]{2,1,0:T(8,128)(2,1)}, bf16[4,256,1536]{2,1,0:T(8,128)(2,1)}, bf16[4,256,1536]{2,1,0:T(8,128...) custom-call(bf16[8,512,1536]{2,1,0:T(8,128)(2,1)} %get-tuple-element, ...), custom_call_target="tpu_custom_call" | custom-call | flops 24000000000 | bytes 100000000 | tf_op jit(solution)/shard_map/routed/pallas_call | solution.py:1373
  409.4 5.2 fusion.10
  414.6 41.3 %routed.6 = (bf16[2,512,1536]{2,1,0:T(8,128)(2,1)}, bf16[2,512,1536]{2,1,0:T(8,128)(2,1)}, bf16[4,256,1536]{2,1,0:T(8,128)(2,1)}, bf16[4,256,1536]{2,1,0:T(8,128...) custom-call(bf16[8,512,1536]{2,1,0:T(8,128)(2,1)} %get-tuple-element, ...), custom_call_target="tpu_custom_call" | custom-call | flops 24000000000 | bytes 100000000 | tf_op jit(solution)/shard_map/routed/pallas_call | solution.py:1373
  455.9 5.5 fusion.8.refs_11_
  462.1 0.9 copy-done.7
  463.0 0.9 copy-done.9
  463.9 3.7 fusion.9.refs_10_
  467.6 42.0 %routed.7 = (bf16[2,512,1536]{2,1,0:T(8,128)(2,1)}, bf16[2,512,1536]{2,1,0:T(8,128)(2,1)}, bf16[4,256,1536]{2,1,0:T(8,128)(2,1)}, bf16[4,256,1536]{2,1,0:T(8,128...) custom-call(bf16[8,512,1536]{2,1,0:T(8,128)(2,1)} %get-tuple-element, ...), custom_call_target="tpu_custom_call" | custom-call | flops 24000000000 | bytes 100000000 | tf_op jit(solution)/shard_map/routed/pallas_call | solution.py:1373
  509.6 13.3 %expert_grads.5 = bf16[4,4,512,384]{3,2,1,0:T(8,128)(2,1)} custom-call(bf16[4,256,512]{2,1,0:T(8,128)(2,1)} %get-tuple-element.149.refs_0_, bf16[4,256,512]{2,1,0:T(8,128)(2,1)} %get-tuple-element.150.refs_1_, bf16[4,256,512]{2,1,0:T(8,128)(2,1)} %get-tuple-element.151.refs_2_, bf16[4,256,512]{2,1,0:T(8,128)(2,1)} %get-tuple-element.152.refs_3_, ...), custom_call_target="tpu_custom_call" | custom-call | flops 7000000000 | bytes 30000000 | tf_op jit(solution)/shard_map/expert_grads/pallas_call | solution.py:1455
  523.1 11.7 %expert_grads.4 = bf16[4,4,384,512]{3,2,1,0:T(8,128)(2,1)} custom-call(bf16[4,256,1536]{2,1,0:T(8,128)(2,1)} %get-tuple-element.137.refs_0_, bf16[4,256,1536]{2,1,0:T(8,128)(2,1)} %get-tuple-element.138.refs_1_, bf16[4,256,1536]{2,1,0:T(8,128)(2,1)} %get-tuple-element.139.refs_2_, bf16[4,256,1536]{2,1,0:T(8,128)(2,1)} %get-tuple-element.140.refs_3_, ...), custom_call_target="tpu_custom_call" | custom-call | flops 7000000000 | bytes 30000000 | tf_op jit(solution)/shard_map/expert_grads/pallas_call | solution.py:1455
  542.5 0.7 constant_dynamic-slice_fusion
  543.8 0.6 iota_compare_fusion.6
  544.6 0.7 iota_compare_fusion.5
  545.5 0.7 iota_compare_fusion.4
  546.3 0.7 iota_compare_fusion.3
  547.2 0.7 fusion.15
  548.0 3.4 all-to-all-start
  551.4 2.8 slice_bitcast_fusion.refs_10_
  554.1 11.9 %expert_grads.3 = bf16[4,4,384,512]{3,2,1,0:T(8,128)(2,1)} custom-call(bf16[4,256,1536]{2,1,0:T(8,128)(2,1)} %get-tuple-element.137.refs_0_, bf16[4,256,1536]{2,1,0:T(8,128)(2,1)} %get-tuple-element.138.refs_1_, bf16[4,256,1536]{2,1,0:T(8,128)(2,1)} %get-tuple-element.139.refs_2_, bf16[4,256,1536]{2,1,0:T(8,128)(2,1)} %get-tuple-element.140.refs_3_, ...), custom_call_target="tpu_custom_call" | custom-call | flops 7000000000 | bytes 30000000 | tf_op jit(solution)/shard_map/expert_grads/pallas_call | solution.py:1455
  566.0 6.4 fusion.2.refs_17_
  572.4 6.1 add_convert_fusion
  578.6 0.7 copy-done.4
  579.3 1.0 copy-done.6
  580.3 1.0 copy-done.8
  581.3 2.5 fusion.3.refs_16_
  583.8 2.5 fusion.4.refs_15_
  586.3 2.5 fusion.5.refs_14_
  588.8 2.5 fusion.6.refs_13_
  591.2 2.5 fusion.7.refs_12_
  593.7 1.2 slice_bitcast_fusion.1.refs_9_
  595.0 0.7 reshape.291.refs_8_
  595.6 39.0 %block_end.1 = (f32[512,1536]{1,0:T(8,128)}, bf16[512,1536]{1,0:T(8,128)(2,1)}, bf16[512,512]{1,0:T(8,128)(2,1)}, bf16[512,512]{1,0:T(8,128)(2,1)}, bf16[512,153...) custom-call(bf16[4,8,528,384]{3,2,1,0:T(8,128)(2,1)} %get-tuple-element.87.refs_0_, ...), custom_call_target="tpu_custom_call" | custom-call | flops 20000000000 | bytes 40000000 | tf_op jit(solution)/shard_map/block_end/pallas_call | solution.py:361
  634.6 0.8 slice_reduce_fusion.1
  635.7 1.0 pad.29
  636.6 178.7 %dense_sum.1 = (f32[528,384]{1,0:T(8,128)}, f32[384,256]{1,0:T(8,128)}, f32[2,192,128]{2,1,0:T(8,128)}, bf16[3,2,512,1536]{3,2,1,0:T(8,128)(2,1)}) custom-call(bf16[512,1536]{1,0:T(8,128)(2,1)} %get-tuple-element.122.refs_0_, bf16[512,512]{1,0:T(8,128)(2,1)} %get-tuple-element.123.refs_1_, bf16[512,512]{1,0:T(8,128)(2,1)} %get-tuple-element.124.refs_2_, ...), custom_call_target="tpu_custom_call" | custom-call | flops 6442450944 | bytes 350000000 | tf_op jit(solution)/shard_map/dense_sum/pallas_call | solution.py:1077
  815.3 1.3 slice_bitcast_fusion.7
  816.6 1.3 slice_bitcast_fusion.6
  817.9 1.6 slice_bitcast_fusion.4
  819.5 1.6 copy_bitcast_fusion
  821.1 1.8 fusion.29
  822.9 1.9 slice_bitcast_fusion.2
  824.8 5.6 fusion.1
  830.4 3.3 bitcast_convert_fusion
  833.7 3.5 bitcast_convert_fusion.1
  837.2 3.5 bitcast_convert_fusion.2
  (106 shorter events, 4.9 us)
Async XLA Ops:
  7.2 7.0 copy-start
  7.2 7.0 copy-start.32
  7.2 8.8 %copy-start.18 = (bf16[256,192]{0,1:T(8,128)(2,1)S(1)}, bf16[256,192]{0,1:T(8,128)(2,1)}, u32[]{:S(2)}) copy-start(bf16[256,192]{0,1:T(8,128)(2,1)} %param.36) | copy-start | bytes 294916
  7.2 9.5 %copy-start.21 = (s32[512,6]{0,1:T(8,128)S(1)}, s32[512,6]{0,1:T(8,128)}, u32[]{:S(2)}) copy-start(s32[512,6]{0,1:T(8,128)} %param.37) | copy-start | bytes 36868
  7.2 11.0 %copy-start.31 = (bf16[48]{0:T(256)(128)(2,1)S(1)}, bf16[48]{0:T(256)(128)(2,1)}, u32[]{:S(2)}) copy-start(bf16[48]{0:T(256)(128)(2,1)} %param.24) | copy-start | bytes 292
  7.2 11.0 %copy-start.30 = (bf16[48]{0:T(256)(128)(2,1)S(1)}, bf16[48]{0:T(256)(128)(2,1)}, u32[]{:S(2)}) copy-start(bf16[48]{0:T(256)(128)(2,1)} %param.29) | copy-start | bytes 292
  7.3 11.0 %copy-start.16 = (bf16[384,192]{0,1:T(8,128)(2,1)S(1)}, bf16[384,192]{0,1:T(8,128)(2,1)}, u32[]{:S(2)}) copy-start(bf16[384,192]{0,1:T(8,128)(2,1)} %param.25) | copy-start | bytes 442372
  7.3 11.0 %copy-start.22 = (bf16[384,64]{0,1:T(8,128)(2,1)S(1)}, bf16[384,64]{0,1:T(8,128)(2,1)}, u32[]{:S(2)}) copy-start(bf16[384,64]{0,1:T(8,128)(2,1)} %param.26) | copy-start | bytes 147460
  7.3 11.0 %copy-start.23 = (bf16[384,64]{0,1:T(8,128)(2,1)S(1)}, bf16[384,64]{0,1:T(8,128)(2,1)}, u32[]{:S(2)}) copy-start(bf16[384,64]{0,1:T(8,128)(2,1)} %param.27) | copy-start | bytes 147460
  7.3 11.0 %copy-start.17 = (bf16[384,192]{0,1:T(8,128)(2,1)S(1)}, bf16[384,192]{0,1:T(8,128)(2,1)}, u32[]{:S(2)}) copy-start(bf16[384,192]{0,1:T(8,128)(2,1)} %param.28) | copy-start | bytes 442372
  7.3 11.1 %copy-start.29 = (bf16[384,4]{0,1:T(4,128)(2,1)S(1)}, bf16[384,4]{0,1:T(4,128)(2,1)}, u32[]{:S(2)}) copy-start(bf16[384,4]{0,1:T(4,128)(2,1)} %param.30) | copy-start | bytes 9220
  7.3 11.1 %copy-start.20 = (bf16[384,128]{1,0:T(8,128)(2,1)S(1)}, bf16[384,128]{1,0:T(8,128)(2,1)}, u32[]{:S(2)}) copy-start(bf16[384,128]{1,0:T(8,128)(2,1)} %param.34) | copy-start | bytes 294916
  7.3 11.1 %copy-start.19 = (bf16[384,128]{1,0:T(8,128)(2,1)S(1)}, bf16[384,128]{1,0:T(8,128)(2,1)}, u32[]{:S(2)}) copy-start(bf16[384,128]{1,0:T(8,128)(2,1)} %param.35) | copy-start | bytes 294916
  7.3 318.0 %all-gather.4.cloned.1.call-start = ((), (), s32[]{:S(2)}) async-start(), calls=%async_computation.4 | async-start | bytes 7864320 | tf_op jit(solution)/shard_map/all_gather | solution.py:1523
  8.1 317.3 %all-gather.6.cloned.1.call-start = ((), (), s32[]{:S(2)}) async-start(), calls=%async_computation.5 | async-start | bytes 7864320 | tf_op jit(solution)/shard_map/all_gather | solution.py:1524
  8.8 316.6 %all-gather.8.cloned.1.call-start = ((), (), s32[]{:S(2)}) async-start(), calls=%async_computation.6 | async-start | bytes 7864320 | tf_op jit(solution)/shard_map/all_gather | solution.py:1525
  9.5 820.8 %reduce-scatter.14.cloned.1.call-start = ((), (), s32[]{:S(2)}) async-start(), calls=%async_computation.9 | async-start | bytes 7864320
  15.1 164.8 %copy-start.28 = (s32[512]{0:T(512)}, s32[512]{0:T(512)S(1)}, u32[]{:S(2)}) copy-start(s32[512]{0:T(512)S(1)} %convert_reduce_fusion) | copy-start | bytes 6148
  18.4 0.8 copy-start.15
  366.9 42.5 %copy-start.2 = (bf16[2,512,1536]{2,1,0:T(8,128)(2,1)S(1)}, bf16[2,512,1536]{2,1,0:T(8,128)(2,1)}, u32[]{:S(2)}) copy-start(bf16[2,512,1536]{2,1,0:T(8,128)(2,1)} %get-tuple-element.97) | copy-start | bytes 9437188
  455.9 5.5 copy-start.3
  455.9 6.2 copy-start.5
  455.9 7.1 copy-start.7
  455.9 8.0 copy-start.9
  523.0 310.7 %reduce-scatter.12.cloned.1.call-start = ((), (), s32[]{:S(2)}) async-start(), calls=%async_computation.8 | async-start | bytes 7864320
  534.8 12.3 %copy-start.27 = (f32[2,8,512]{2,1,0:T(8,128)S(1)}, f32[2,8,512]{2,1,0:T(8,128)}, u32[]{:S(2)}) copy-start(f32[2,8,512]{2,1,0:T(8,128)} %get-tuple-element.113) | copy-start | bytes 98308
  534.8 12.3 %copy-start.26 = (f32[2,8,512]{2,1,0:T(8,128)S(1)}, f32[2,8,512]{2,1,0:T(8,128)}, u32[]{:S(2)}) copy-start(f32[2,8,512]{2,1,0:T(8,128)} %get-tuple-element.112) | copy-start | bytes 98308
  534.8 12.4 %copy-start.25 = (f32[2,8,512]{2,1,0:T(8,128)S(1)}, f32[2,8,512]{2,1,0:T(8,128)}, u32[]{:S(2)}) copy-start(f32[2,8,512]{2,1,0:T(8,128)} %get-tuple-element.111) | copy-start | bytes 98308
  534.8 12.4 %copy-start.24 = (f32[2,8,512]{2,1,0:T(8,128)S(1)}, f32[2,8,512]{2,1,0:T(8,128)}, u32[]{:S(2)}) copy-start(f32[2,8,512]{2,1,0:T(8,128)} %get-tuple-element.110) | copy-start | bytes 98308
  548.0 47.0 %all-to-all-start = ((f32[8,4,512]{2,1,0:T(4,128)}), f32[8,4,512]{2,1,0:T(4,128)S(1)}, u32[]{:S(2)}, u32[]{:S(2)}) async-start(f32[8,4,512]{2,1,0:T(4,128)} %fusion.15), calls=%async_computation | async-start | bytes 131072 | tf_op jit(solution)/shard_map/all_to_all | solution.py:1563
  551.3 285.9 %reduce-scatter.10.cloned.1.call-start = ((), (), s32[]{:S(2)}) async-start(), calls=%async_computation.7 | async-start | bytes 7864320
  566.0 12.6 %copy-start.10 = (bf16[2,512,1536]{2,1,0:T(8,128)(2,1)S(1)}, bf16[2,512,1536]{2,1,0:T(8,128)(2,1)}, u32[]{:S(2)}) copy-start(bf16[2,512,1536]{2,1,0:T(8,128)(2,1)} %get-tuple-element.103) | copy-start | bytes 9437188
  566.0 12.6 %copy-start.11 = (bf16[2,512,1536]{2,1,0:T(8,128)(2,1)S(1)}, bf16[2,512,1536]{2,1,0:T(8,128)(2,1)}, u32[]{:S(2)}) copy-start(bf16[2,512,1536]{2,1,0:T(8,128)(2,1)} %get-tuple-element.104) | copy-start | bytes 9437188
  566.0 12.6 %copy-start.12 = (bf16[2,512,1536]{2,1,0:T(8,128)(2,1)S(1)}, bf16[2,512,1536]{2,1,0:T(8,128)(2,1)}, u32[]{:S(2)}) copy-start(bf16[2,512,1536]{2,1,0:T(8,128)(2,1)} %get-tuple-element.107) | copy-start | bytes 9437188
  566.0 12.6 %copy-start.14 = (bf16[2,512,1536]{2,1,0:T(8,128)(2,1)S(1)}, bf16[2,512,1536]{2,1,0:T(8,128)(2,1)}, u32[]{:S(2)}) copy-start(bf16[2,512,1536]{2,1,0:T(8,128)(2,1)} %get-tuple-element.108) | copy-start | bytes 9437188
  572.4 6.9 copy-start.4
  572.4 7.9 copy-start.6
  572.4 8.9 %copy-start.8 = (bf16[2,512,1536]{2,1,0:T(8,128)(2,1)S(1)}, bf16[2,512,1536]{2,1,0:T(8,128)(2,1)}, u32[]{:S(2)}) copy-start(bf16[2,512,1536]{2,1,0:T(8,128)(2,1)} %get-tuple-element.100) | copy-start | bytes 9437188
  636.6 188.2 %copy-start.13 = (bf16[2,512,1536]{2,1,0:T(8,128)(2,1)S(1)}, bf16[2,512,1536]{2,1,0:T(8,128)(2,1)}, u32[]{:S(2)}) copy-start(bf16[2,512,1536]{2,1,0:T(8,128)(2,1)} %get-tuple-element.107) | copy-start | bytes 9437188
  833.7 7.0 copy-start.1
Sparse Core Ops, SparseCore 0:
  10.0 150.9 all-gather.3
  162.8 72.1 all-gather.5
  236.8 69.9 all-gather.7
  523.1 86.7 reduce-scatter.13
  612.7 127.4 reduce-scatter.11
  743.1 90.0 reduce-scatter.9

commit v5 on v4

--- a/solution.py
+++ b/solution.py
@@ -397,7 +397,12 @@
     def peer_row(self, step):
         return lax.rem(self.row + step, self.rows_n)
 
-    def greet(self, with_rows, per_row=0, downs_back=0):
+    def square(self):
+        across = self.row + 1 - 2 * lax.rem(self.row, 2)
+        along = lax.rem(self.row + 2, 4)
+        return across, along, along + 1 - 2 * lax.rem(along, 2)
+
+    def greet(self, with_rows, downs_back=0):
         barrier = pltpu.get_barrier_semaphore()
 
         def hello(row, col):
@@ -424,15 +429,6 @@
             for step in range(1, self.rows_n):
                 hello(self.peer_row(step), self.col)
             count = count + (self.rows_n - 1)
-        if per_row:
-            source = lax.div(self.col, per_row)
-            for col in range(2 * self.chips):
-
-                @pl.when(jnp.logical_not((source == self.row) & (self.col == col)))
-                def _():
-                    hello(source, jnp.int32(col))
-
-            count = count + self.rows_n * per_row - (source == self.row).astype(jnp.int32)
         if downs_back:
             goal = lax.div(self.col, downs_back)
             for turn in range(downs_back):
@@ -480,6 +476,82 @@
             @pl.when(self.ends[1 - which])
             def _():
                 self.copies[which].wait_recv()
+
+
+class RoundStart:
+    def __init__(self, place, call_refs, held, came, held_sems, came_sems):
+        self.place, self.call_refs = place, call_refs
+        self.held, self.came = held, came
+        self.held_sems, self.came_sems = held_sems, came_sems
+        self.tables = round_tables(place.chips)[1:]
+
+    def bring(self, which, call):
+        own, other = self.call_refs[2 * call], self.call_refs[2 * call + 1]
+        return (
+            pltpu.make_async_copy(own.at[1], self.held.at[which], self.held_sems.at[which]),
+            pltpu.make_async_copy(other.at[1], self.came.at[which], self.came_sems.at[which]),
+        )
+
+    def add_came(self, which):
+        part = self.came.shape[1] // 4
+        for at in range(0, self.came.shape[1], part):
+            span = slice(at, at + part)
+            self.held[which, span] = (
+                self.held[which, span].astype(F32) + self.came[which, span].astype(F32)
+            ).astype(BF)
+
+    def prepare(self, turn):
+        for which in range(2):
+            call = jnp.int32(0)
+            for chip in range(self.place.chips):
+                number = self.tables[which][chip][turn]
+                call = call + jnp.where(self.place.chip == chip, number, 0)
+            for i in range(turn + 1):
+
+                @pl.when(call == i)
+                def _():
+                    for copy in self.bring(which, i):
+                        copy.start()
+
+        for which in range(2):
+            for copy in self.bring(which, 0):
+                copy.wait()
+            self.add_came(which)
+
+    def add(self, before):
+        comes = (self.place.chip > 0, self.place.chip < self.place.chips - 1)
+
+        def copy(which):
+            return pltpu.make_async_copy(
+                before[which], self.came.at[which], self.came_sems.at[which]
+            )
+
+        for which in range(2):
+
+            @pl.when(comes[which])
+            def _():
+                copy(which).start()
+
+        for which in range(2):
+
+            @pl.when(comes[which])
+            def _():
+                copy(which).wait()
+                self.add_came(which)
+
+    def moves(self, after, send_sems, recv_sems):
+        return Moves(
+            self.place, self.held.at[0], self.held.at[1], *after, send_sems, recv_sems
+        )
+
+    @staticmethod
+    def scratch(block):
+        return [
+            pltpu.VMEM((2,) + block, BF),
+            pltpu.VMEM((2,) + block, BF),
+            pltpu.SemaphoreType.DMA((2,)),
+            pltpu.SemaphoreType.DMA((2,)),
+        ]
 
 
 class LineGather:
@@ -607,40 +679,87 @@
     )(*arrays)
 
 
-def first_gather(bundle, cotangent, routes_t, shared, downs, collective_id, rows_n, cols_n):
+def first_gather(
+    bundle, cotangent, routes_t, shared, downs, expert, later, collective_id, rows_n, cols_n
+):
     per_row = downs.shape[0]
-
-    def kernel(
-        bundle_ref, dy_ref, rt_ref, sh_ref, sd_ref,
-        full_ref, dy_all, rt_all, sh_all, sd_all, *sems
-    ):
+    square = rows_n == 4
+    n_goals = 2 if square else rows_n - 1
+    n_later = len(later)
+    inner = expert.shape[1]
+    half_experts = expert.shape[0] // 2
+
+    def kernel(*refs):
+        bundle_ref, dy_ref, rt_ref, sh_ref, sd_ref, ex_ref = refs[:6]
+        refs = refs[6 + n_later :]
+        full_ref, dy_all, rt_all, sh_all, sd_all, ex_all = refs[:6]
+        down_line, *sems = refs[6 + n_later :]
         place = Place(rows_n, cols_n)
         b_sems, sems = sems[:4], sems[4:]
         d_sems, sems = sems[:4], sems[4:]
         r_sems, sems = sems[:4], sems[4:]
-        row_send, row_core, row_recv, sh_send, sh_recv, sh_local, sd_send, sd_recv = sems
-        place.greet(True, per_row)
+        l_sems, sems = sems[:4], sems[4:]
+        (
+            row_send, row_core, row_recv, sh_send, sh_recv, sh_local, sd_send, sd_recv,
+            sd_local, ex_send, ex_recv, ex_local,
+        ) = sems
+        place.greet(True)
         row, col = place.row, place.col
+        across = along = corner = None
+        goals = [place.peer_row(step) for step in range(1, rows_n)]
+        sources = goals
+        if square:
+            across, along, corner = place.square()
+            goals, sources = [across, along], [across, along, corner]
         weights = LineGather(place, bundle_ref, full_ref.at[row], *b_sems)
         grads = LineGather(place, dy_ref, dy_all, *d_sems)
         picks = LineGather(place, rt_ref, rt_all, *r_sems)
 
-        def to_row(block, step, src=None):
+        def to_row(block, n, src=None):
             home = full_ref.at[row, block]
             return remote(
-                home if src is None else src, home, row_send.at[block, step],
-                row_recv.at[row, block], (place.peer_row(step), col),
+                home if src is None else src, home, row_send.at[block, n],
+                row_recv.at[row, block], (goals[n], col),
             )
 
         def push(block, src=None):
-            for step in range(1, rows_n):
-                to_row(block, step, src).start()
-
-        def from_row(other_row, block):
-            home = full_ref.at[other_row, block]
+            for n in range(n_goals):
+                to_row(block, n, src).start()
+
+        def from_row(source, block):
+            home = full_ref.at[source, block]
             return remote(
-                home, home, row_core.at[other_row, block], row_recv.at[other_row, block],
+                home, home, row_core.at[source, block], row_recv.at[source, block],
                 (row, place.other),
+            )
+
+        def onward(source, block, goal):
+            home = full_ref.at[source, block]
+            return remote(
+                home, home, row_send.at[block, 2], row_recv.at[source, block], (goal, col)
+            )
+
+        def take(source, block):
+            copy = from_row(source, block)
+            copy.wait_recv()
+            copy.start()
+
+        def expert_rows(source, half):
+            return ex_all.at[
+                pl.ds(half * half_experts, half_experts),
+                pl.ds(pl.multiple_of(source * inner, inner), inner),
+            ]
+
+        def expert_to(n, half):
+            return remote(
+                ex_ref.at[pl.ds(half * half_experts, half_experts)], expert_rows(row, half),
+                ex_send.at[n, half], ex_recv.at[row, half], (goals[n], col),
+            )
+
+        def expert_onward(source, half, goal):
+            home = expert_rows(source, half)
+            return remote(
+                home, home, ex_send.at[2, half], ex_recv.at[source, half], (goal, col)
             )
 
         def shared_to(step):
@@ -649,55 +768,86 @@
                 (place.peer_row(step), col),
             )
 
-        down_row = lax.div(col, per_row)
-
-        def downs_to(act_far, act_here):
-            for step in range(rows_n):
-                for turn in range(per_row):
-                    goal_row, goal_col = place.peer_row(step), per_row * row + turn
-                    here = (goal_col == col) if step == 0 else None
-                    far = remote(
-                        sd_ref.at[turn], sd_all.at[col], sd_send.at[step, turn],
-                        sd_recv.at[col], (goal_row, goal_col),
-                    )
-                    if here is None:
-                        act_far(far)
-                        continue
-
-                    @pl.when(here)
-                    def _():
-                        act_here(
-                            pltpu.make_async_copy(
-                                sd_ref.at[turn], sd_all.at[col], sd_recv.at[col]
-                            )
-                        )
-
-                    @pl.when(jnp.logical_not(here))
-                    def _():
-                        act_far(far)
+        lines = LineGather(place, sd_ref, down_line, *l_sems)
+        holder = lax.div(col, per_row) == row
+        pieces = down_line.at[:, lax.rem(col, per_row)]
+        pieces_here = pltpu.make_async_copy(pieces, sd_all, sd_local)
+
+        def downs_to(step):
+            return remote(
+                pieces, sd_all, sd_send.at[step], sd_recv, (place.peer_row(step), col)
+            )
 
         weights.start()
         push(col, bundle_ref)
+        if square:
+            for n, half in ((0, 0), (1, 1)):
+                expert_to(n, half).start()
+        lines.start()
+        for dist in range(1, place.chips):
+            weights.step(dist, push)
+            lines.step(dist)
+        grads.start()
+        picks.start()
+        lines.finish()
+
+        @pl.when(holder)
+        def _():
+            pieces_here.start()
+            for step in range(1, rows_n):
+                downs_to(step).start()
+
+        if square:
+            for n, half in ((0, 1), (1, 0)):
+                expert_to(n, half).start()
+        else:
+            for n in range(n_goals):
+                for half in range(2):
+                    expert_to(n, half).start()
         shared_here = pltpu.make_async_copy(sh_ref, sh_all.at[row], sh_local)
         shared_here.start()
+        expert_here = [
+            pltpu.make_async_copy(
+                ex_ref.at[pl.ds(half * half_experts, half_experts)], expert_rows(row, half),
+                ex_local.at[half],
+            )
+            for half in range(2)
+        ]
+        for copy in expert_here:
+            copy.start()
         for step in range(1, rows_n):
             shared_to(step).start()
-        for dist in range(1, place.chips):
-            weights.step(dist, push)
-        downs_to(lambda far: far.start(), lambda here: here.start())
-        grads.start()
-        picks.start()
         for dist in range(1, place.chips - 1):
             grads.step(dist)
             picks.step(dist)
-        for step in range(1, rows_n):
-            other_row = place.peer_row(step)
+            if square and dist == 1:
+
+                @pl.loop(0, place.chips)
+                def _(i):
+                    chip = lax.rem(place.chip + i, place.chips)
+                    block = 2 * chip + place.core
+                    even = lax.rem(chip, 2) == 0
+                    take(across, block)
+
+                    @pl.when(even)
+                    def _():
+                        onward(across, block, along).start()
+
+                    take(along, block)
+
+                    @pl.when(jnp.logical_not(even))
+                    def _():
+                        onward(along, block, across).start()
+
+                expert_onward(across, 0, along).wait_recv()
+                expert_onward(across, 0, along).start()
+                expert_onward(along, 1, across).wait_recv()
+                expert_onward(along, 1, across).start()
+        for source in [corner] if square else sources:
 
             @pl.loop(0, place.chips)
             def _(chip):
-                copy = from_row(other_row, 2 * chip + place.core)
-                copy.wait_recv()
-                copy.start()
+                take(source, 2 * chip + place.core)
 
         grads.step(place.chips - 1)
         picks.step(place.chips - 1)
@@ -705,17 +855,33 @@
         grads.finish()
         picks.finish()
         shared_here.wait()
-        downs_to(lambda far: far.wait_send(), lambda here: here.wait())
-
-        @pl.loop(0, cols_n)
-        def _(source):
-            @pl.when(jnp.logical_not((source == col) & (down_row == row)))
-            def _():
-                remote(
-                    sd_ref.at[0], sd_all.at[source], sd_send.at[0, 0], sd_recv.at[source],
-                    (row, place.other),
-                ).wait_recv()
-
+        for copy in expert_here:
+            copy.wait()
+
+        @pl.when(holder)
+        def _():
+            pieces_here.wait()
+            for step in range(1, rows_n):
+                downs_to(step).wait_send()
+
+        @pl.when(jnp.logical_not(holder))
+        def _():
+            downs_to(1).wait_recv()
+
+        for n in range(n_goals):
+            for half in range(2):
+                expert_to(n, half).wait_send()
+        if square:
+            expert_onward(across, 0, along).wait_send()
+            expert_onward(along, 1, across).wait_send()
+            expert_onward(across, 1, along).wait_recv()
+            expert_onward(along, 0, across).wait_recv()
+            expert_onward(corner, 0, along).wait_recv()
+            expert_onward(corner, 1, along).wait_recv()
+        else:
+            for source in sources:
+                for half in range(2):
+                    expert_onward(source, half, source).wait_recv()
         for step in range(1, rows_n):
             other_row = place.peer_row(step)
             shared_to(step).wait_send()
@@ -724,37 +890,52 @@
                 (other_row, col),
             ).wait_recv()
 
-            @pl.loop(0, place.chips)
-            def _(chip):
-                to_row(2 * chip + place.core, step).wait_send()
-                from_row(other_row, 2 * chip + place.core).wait_send()
-                from_row(other_row, 2 * chip + 1 - place.core).wait_recv()
-
+        @pl.loop(0, place.chips)
+        def _(chip):
+            block = 2 * chip + place.core
+            for n in range(n_goals):
+                to_row(block, n).wait_send()
+            if square:
+                onward(across, block, along).wait_send()
+            for source in sources:
+                from_row(source, block).wait_send()
+                from_row(source, 2 * chip + 1 - place.core).wait_recv()
+
+    outs = [
+        jax.ShapeDtypeStruct((rows_n, cols_n) + bundle.shape, bundle.dtype),
+        jax.ShapeDtypeStruct((cols_n,) + cotangent.shape, cotangent.dtype),
+        jax.ShapeDtypeStruct((cols_n,) + routes_t.shape, routes_t.dtype),
+        jax.ShapeDtypeStruct((rows_n,) + shared.shape, shared.dtype),
+        jax.ShapeDtypeStruct((cols_n,) + downs.shape[1:], downs.dtype),
+        jax.ShapeDtypeStruct(
+            (expert.shape[0], rows_n * inner, expert.shape[2]), expert.dtype
+        ),
+    ] + [jax.ShapeDtypeStruct(a.shape, a.dtype) for a in later]
+    outs.append(jax.ShapeDtypeStruct((cols_n,) + downs.shape, downs.dtype))
     return pl.pallas_call(
         kernel,
-        in_specs=[ANY] * 5,
-        out_specs=[ANY] * 5,
-        out_shape=[
-            jax.ShapeDtypeStruct((rows_n, cols_n) + bundle.shape, bundle.dtype),
-            jax.ShapeDtypeStruct((cols_n,) + cotangent.shape, cotangent.dtype),
-            jax.ShapeDtypeStruct((cols_n,) + routes_t.shape, routes_t.dtype),
-            jax.ShapeDtypeStruct((rows_n,) + shared.shape, shared.dtype),
-            jax.ShapeDtypeStruct((cols_n,) + downs.shape[1:], downs.dtype),
-        ],
-        scratch_shapes=gather_sems(cols_n) * 3
+        in_specs=[ANY] * (6 + n_later),
+        out_specs=[ANY] * (7 + n_later),
+        out_shape=outs,
+        input_output_aliases={6 + i: 6 + i for i in range(n_later)},
+        scratch_shapes=gather_sems(cols_n) * 4
         + [
-            pltpu.SemaphoreType.DMA((cols_n, rows_n)),
+            pltpu.SemaphoreType.DMA((cols_n, max(rows_n, 3))),
             pltpu.SemaphoreType.DMA((rows_n, cols_n)),
             pltpu.SemaphoreType.DMA((rows_n, cols_n)),
             pltpu.SemaphoreType.DMA((rows_n,)),
             pltpu.SemaphoreType.DMA((rows_n,)),
             pltpu.SemaphoreType.DMA,
-            pltpu.SemaphoreType.DMA((rows_n, per_row)),
-            pltpu.SemaphoreType.DMA((cols_n,)),
+            pltpu.SemaphoreType.DMA((rows_n,)),
+            pltpu.SemaphoreType.DMA,
+            pltpu.SemaphoreType.DMA,
+            pltpu.SemaphoreType.DMA((max(rows_n, 3), 2)),
+            pltpu.SemaphoreType.DMA((rows_n, 2)),
+            pltpu.SemaphoreType.DMA((2,)),
         ],
         compiler_params=pltpu.CompilerParams(collective_id=collective_id, has_side_effects=True),
         name="first_gather",
-    )(bundle, cotangent, routes_t, shared, downs)
+    )(bundle, cotangent, routes_t, shared, downs, expert, *later)
 
 
 def line_sum_loop(place, mine, recv, send_sems, recv_sems, parts, ready):
@@ -854,10 +1035,11 @@
     return result, drain
 
 
-def dense_sum(lefts, rights, tails, shared, rounds, collective_id, rows_n, cols_n):
-    n_rounds = len(rounds)
-    moved = rounds[0][0]
+def dense_sum(lefts, rights, tails, shared, calls, collective_id, rows_n, cols_n):
     chips = cols_n // 2
+    n_rounds = chips - 1
+    moved = jax.ShapeDtypeStruct(calls[0][0].shape[1:], BF)
+    square = rows_n == 4
     inner = shared.shape[1]
     units = shared.shape[2] // 3
     per_row = cols_n // rows_n
@@ -868,14 +1050,14 @@
     def kernel(*refs):
         left_refs, right_refs = refs[:n], refs[n : 2 * n]
         (
-            tail_ref, sh_ref, *round_refs
-        ) = refs[2 * n : 2 * n + 2 + 2 * n_rounds]
+            tail_ref, sh_ref, *call_refs
+        ) = refs[2 * n : 2 * n + 2 + 2 * chips]
         (
             out_ref, sh_out, sd_out, arrivals,
             both, extra, rows_in, recv, sh_in, sd_cut, held, came, held_sems, came_sems,
             core_send, core_recv, row_send, row_recv, send_sems, recv_sems,
             sh_send, sh_recv, sh_local, move_send, move_recv, sd_send, sd_recv,
-        ) = refs[2 * n + 2 + 2 * n_rounds :]
+        ) = refs[2 * n + 2 + 2 * chips :]
         place = Place(rows_n, cols_n)
         row, col = place.row, place.col
         mine = both.at[place.core]
@@ -884,51 +1066,69 @@
         down_row = lax.div(col, per_row)
         place.greet(True, downs_back=per_row)
 
+        tables = round_tables(chips)[1:]
+
         def moves(turn):
-            pair = round_refs[:2] if turn == 0 else (held.at[0], held.at[1])
             return Moves(
-                place, *pair, arrivals.at[turn, 0], arrivals.at[turn, 1], move_send.at[turn],
-                move_recv.at[turn],
-            )
-
-        def hold(turn):
-            return [
-                pltpu.make_async_copy(
-                    round_refs[2 * turn + which], held.at[which], held_sems.at[which]
-                )
-                for which in range(2)
-            ]
+                place, held.at[0], held.at[1], arrivals.at[turn, 0], arrivals.at[turn, 1],
+                move_send.at[turn], move_recv.at[turn],
+            )
+
+        def add_came(which):
+            part = came.shape[1] // 4
+            for at in range(0, came.shape[1], part):
+                span = slice(at, at + part)
+                held[which, span] = (
+                    held[which, span].astype(F32) + came[which, span].astype(F32)
+                ).astype(BF)
+
+        def bring(which, own, other):
+            return (
+                pltpu.make_async_copy(own, held.at[which], held_sems.at[which]),
+                pltpu.make_async_copy(other, came.at[which], came_sems.at[which]),
+            )
 
         def next_round(turn):
-            moves(turn - 1).wait_send()
-            copies = hold(turn)
-            for copy in copies:
-                copy.start()
-            moves(turn - 1).wait_recv()
-            for which, comes in ((0, place.chip > 0), (1, place.chip < chips - 1)):
-                bring = pltpu.make_async_copy(
-                    arrivals.at[turn - 1, which], came.at[which], came_sems.at[which]
-                )
-
-                @pl.when(comes)
-                def _():
-                    bring.start()
-
-                copies[which].wait()
-
-                @pl.when(comes)
-                def _():
-                    bring.wait()
-                    part = came.shape[1] // 4
-                    for at in range(0, came.shape[1], part):
-                        span = slice(at, at + part)
-                        held[which, span] = (
-                            held[which, span].astype(F32) + came[which, span].astype(F32)
-                        ).astype(BF)
+            if turn:
+                moves(turn - 1).wait_send()
+            for which in range(2):
+                call = jnp.int32(0)
+                for chip in range(chips):
+                    call = call + jnp.where(place.chip == chip, tables[which][chip][turn], 0)
+                for i in range(turn + 1):
+
+                    @pl.when(call == i)
+                    def _():
+                        for copy in bring(which, call_refs[2 * i].at[0], call_refs[2 * i + 1].at[0]):
+                            copy.start()
+
+            for which in range(2):
+                for copy in bring(which, call_refs[0].at[0], call_refs[1].at[0]):
+                    copy.wait()
+                add_came(which)
+            if turn:
+                moves(turn - 1).wait_recv()
+                comes = (place.chip > 0, place.chip < chips - 1)
+                for which in range(2):
+
+                    @pl.when(comes[which])
+                    def _():
+                        pltpu.make_async_copy(
+                            arrivals.at[turn - 1, which], came.at[which], came_sems.at[which]
+                        ).start()
+
+                for which in range(2):
+
+                    @pl.when(comes[which])
+                    def _():
+                        pltpu.make_async_copy(
+                            arrivals.at[turn - 1, which], came.at[which], came_sems.at[which]
+                        ).wait()
+                        add_came(which)
 
             moves(turn).start()
 
-        moves(0).start()
+        next_round(0)
 
         def downs_to(turn, act_far, act_here):
             goal_col = per_row * row + turn
@@ -971,6 +1171,20 @@
                 (source, col),
             )
 
+        across = along = corner = None
+        if square:
+            across, along, corner = place.square()
+
+        def ways(chip):
+            return (across, along) if chip % 2 == 0 else (along, across)
+
+        def to_near(goal, slot, chip):
+            near = ways(chip)[1 if slot == 2 else 0]
+            return remote(
+                mine.at[goal, chip], rows_in.at[slot, chip], row_send.at[slot, chip],
+                row_recv.at[slot, chip], (near, col),
+            )
+
         def to_row(goal, chip):
             return remote(
                 mine.at[goal, chip], rows_in.at[row, chip], row_send.at[goal, chip],
@@ -997,7 +1211,26 @@
                     mine[goal, chip] = (
                         mine[goal, chip].astype(F32) + extra[goal, chip].astype(F32)
                     ).astype(BF)
-                    to_row(goal, chip).start()
+                    if not square:
+                        to_row(goal, chip).start()
+                        continue
+
+                    @pl.when(goal == ways(chip)[0])
+                    def _():
+                        to_near(goal, 0, chip).start()
+
+                    @pl.when(goal == corner)
+                    def _():
+                        to_near(goal, 1, chip).start()
+
+        def hand_on():
+            for chip in order:
+                goal = ways(chip)[1]
+                to_near(goal, 1, chip).wait_recv()
+                mine[goal, chip] = (
+                    mine[goal, chip].astype(F32) + rows_in[1, chip].astype(F32)
+                ).astype(BF)
+                to_near(goal, 2, chip).start()
 
         for step in range(1, rows_n):
             shared_to(step).start()
@@ -1020,6 +1253,8 @@
         push(rows_n - 1)
         for turn in range(1, n_rounds):
             next_round(turn)
+            if square and turn == 1:
+                hand_on()
         shared_here.wait()
         for step in range(1, rows_n):
             shared_from(step).wait_recv()
@@ -1034,9 +1269,17 @@
 
         def ready(chip):
             total = mine[row, chip].astype(F32) + extra[row, chip].astype(F32)
-            for step in range(1, rows_n):
-                from_row(step, chip).wait_recv()
-                total = total + rows_in[place.peer_row(step), chip].astype(F32)
+            if square:
+                for slot in (0, 2):
+                    remote(
+                        mine.at[row, chip], rows_in.at[slot, chip], row_send.at[slot, chip],
+                        row_recv.at[slot, chip], (across, col),
+                    ).wait_recv()
+                    total = total + rows_in[slot, chip].astype(F32)
+            else:
+                for step in range(1, rows_n):
+                    from_row(step, chip).wait_recv()
+                    total = total + rows_in[place.peer_row(step), chip].astype(F32)
             mine[row, chip] = total.astype(BF)
 
         result, drain = line_sum_loop(
@@ -1068,15 +1311,22 @@
         for goal in range(rows_n):
             swap(goal).wait_send()
 
-            @pl.when(goal != row)
-            def _():
-                for chip in range(chips):
-                    to_row(goal, chip).wait_send()
+            if not square:
+
+                @pl.when(goal != row)
+                def _():
+                    for chip in range(chips):
+                        to_row(goal, chip).wait_send()
+
+        if square:
+            for chip in range(chips):
+                for slot in range(3):
+                    to_near(row, slot, chip).wait_send()
 
     vmem = pl.BlockSpec(memory_space=pltpu.VMEM)
     return pl.pallas_call(
         kernel,
-        in_specs=[vmem] * (2 * n + 1) + [ANY] * (1 + 2 * n_rounds),
+        in_specs=[vmem] * (2 * n + 1) + [ANY] * (1 + 2 * chips),
         out_specs=[vmem, vmem, vmem, ANY],
         out_shape=[
             jax.ShapeDtypeStruct(block, F32),
@@ -1117,7 +1367,7 @@
             flops=2 * 512 * 1536 * 4096, bytes_accessed=350_000_000, transcendentals=0
         ),
         name="dense_sum",
-    )(*lefts, *rights, tails, shared, *[part for pair in rounds for part in pair])
+    )(*lefts, *rights, tails, shared, *[part for pair in calls for part in pair])
 
 
 def round_tables(chips):
@@ -1137,32 +1387,12 @@
     def __init__(self, cols_n):
         self.chips = cols_n // 2
         here = lax.axis_index("col") // 2
-        _, up, down = round_tables(self.chips)
-        self.up_call = jnp.array(up, jnp.int32)[here]
-        self.down_call = jnp.array(down, jnp.int32)[here]
         self.not_first, self.not_last = here > 0, here < self.chips - 1
         self.sums = []
         self.below = self.above = None
 
     def add(self, own, other):
         self.sums.append((own, other))
-
-    def held(self, call):
-        total = None
-        for i, (own, other) in enumerate(self.sums):
-            value = own.astype(F32) + other.astype(F32)
-            total = value if i == 0 else jnp.where(call == i, value, total)
-        return total
-
-    def kept(self, turn):
-        return [self.held(call[turn]).astype(BF) for call in (self.up_call, self.down_call)]
-
-    def outgoing(self, turn):
-        ups, downs = self.held(self.up_call[turn]), self.held(self.down_call[turn])
-        if turn:
-            ups = ups + jnp.where(self.not_first, self.below.astype(F32), 0.0)
-            downs = downs + jnp.where(self.not_last, self.above.astype(F32), 0.0)
-        return ups.astype(BF), downs.astype(BF)
 
     def arrived(self, below, above):
         self.below, self.above = below, above
@@ -1174,11 +1404,14 @@
         return total + jnp.where(self.not_last, self.above.astype(F32), 0.0)
 
 
-def routed_kernel(call, rows_n, cols_n, n_moves, *refs):
+def routed_kernel(call, rows_n, cols_n, *refs):
     (
         x_hbm, dy_hbm, routes_hbm, routes_t_hbm, gates_hbm, eg_ref, eu_ref, ed_ref, sgu_ref, sd_ref
     ) = refs[:10]
-    up_down, refs = refs[10 : 10 + n_moves], refs[10 + n_moves :]
+    n_moves = 2 if call else 0
+    n_before = 2 if call > 1 else 0
+    call_refs, refs = refs[10 : 10 + 2 * call], refs[10 + 2 * call :]
+    before, refs = refs[:n_before], refs[n_before:]
     (
         own_hbm, other_hbm, xs_hbm, dys_hbm, hid_ref, gg_ref, gu_ref, ggw_ref, shared_ref
     ) = refs[:9]
@@ -1186,7 +1419,7 @@
     (
         x_ref, dy_ref, routes_ref, routes_t_ref, gates_ref,
         xs, dys, pick, back_pick, wide_out, wide_gx, slot_gate, stage,
-        load_sems, slot_sems, own_sems, core_send, core_recv, move_send, move_recv,
+        load_sems, slot_sems, own_sems, core_send, core_recv, *refs,
     ) = refs
     place = Place(rows_n, cols_n)
     my_core = place.core
@@ -1205,7 +1438,8 @@
     ]
     moves = None
     if n_moves:
-        moves = Moves(place, *up_down, *arrivals, move_send, move_recv)
+        line = RoundStart(place, call_refs, *refs[:4])
+        moves = line.moves(arrivals, *refs[4:])
     e = pl.program_id(0)
     total = x_ref.shape[1]
     cap = xs.shape[1] // 2
@@ -1234,6 +1468,9 @@
             load.start()
         place.greet(False)
         if n_moves:
+            line.prepare(call - 1)
+            if n_before:
+                line.add(before)
             moves.start()
         ggw_ref[...] = jnp.zeros_like(ggw_ref)
         for load in loads:
@@ -1354,7 +1591,12 @@
             core_copy(which).wait_recv()
 
 
-def routed(call, rows_n, x_all, dy_all, routes, routes_t, gates, egate, eup, edown, sgu, sdown, moves):
+def routed(
+    call, rows_n, x_all, dy_all, routes, routes_t, gates, egate, eup, edown, sgu, sdown, calls,
+    before,
+):
+    call_args = [part for pair in calls for part in pair] + list(before)
+    n_moves = 2 if call else 0
     cols_n, total, width = x_all.shape
     cap = 4 * total * TOP // (3 * EXP_DEV * cols_n)
     slots = 2 * cap
@@ -1371,19 +1613,19 @@
 
     slot_block = each(slots, ffn)
     return pl.pallas_call(
-        functools.partial(routed_kernel, call, rows_n, cols_n, len(moves)),
+        functools.partial(routed_kernel, call, rows_n, cols_n),
         grid=(EXP_DEV,),
         in_specs=[ANY] * 5
         + [
             each(width, ffn), each(width, ffn), each(ffn, width), whole(*sgu.shape),
             whole(*sdown.shape),
         ]
-        + [ANY] * len(moves),
+        + [ANY] * len(call_args),
         out_specs=[
             ANY, ANY, ANY, ANY, slot_block, slot_block, slot_block,
             whole(2, 8, total), whole(width, 3 * hidden_units),
         ]
-        + [ANY] * len(moves),
+        + [ANY] * n_moves,
         out_shape=[
             jax.ShapeDtypeStruct((2, total, width), BF),
             jax.ShapeDtypeStruct((2, total, width), BF),
@@ -1395,7 +1637,7 @@
             jax.ShapeDtypeStruct((2, 8, total), F32),
             jax.ShapeDtypeStruct((width, 3 * hidden_units), F32),
         ]
-        + [jax.ShapeDtypeStruct(a.shape, a.dtype) for a in moves],
+        + [jax.ShapeDtypeStruct((total, width), BF)] * n_moves,
         scratch_shapes=[
             pltpu.VMEM((2, total, width), BF),
             pltpu.VMEM((2, total, width), BF),
@@ -1415,9 +1657,13 @@
             pltpu.SemaphoreType.DMA((2,)),
             pltpu.SemaphoreType.DMA((2,)),
             pltpu.SemaphoreType.DMA((2,)),
-            pltpu.SemaphoreType.DMA((2,)),
-            pltpu.SemaphoreType.DMA((2,)),
-        ],
+        ]
+        + (
+            RoundStart.scratch((total, width))
+            + [pltpu.SemaphoreType.DMA((2,)), pltpu.SemaphoreType.DMA((2,))]
+            if call
+            else []
+        ),
         compiler_params=pltpu.CompilerParams(
             collective_id=4 + call, has_side_effects=True, vmem_limit_bytes=60 * 1024 * 1024
         ),
@@ -1426,7 +1672,7 @@
         ),
         name="routed",
     )(
-        x_all, dy_all, routes, routes_t, gates, egate, eup, edown, sgu, sdown, *moves
+        x_all, dy_all, routes, routes_t, gates, egate, eup, edown, sgu, sdown, *call_args
     )
 
 
@@ -1509,8 +1755,8 @@
     shared = jnp.concatenate([s_gate, s_up], axis=1)
     per_row = s_down.shape[0] // units
     downs = s_down.reshape(per_row, units, s_down.shape[1])
-    full, dy_all, routes_all, sgu, sdown = first_gather(
-        bundle, cotangent, routes_t, shared, downs, 0, rows_n, cols_n
+    full, dy_all, routes_all, sgu, sdown, egate, e_up, e_down, _ = first_gather(
+        bundle, cotangent, routes_t, shared, downs, e_gate, [e_up, e_down], 0, rows_n, cols_n
     )
     sdown = jnp.swapaxes(sdown, 0, 1).reshape(units, width)
     sgu = sgu.reshape(width, 2 * units)
@@ -1520,11 +1766,13 @@
     n_gain = g_attn.shape[0]
     gains = full[:, :, t_at + EXP_DEV : t_at + EXP_DEV + 2, :n_gain].transpose(2, 0, 1, 3)
     gains = gains.reshape(2, width).astype(F32)
-    egate = lax.all_gather(e_gate, "row", axis=1, tiled=True)
     eup = lax.all_gather(e_up, "row", axis=1, tiled=True)
     edown = lax.all_gather(e_down, "row", axis=2, tiled=True)
-    own_lens = lengths[deal.reshape(-1) * cols_n + col_here, row_here]
-    seq_ends = jnp.cumsum(own_lens)
+    by_row = lengths.reshape(rows_n, cols_n, rows_n)
+    by_row = lax.dynamic_slice(by_row, (0, col_here, row_here), (rows_n, 1, 1)).reshape(1, rows_n)
+    row_ids = jnp.arange(rows_n, dtype=jnp.int32)
+    own_lens = jnp.sum(jnp.where(deal.reshape(-1, 1) == row_ids, by_row, 0), axis=1)
+    seq_ends = jnp.sum(jnp.where(row_ids[None, :] <= row_ids[:, None], own_lens, 0), axis=1)
     places = jnp.arange(total, dtype=jnp.int32)
     segment = jnp.sum((places[:, None] >= seq_ends[None, :]).astype(jnp.int32), axis=1)
 
@@ -1537,38 +1785,35 @@
     chips = cols_n // 2
     my_order = jnp.array(round_tables(chips)[0], jnp.int32)[col_here // 2]
     routes_rows = jnp.swapaxes(routes_all, 1, 2)
-    gx_sum, moe_sum = LineRounds(cols_n), LineRounds(cols_n)
-    saved, ggw, grad_sh = [], 0.0, 0.0
+    moe_sum = LineRounds(cols_n)
+    saved, calls, before, ggw, grad_sh = [], [], (), [], 0.0
     for call in range(chips):
-        moves = gx_sum.outgoing(call - 1) if call else ()
         own, other, *keep = routed(
             call, rows_n, x_all, dy_all, routes_all, routes_rows, gates_all, egate, eup, edown,
-            sgu, sdown, moves,
+            sgu, sdown, calls, before,
         )
         saved.append(keep[:5])
         ggw_part, sh_part, *arrivals = keep[5:]
-        if call:
-            gx_sum.arrived(*arrivals)
+        before = tuple(arrivals)
         grad_sh = grad_sh + sh_part
-        is_unit = jnp.arange(chips, dtype=jnp.int32)[:, None, None, None] == my_order[call]
-        ggw = ggw + jnp.where(is_unit, ggw_part[None], 0.0)
-        gx_sum.add(own[1], other[1])
-        moe_sum.add(own[0], other[0])
+        ggw.append(ggw_part)
+        calls.append((own, other))
     xs, dys, hid, gg, gu = zip(*saved)
     grad_edown = expert_grads(hid, dys, rows_n, False)
     grad_egate = expert_grads(xs, gg, rows_n, True)
     grad_eup = expert_grads(xs, gu, rows_n, True)
-    ggw = ggw.reshape(cols_n, 8, total)[:, :EXP_DEV]
+    ggw = jnp.stack(ggw)[:, None, :, :EXP_DEV]
+    is_unit = my_order[:, None] == jnp.arange(chips, dtype=jnp.int32)
+    ggw = jnp.sum(jnp.where(is_unit[:, :, None, None, None], ggw, 0.0), axis=0)
+    ggw = ggw.reshape(cols_n, EXP_DEV, total)
 
     ggw_home = lax.all_to_all(ggw, "col", split_axis=0, concat_axis=0, tiled=True)
     grad_tokens, gq, gk, gv, grad_attn_b, logits_left, gain_grads = block_end(
         tokens, cotangent, full, extents, gains, segment, routes, gates,
         ggw_home.reshape(experts, total),
-        (gx_sum.sums[-1][0], gx_sum.sums[-1][1], gx_sum.below, gx_sum.above),
+        (calls[-1][0][1], calls[-1][1][1], *before),
         queries, keys, values, log_totals, after_attn, scale_one, scale_two,
     )
-
-    rounds = [moe_sum.outgoing(0)] + [moe_sum.kept(turn) for turn in range(1, chips - 1)]
 
     def gain_rows(grad):
         part = grad.reshape(rows_n, cols_n, 1, n_gain)
@@ -1581,8 +1826,9 @@
     dense, dense_sh, sd_parts, arrivals = dense_sum(
         [gq, gk, gv, grad_attn_b, logits_left],
         [normed_one, normed_one, normed_one, mixed, normed_two],
-        tails, grads_sh, rounds, 2, rows_n, cols_n,
+        tails, grads_sh, calls, 2, rows_n, cols_n,
     )
+    moe_sum.add(calls[-1][0][0], calls[-1][1][0])
     moe_sum.arrived(arrivals[-1, 0], arrivals[-1, 1])
     output = (after_attn + moe_sum.result()).astype(BF)
     out_wq = dense[:q_w].T

time: 858 us -> 806 us (0.939)
  other arithmetic: 64 us -> 24 us
  between operations: 26.7 us -> 14.5 us
    convert_element_type x10 -> x0, other arithmetic: 36.6 us -> none  [the longest x6 22.8 us: outgoing(): return (ups.astype(BF), downs.astype(BF))]
    pallas_call x6, Pallas kernels: 499 us -> 508 us  [the longest x4 182 us: routed(): pl.pallas_call(functools.partial(routed_kernel, call, rows_n, cols_n), gr...]
  transfers between devices with their start and end apart: 7 -> 6, of which waited for: 0 -> 1; matrix products, arithmetic and copies ran while one was open for 9% -> 5% of each run, Pallas kernels for 64% -> 48%
where the time goes in v5:
time: 806 us; the launch traced here: 803 us
  Pallas kernels  724 us (90%)
  local copies, waits for them, and re-layouts  27.5 us (3%)
  other arithmetic  24 us (3%)
  between operations  14.5 us (2%)
  waiting for transfers between devices  8.25 us (1%)
    pallas_call x4, Pallas kernels, routed(): pl.pallas_call(functools.partial(routed_kernel, call, rows_n, cols_n), gr...  182 us
    pallas_call x1, Pallas kernels, dense_sum(): pl.pallas_call(kernel, in_specs=[vmem] * (2 * n + 1) + [ANY] * (1 + 2 * c...  179 us
    pallas_call x1, Pallas kernels, first_gather(): pl.pallas_call(kernel, in_specs=[ANY] * (6 + n_later), out_specs=[ANY] *...  146 us
    pallas_call x1, Pallas kernels, line_gather(): pl.pallas_call(kernel, in_specs=[ANY] * n, out_specs=[ANY] * n, out_shape...  114 us
    pallas_call x1, Pallas kernels, block_end(): pl.pallas_call(kernel, in_specs=[pl.BlockSpec(memory_space=pl.ANY)] * n +...  38.8 us
    pallas_call x3, Pallas kernels, expert_grads(): pl.pallas_call(functools.partial(expert_grads_kernel, units_n, rows_n, cu...  37 us
    pallas_call x1, Pallas kernels, block_start(): pl.pallas_call(kernel, in_specs=[pl.BlockSpec(memory_space=pl.ANY)] * n +...  27.3 us
  transfers between devices with their start and end apart: 6, of which 1 were waited for; matrix products, arithmetic and copies ran while one was open for 5% of the time, Pallas kernels for 48%

profile of v5, /device:TPU:2, one launch (start us, length us, event | category | flops | bytes accessed | tf_op | source)
XLA Modules:
  0.0 803.1 jit_solution(6752166134785961571)
XLA Ops:
  7.3 0.0 all-gather.3.cloned.1.call-start
  7.4 2.8 copy.99.refs_6_
  10.2 1.2 copy.100.refs_7_
  11.4 0.8 copy.74
  12.3 0.7 pad_maximum_fusion.refs_3_
  13.0 0.6 pad.25.refs_2_
  13.6 0.7 copy-done.5
  14.4 146.3 %first_gather.1 = (bf16[4,8,528,384]{3,2,1,0:T(8,128)(2,1)}, bf16[8,512,1536]{2,1,0:T(8,128)(2,1)}, s32[8,8,512]{2,1,0:T(8,128)}, bf16[4,384,256]{2,1,0:T(8,128)...) custom-call(bf16[528,384]{1,0:T(8,128)(2,1)} %copy-done.5, ...), custom_call_target="tpu_custom_call", output_to_operand_aliasing={{6}: (6, {}), {7}: (7, {})} | custom-call | tf_op jit(solution)/shard_map/first_gather/pallas_call | solution.py:915
  160.7 0.0 all-gather.3.cloned.1.call-update
  160.8 0.0 all-gather.5.cloned.1.call-start
  160.8 0.7 all-gather.5.cloned.1.call-update
  161.5 0.3 reduce-scatter.14.cloned.1.call-start
  161.8 0.9 copy.77.refs_5_.refs_6_
  162.6 0.1 reshape.108
  162.7 0.2 dynamic-slice_reduce_fusion
  162.9 0.2 select_reduce_fusion.2
  163.1 0.1 select_reduce_fusion.1
  163.2 0.1 convert_reduce_fusion
  163.3 0.9 copy.76.refs_3_.refs_4_
  164.2 0.9 convert_bitcast_fusion
  165.0 0.7 reshape.116.refs_2_.refs_3_
  165.7 1.9 copy.78
  167.7 0.3 copy.79
  167.9 0.9 copy.83.refs_9_
  168.9 27.3 %block_start.1 = (bf16[512,1536]{1,0:T(8,128)(2,1)}, bf16[512,1536]{1,0:T(8,128)(2,1)}, bf16[512,512]{1,0:T(8,128)(2,1)}, bf16[512,512]{1,0:T(8,128)(2,1)}, bf16...) custom-call(bf16[4,8,528,384]{3,2,1,0:T(8,128)(2,1)} %get-tuple-elem, ...), custom_call_target="tpu_custom_call" | custom-call | flops 10000000000 | bytes 30000000 | tf_op jit(solution)/shard_map/block_start/pallas_call | solution.py:243
  196.2 113.8 %line_gather.1 = (bf16[8,512,1536]{2,1,0:T(8,128)(2,1)}, f32[8,8,512]{2,1,0:T(8,128)}) custom-call(bf16[512,1536]{1,0:T(8,128)(2,1)} %get-tuple-element.92.refs_0_.refs_9_, f32[8,512]{1,0:T(8,128)} %get-tuple-element.93.refs_1_), custom_call_target="tpu_custom_call" | custom-call | tf_op jit(solution)/shard_map/line_gather/pallas_call | solution.py:671
  310.0 0.0 all-gather.3.cloned.1.call-done.refs_6_
  310.0 7.5 all-gather.5.cloned.1.call-done.refs_7_
  317.5 37.9 %routed.4 = (bf16[2,512,1536]{2,1,0:T(8,128)(2,1)}, bf16[2,512,1536]{2,1,0:T(8,128)(2,1)}, bf16[4,256,1536]{2,1,0:T(8,128)(2,1)}, bf16[4,256,1536]{2,1,0:T(8,128...) custom-call(bf16[8,512,1536]{2,1,0:T(8,128)(2,1)} %get-tuple-element, ...), custom_call_target="tpu_custom_call" | custom-call | flops 24000000000 | bytes 100000000 | tf_op jit(solution)/shard_map/routed/pallas_call | solution.py:1615
  355.4 47.0 %routed.5 = (bf16[2,512,1536]{2,1,0:T(8,128)(2,1)}, bf16[2,512,1536]{2,1,0:T(8,128)(2,1)}, bf16[4,256,1536]{2,1,0:T(8,128)(2,1)}, bf16[4,256,1536]{2,1,0:T(8,128...) custom-call(bf16[8,512,1536]{2,1,0:T(8,128)(2,1)} %get-tuple-element, ...), custom_call_target="tpu_custom_call" | custom-call | flops 24000000000 | bytes 100000000 | tf_op jit(solution)/shard_map/routed/pallas_call | solution.py:1615
  402.4 48.7 %routed.6 = (bf16[2,512,1536]{2,1,0:T(8,128)(2,1)}, bf16[2,512,1536]{2,1,0:T(8,128)(2,1)}, bf16[4,256,1536]{2,1,0:T(8,128)(2,1)}, bf16[4,256,1536]{2,1,0:T(8,128...) custom-call(bf16[8,512,1536]{2,1,0:T(8,128)(2,1)} %get-tuple-element, ...), custom_call_target="tpu_custom_call" | custom-call | flops 24000000000 | bytes 100000000 | tf_op jit(solution)/shard_map/routed/pallas_call | solution.py:1615
  451.1 48.2 %routed.7 = (bf16[2,512,1536]{2,1,0:T(8,128)(2,1)}, bf16[2,512,1536]{2,1,0:T(8,128)(2,1)}, bf16[4,256,1536]{2,1,0:T(8,128)(2,1)}, bf16[4,256,1536]{2,1,0:T(8,128...) custom-call(bf16[8,512,1536]{2,1,0:T(8,128)(2,1)} %get-tuple-element, ...), custom_call_target="tpu_custom_call" | custom-call | flops 24000000000 | bytes 100000000 | tf_op jit(solution)/shard_map/routed/pallas_call | solution.py:1615
  499.4 13.3 %expert_grads.5 = bf16[4,4,512,384]{3,2,1,0:T(8,128)(2,1)} custom-call(bf16[4,256,512]{2,1,0:T(8,128)(2,1)} %get-tuple-element.155.refs_0_, bf16[4,256,512]{2,1,0:T(8,128)(2,1)} %get-tuple-element.156.refs_1_, bf16[4,256,512]{2,1,0:T(8,128)(2,1)} %get-tuple-element.157.refs_2_, bf16[4,256,512]{2,1,0:T(8,128)(2,1)} %get-tuple-element.158.refs_3_, ...), custom_call_target="tpu_custom_call" | custom-call | flops 7000000000 | bytes 30000000 | tf_op jit(solution)/shard_map/expert_grads/pallas_call | solution.py:1701
  512.7 0.0 reduce-scatter.14.cloned.1.call-update
  512.7 0.0 reduce-scatter.12.cloned.1.call-start
  512.7 11.8 %expert_grads.4 = bf16[4,4,384,512]{3,2,1,0:T(8,128)(2,1)} custom-call(bf16[4,256,1536]{2,1,0:T(8,128)(2,1)} %get-tuple-element.143.refs_0_, bf16[4,256,1536]{2,1,0:T(8,128)(2,1)} %get-tuple-element.144.refs_1_, bf16[4,256,1536]{2,1,0:T(8,128)(2,1)} %get-tuple-element.145.refs_2_, bf16[4,256,1536]{2,1,0:T(8,128)(2,1)} %get-tuple-element.146.refs_3_, ...), custom_call_target="tpu_custom_call" | custom-call | flops 7000000000 | bytes 30000000 | tf_op jit(solution)/shard_map/expert_grads/pallas_call | solution.py:1701
  524.5 0.0 reduce-scatter.10.cloned.1.call-start
  524.6 11.9 %expert_grads.3 = bf16[4,4,384,512]{3,2,1,0:T(8,128)(2,1)} custom-call(bf16[4,256,1536]{2,1,0:T(8,128)(2,1)} %get-tuple-element.143.refs_0_, bf16[4,256,1536]{2,1,0:T(8,128)(2,1)} %get-tuple-element.144.refs_1_, bf16[4,256,1536]{2,1,0:T(8,128)(2,1)} %get-tuple-element.145.refs_2_, bf16[4,256,1536]{2,1,0:T(8,128)(2,1)} %get-tuple-element.146.refs_3_, ...), custom_call_target="tpu_custom_call" | custom-call | flops 7000000000 | bytes 30000000 | tf_op jit(solution)/shard_map/expert_grads/pallas_call | solution.py:1701
  536.6 0.0 reduce-scatter.10.cloned.1.call-update
  536.6 0.8 dynamic-slice_bitcast_fusion
  537.5 0.1 iota_compare_fusion.3
  537.6 0.8 select_reduce_fusion
  538.3 3.9 all-to-all-start
  542.3 5.2 add_convert_fusion
  547.4 0.6 copy-done.2
  548.0 1.9 slice_bitcast_fusion
  549.9 0.7 reshape.112.refs_8_
  550.6 38.8 %block_end.1 = (f32[512,1536]{1,0:T(8,128)}, bf16[512,1536]{1,0:T(8,128)(2,1)}, bf16[512,512]{1,0:T(8,128)(2,1)}, bf16[512,512]{1,0:T(8,128)(2,1)}, bf16[512,153...) custom-call(bf16[4,8,528,384]{3,2,1,0:T(8,128)(2,1)} %get-tuple-element.90.refs_0_, ...), custom_call_target="tpu_custom_call" | custom-call | flops 20000000000 | bytes 40000000 | tf_op jit(solution)/shard_map/block_end/pallas_call | solution.py:361
  589.4 0.8 slice_reduce_fusion.1
  590.2 0.1 reshape_squeeze.6
  590.3 0.1 reshape_squeeze.7
  590.3 0.1 fusion.2
  590.4 1.0 pad.28
  591.4 179.4 %dense_sum.1 = (f32[528,384]{1,0:T(8,128)}, f32[384,256]{1,0:T(8,128)}, f32[2,192,128]{2,1,0:T(8,128)}, bf16[3,2,512,1536]{3,2,1,0:T(8,128)(2,1)}) custom-call(bf16[512,1536]{1,0:T(8,128)(2,1)} %get-tuple-element.128.refs_0_, bf16[512,512]{1,0:T(8,128)(2,1)} %get-tuple-element.129.refs_1_, bf16[512,512]{1,0:T(8,128)(2,1)} %get-tuple-element.130.refs_2_, ...), custom_call_target="tpu_custom_call" | custom-call | flops 6442450944 | bytes 350000000 | tf_op jit(solution)/shard_map/dense_sum/pallas_call | solution.py:1327
  770.8 1.3 slice_bitcast_fusion.7
  772.1 1.3 slice_bitcast_fusion.6
  773.4 1.6 slice_bitcast_fusion.4
  775.0 1.6 copy_bitcast_fusion
  776.6 1.8 fusion.10
  778.4 1.9 slice_bitcast_fusion.2
  780.3 5.6 fusion.1
  786.0 3.3 bitcast_convert_fusion
  789.3 3.5 bitcast_convert_fusion.1
  792.8 3.5 bitcast_convert_fusion.2
  (63 shorter events, 0.2 us)
Async XLA Ops:
  7.2 5.1 copy-start.24
  7.2 4.2 copy-start.7
  7.2 5.0 copy-start.14
  7.2 5.0 copy-start.15
  7.2 5.0 copy-start.8
  7.2 5.0 copy-start.23
  7.2 6.4 copy-start.21
  7.3 2.9 copy-start.4
  7.3 5.0 copy-start.12
  7.3 5.0 copy-start.11
  7.3 4.1 copy-start.10
  7.3 5.7 copy-start.13
  7.3 302.7 %all-gather.3.cloned.1.call-start = ((), (), s32[]{:S(2)}) async-start(), calls=%async_computation.4 | async-start | bytes 7864320 | tf_op jit(solution)/shard_map/all_gather | solution.py:1769
  13.6 0.8 copy-start.5
  160.7 2.0 copy-start.22
  160.7 2.2 copy-start.25
  160.7 5.0 copy-start.9
  160.7 6.9 copy-start.6
  160.8 156.7 %all-gather.5.cloned.1.call-start = ((), (), s32[]{:S(2)}) async-start(), calls=%async_computation.5 | async-start | bytes 7864320 | tf_op jit(solution)/shard_map/all_gather | solution.py:1770
  161.5 624.5 %reduce-scatter.14.cloned.1.call-start = ((), (), s32[]{:S(2)}) async-start(), calls=%async_computation.8 | async-start | bytes 7864320
  163.3 5.6 copy-start.20
  512.7 276.6 %reduce-scatter.12.cloned.1.call-start = ((), (), s32[]{:S(2)}) async-start(), calls=%async_computation.7 | async-start | bytes 7864320
  524.5 268.2 %reduce-scatter.10.cloned.1.call-start = ((), (), s32[]{:S(2)}) async-start(), calls=%async_computation.6 | async-start | bytes 7864320
  536.5 1.0 copy-start.16
  536.5 1.0 copy-start.17
  536.5 1.0 copy-start.18
  536.5 1.0 copy-start.19
  536.6 5.7 copy-start.3
  538.3 11.6 %all-to-all-start = ((f32[8,4,512]{2,1,0:T(4,128)}), f32[8,4,512]{2,1,0:T(4,128)S(1)}, u32[]{:S(2)}, u32[]{:S(2)}) async-start(f32[8,4,512]{2,1,0:T(4,128)} %bitcast.23), calls=%async_computation | async-start | bytes 131072 | tf_op jit(solution)/shard_map/all_to_all | solution.py:1810
  542.2 5.2 copy-start
  542.3 5.8 copy-start.2
  591.4 189.0 %copy-start.1 = (bf16[2,512,1536]{2,1,0:T(8,128)(2,1)S(1)}, bf16[2,512,1536]{2,1,0:T(8,128)(2,1)}, u32[]{:S(2)}) copy-start(bf16[2,512,1536]{2,1,0:T(8,128)(2,1)} %get-tuple-element.113.refs_18_) | copy-start | bytes 9437188
Sparse Core Ops, SparseCore 0:
  160.9 84.6 all-gather.2
  247.4 69.9 all-gather.4
  512.8 74.0 reduce-scatter.13
  589.8 116.2 reduce-scatter.11
  708.9 78.4 reduce-scatter.9

commit v6 on v5

--- a/solution.py
+++ b/solution.py
@@ -479,28 +479,40 @@
 
 
 class RoundStart:
-    def __init__(self, place, call_refs, held, came, held_sems, came_sems):
-        self.place, self.call_refs = place, call_refs
-        self.held, self.came = held, came
-        self.held_sems, self.came_sems = held_sems, came_sems
+    PARTS = 4
+
+    def __init__(self, place, call_refs, after, held, came, brought, load_sems, sends, recvs):
+        self.place, self.call_refs, self.after = place, call_refs, after
+        self.held, self.came, self.brought = held, came, brought
+        self.load_sems, self.sends, self.recvs = load_sems, sends, recvs
         self.tables = round_tables(place.chips)[1:]
-
-    def bring(self, which, call):
-        own, other = self.call_refs[2 * call], self.call_refs[2 * call + 1]
-        return (
-            pltpu.make_async_copy(own.at[1], self.held.at[which], self.held_sems.at[which]),
-            pltpu.make_async_copy(other.at[1], self.came.at[which], self.came_sems.at[which]),
+        self.leaves = (place.chip < place.chips - 1, place.chip > 0)
+        self.comes = (place.chip > 0, place.chip < place.chips - 1)
+
+    def loads(self, which, call):
+        pair = (self.held, self.came)
+        return [
+            pltpu.make_async_copy(
+                self.call_refs[2 * call + i].at[1], pair[i].at[which], self.load_sems.at[which, i]
+            )
+            for i in range(2)
+        ]
+
+    def earlier(self, which, before):
+        return pltpu.make_async_copy(
+            before[which], self.brought.at[which], self.load_sems.at[which, 2]
         )
 
-    def add_came(self, which):
-        part = self.came.shape[1] // 4
-        for at in range(0, self.came.shape[1], part):
-            span = slice(at, at + part)
-            self.held[which, span] = (
-                self.held[which, span].astype(F32) + self.came[which, span].astype(F32)
-            ).astype(BF)
-
-    def prepare(self, turn):
+    def copy(self, which, part):
+        rows = self.held.shape[1] // self.PARTS
+        span = pl.ds(part * rows, rows)
+        return remote(
+            self.held.at[which, span], self.after[which].at[span], self.sends.at[which, part],
+            self.recvs.at[which, part],
+            (self.place.row, self.place.col + (2, -2)[which]),
+        )
+
+    def load(self, turn, before):
         for which in range(2):
             call = jnp.int32(0)
             for chip in range(self.place.chips):
@@ -510,47 +522,60 @@
 
                 @pl.when(call == i)
                 def _():
-                    for copy in self.bring(which, i):
+                    for copy in self.loads(which, i):
                         copy.start()
 
+            if before:
+
+                @pl.when(self.comes[which])
+                def _():
+                    self.earlier(which, before).start()
+
+    def send(self, before):
         for which in range(2):
-            for copy in self.bring(which, 0):
+            for copy in self.loads(which, 0):
                 copy.wait()
-            self.add_came(which)
-
-    def add(self, before):
-        comes = (self.place.chip > 0, self.place.chip < self.place.chips - 1)
-
-        def copy(which):
-            return pltpu.make_async_copy(
-                before[which], self.came.at[which], self.came_sems.at[which]
-            )
-
+            if before:
+
+                @pl.when(self.comes[which])
+                def _():
+                    self.earlier(which, before).wait()
+
+        rows = self.held.shape[1] // self.PARTS
+        for part in range(self.PARTS):
+            span = slice(part * rows, (part + 1) * rows)
+            for which in range(2):
+
+                @pl.when(self.leaves[which])
+                def _():
+                    total = self.held[which, span].astype(F32) + self.came[which, span].astype(F32)
+                    if before:
+                        more = self.brought[which, span].astype(F32)
+                        total = total + jnp.where(self.comes[which], more, 0.0)
+                    self.held[which, span] = total.astype(BF)
+                    self.copy(which, part).start()
+
+    def wait(self):
         for which in range(2):
-
-            @pl.when(comes[which])
-            def _():
-                copy(which).start()
-
-        for which in range(2):
-
-            @pl.when(comes[which])
-            def _():
-                copy(which).wait()
-                self.add_came(which)
-
-    def moves(self, after, send_sems, recv_sems):
-        return Moves(
-            self.place, self.held.at[0], self.held.at[1], *after, send_sems, recv_sems
-        )
-
-    @staticmethod
-    def scratch(block):
+            for part in range(self.PARTS):
+
+                @pl.when(self.leaves[which])
+                def _():
+                    self.copy(which, part).wait_send()
+
+                @pl.when(self.comes[which])
+                def _():
+                    self.copy(which, part).wait_recv()
+
+    @classmethod
+    def scratch(cls, block):
         return [
             pltpu.VMEM((2,) + block, BF),
             pltpu.VMEM((2,) + block, BF),
-            pltpu.SemaphoreType.DMA((2,)),
-            pltpu.SemaphoreType.DMA((2,)),
+            pltpu.VMEM((2,) + block, BF),
+            pltpu.SemaphoreType.DMA((2, 3)),
+            pltpu.SemaphoreType.DMA((2, cls.PARTS)),
+            pltpu.SemaphoreType.DMA((2, cls.PARTS)),
         ]
 
 
@@ -1436,10 +1461,7 @@
             )
         )
     ]
-    moves = None
-    if n_moves:
-        line = RoundStart(place, call_refs, *refs[:4])
-        moves = line.moves(arrivals, *refs[4:])
+    line = RoundStart(place, call_refs, arrivals, *refs) if n_moves else None
     e = pl.program_id(0)
     total = x_ref.shape[1]
     cap = xs.shape[1] // 2
@@ -1464,14 +1486,13 @@
 
     @pl.when(e == 0)
     def _():
+        if n_moves:
+            line.load(call - 1, before)
         for load in loads:
             load.start()
         place.greet(False)
         if n_moves:
-            line.prepare(call - 1)
-            if n_before:
-                line.add(before)
-            moves.start()
+            line.send(before)
         ggw_ref[...] = jnp.zeros_like(ggw_ref)
         for load in loads:
             load.wait()
@@ -1552,7 +1573,8 @@
 
     @pl.when(e == EXP_DEV - 1)
     def _():
-        for core in range(2):
+        for part in range(2):
+            core = my_core if part else 1 - my_core
             both = mm(x_ref[core], sgu_ref[...])
             s_act, s_slope = silu_parts(both[:, :hidden_units])
             s_up = both[:, hidden_units:]
@@ -1571,20 +1593,18 @@
                 stage[0, core, :, cols] = value.astype(BF)
                 made = mm_tn(x_ref[core, :, cols], grad_both)
                 made_d = mm_tn(dy_ref[core, :, cols], s_hidden)
-                if core == 0:
+                if part == 0:
                     shared_ref[cols, : 2 * hidden_units] = made
                     shared_ref[cols, 2 * hidden_units :] = made_d
                 else:
                     shared_ref[cols, : 2 * hidden_units] += made
                     shared_ref[cols, 2 * hidden_units :] += made_d
-        for which in (1, 0):
-            core_copy(which).start()
-            own_copy(which).start()
+            for which in (1, 0):
+                (own_copy if part else core_copy)(which).start()
         slot_copy(0).wait()
         slot_copy(1).wait()
         if n_moves:
-            moves.wait_send()
-            moves.wait_recv()
+            line.wait()
         for which in (1, 0):
             own_copy(which).wait()
             core_copy(which).wait_send()
@@ -1659,10 +1679,7 @@
             pltpu.SemaphoreType.DMA((2,)),
         ]
         + (
-            RoundStart.scratch((total, width))
-            + [pltpu.SemaphoreType.DMA((2,)), pltpu.SemaphoreType.DMA((2,))]
-            if call
-            else []
+            RoundStart.scratch((total, width)) if call else []
         ),
         compiler_params=pltpu.CompilerParams(
             collective_id=4 + call, has_side_effects=True, vmem_limit_bytes=60 * 1024 * 1024
@@ -1754,10 +1771,11 @@
     units = s_gate.shape[1]
     shared = jnp.concatenate([s_gate, s_up], axis=1)
     per_row = s_down.shape[0] // units
-    downs = s_down.reshape(per_row, units, s_down.shape[1])
+    downs = s_down.reshape(per_row, units * s_down.shape[1] // 128, 128)
     full, dy_all, routes_all, sgu, sdown, egate, e_up, e_down, _ = first_gather(
         bundle, cotangent, routes_t, shared, downs, e_gate, [e_up, e_down], 0, rows_n, cols_n
     )
+    sdown = sdown.reshape(cols_n, units, width // cols_n)
     sdown = jnp.swapaxes(sdown, 0, 1).reshape(units, width)
     sgu = sgu.reshape(width, 2 * units)
 

time: 806 us -> 795 us (0.986)
  Pallas kernels: 724 us -> 715 us
where the time goes in v6:
time: 795 us; the launch traced here: 792 us
  Pallas kernels  715 us (90%)
  local copies, waits for them, and re-layouts  28.2 us (4%)
  other arithmetic  23.8 us (3%)
  between operations  14.5 us (2%)
    pallas_call x1, Pallas kernels, dense_sum(): pl.pallas_call(kernel, in_specs=[vmem] * (2 * n + 1) + [ANY] * (1 + 2 * c...  180 us
    pallas_call x4, Pallas kernels, routed(): pl.pallas_call(functools.partial(routed_kernel, call, rows_n, cols_n), gr...  175 us
    pallas_call x1, Pallas kernels, first_gather(): pl.pallas_call(kernel, in_specs=[ANY] * (6 + n_later), out_specs=[ANY] *...  144 us
    pallas_call x1, Pallas kernels, line_gather(): pl.pallas_call(kernel, in_specs=[ANY] * n, out_specs=[ANY] * n, out_shape...  111 us
    pallas_call x1, Pallas kernels, block_end(): pl.pallas_call(kernel, in_specs=[pl.BlockSpec(memory_space=pl.ANY)] * n +...  38.8 us
    pallas_call x3, Pallas kernels, expert_grads(): pl.pallas_call(functools.partial(expert_grads_kernel, units_n, rows_n, cu...  37.8 us
    pallas_call x1, Pallas kernels, block_start(): pl.pallas_call(kernel, in_specs=[pl.BlockSpec(memory_space=pl.ANY)] * n +...  27.3 us
  transfers between devices with their start and end apart: 6, of which 1 were waited for; matrix products, arithmetic and copies ran while one was open for 5% of the time, Pallas kernels for 48%

profile of v6, /device:TPU:2, one launch (start us, length us, event | category | flops | bytes accessed | tf_op | source)
XLA Modules:
  0.0 791.7 jit_solution(15410438603432248182)
XLA Ops:
  7.3 0.0 all-gather.3.cloned.1.call-start
  7.3 2.8 copy.99.refs_6_
  10.2 1.2 copy.100.refs_7_
  11.4 0.1 copy.74
  11.5 0.8 reshape.110.refs_4_
  12.5 0.7 pad_maximum_fusion.refs_3_
  13.2 0.6 pad.25.refs_2_
  13.8 0.7 copy-done.5
  14.5 144.2 %first_gather.1 = (bf16[4,8,528,384]{3,2,1,0:T(8,128)(2,1)}, bf16[8,512,1536]{2,1,0:T(8,128)(2,1)}, s32[8,8,512]{2,1,0:T(8,128)}, bf16[4,384,256]{2,1,0:T(8,128)...) custom-call(bf16[528,384]{1,0:T(8,128)(2,1)} %copy-done.5, ...), custom_call_target="tpu_custom_call", output_to_operand_aliasing={{6}: (6, {}), {7}: (7, {})} | custom-call | tf_op jit(solution)/shard_map/first_gather/pallas_call | solution.py:940
  158.8 0.0 all-gather.3.cloned.1.call-update
  158.8 0.0 all-gather.5.cloned.1.call-start
  158.9 0.7 all-gather.5.cloned.1.call-update
  159.6 0.3 reduce-scatter.14.cloned.1.call-start
  159.8 0.9 copy.77.refs_5_.refs_6_
  160.7 0.1 reshape.111
  160.8 0.2 dynamic-slice_reduce_fusion
  161.0 0.2 select_reduce_fusion.2
  161.2 0.1 select_reduce_fusion.1
  161.3 0.1 convert_reduce_fusion
  161.4 0.9 copy.76.refs_3_.refs_4_
  162.2 0.9 convert_bitcast_fusion
  163.1 0.7 reshape.120.refs_2_.refs_3_
  163.8 1.9 copy.78
  165.7 0.3 reshape.113
  166.1 0.3 copy.79
  166.3 0.9 copy.83.refs_9_
  167.3 27.3 %block_start.1 = (bf16[512,1536]{1,0:T(8,128)(2,1)}, bf16[512,1536]{1,0:T(8,128)(2,1)}, bf16[512,512]{1,0:T(8,128)(2,1)}, bf16[512,512]{1,0:T(8,128)(2,1)}, bf16...) custom-call(bf16[4,8,528,384]{3,2,1,0:T(8,128)(2,1)} %get-tuple-elem, ...), custom_call_target="tpu_custom_call" | custom-call | flops 10000000000 | bytes 30000000 | tf_op jit(solution)/shard_map/block_start/pallas_call | solution.py:243
  194.6 111.3 %line_gather.1 = (bf16[8,512,1536]{2,1,0:T(8,128)(2,1)}, f32[8,8,512]{2,1,0:T(8,128)}) custom-call(bf16[512,1536]{1,0:T(8,128)(2,1)} %get-tuple-element.92.refs_0_.refs_9_, f32[8,512]{1,0:T(8,128)} %get-tuple-element.93.refs_1_), custom_call_target="tpu_custom_call" | custom-call | tf_op jit(solution)/shard_map/line_gather/pallas_call | solution.py:696
  305.9 0.0 all-gather.3.cloned.1.call-done.refs_6_
  305.9 5.9 all-gather.5.cloned.1.call-done.refs_7_
  311.8 34.0 %routed.4 = (bf16[2,512,1536]{2,1,0:T(8,128)(2,1)}, bf16[2,512,1536]{2,1,0:T(8,128)(2,1)}, bf16[4,256,1536]{2,1,0:T(8,128)(2,1)}, bf16[4,256,1536]{2,1,0:T(8,128...) custom-call(bf16[8,512,1536]{2,1,0:T(8,128)(2,1)} %get-tuple-element, ...), custom_call_target="tpu_custom_call" | custom-call | flops 24000000000 | bytes 100000000 | tf_op jit(solution)/shard_map/routed/pallas_call | solution.py:1635
  345.8 46.3 %routed.5 = (bf16[2,512,1536]{2,1,0:T(8,128)(2,1)}, bf16[2,512,1536]{2,1,0:T(8,128)(2,1)}, bf16[4,256,1536]{2,1,0:T(8,128)(2,1)}, bf16[4,256,1536]{2,1,0:T(8,128...) custom-call(bf16[8,512,1536]{2,1,0:T(8,128)(2,1)} %get-tuple-element, ...), custom_call_target="tpu_custom_call" | custom-call | flops 24000000000 | bytes 100000000 | tf_op jit(solution)/shard_map/routed/pallas_call | solution.py:1635
  392.2 47.6 %routed.6 = (bf16[2,512,1536]{2,1,0:T(8,128)(2,1)}, bf16[2,512,1536]{2,1,0:T(8,128)(2,1)}, bf16[4,256,1536]{2,1,0:T(8,128)(2,1)}, bf16[4,256,1536]{2,1,0:T(8,128...) custom-call(bf16[8,512,1536]{2,1,0:T(8,128)(2,1)} %get-tuple-element, ...), custom_call_target="tpu_custom_call" | custom-call | flops 24000000000 | bytes 100000000 | tf_op jit(solution)/shard_map/routed/pallas_call | solution.py:1635
  439.8 47.0 %routed.7 = (bf16[2,512,1536]{2,1,0:T(8,128)(2,1)}, bf16[2,512,1536]{2,1,0:T(8,128)(2,1)}, bf16[4,256,1536]{2,1,0:T(8,128)(2,1)}, bf16[4,256,1536]{2,1,0:T(8,128...) custom-call(bf16[8,512,1536]{2,1,0:T(8,128)(2,1)} %get-tuple-element, ...), custom_call_target="tpu_custom_call" | custom-call | flops 24000000000 | bytes 100000000 | tf_op jit(solution)/shard_map/routed/pallas_call | solution.py:1635
  486.7 13.3 %expert_grads.5 = bf16[4,4,512,384]{3,2,1,0:T(8,128)(2,1)} custom-call(bf16[4,256,512]{2,1,0:T(8,128)(2,1)} %get-tuple-element.155.refs_0_, bf16[4,256,512]{2,1,0:T(8,128)(2,1)} %get-tuple-element.156.refs_1_, bf16[4,256,512]{2,1,0:T(8,128)(2,1)} %get-tuple-element.157.refs_2_, bf16[4,256,512]{2,1,0:T(8,128)(2,1)} %get-tuple-element.158.refs_3_, ...), custom_call_target="tpu_custom_call" | custom-call | flops 7000000000 | bytes 30000000 | tf_op jit(solution)/shard_map/expert_grads/pallas_call | solution.py:1718
  500.0 0.0 reduce-scatter.12.cloned.1.call-start
  500.1 11.8 %expert_grads.4 = bf16[4,4,384,512]{3,2,1,0:T(8,128)(2,1)} custom-call(bf16[4,256,1536]{2,1,0:T(8,128)(2,1)} %get-tuple-element.143.refs_0_, bf16[4,256,1536]{2,1,0:T(8,128)(2,1)} %get-tuple-element.144.refs_1_, bf16[4,256,1536]{2,1,0:T(8,128)(2,1)} %get-tuple-element.145.refs_2_, bf16[4,256,1536]{2,1,0:T(8,128)(2,1)} %get-tuple-element.146.refs_3_, ...), custom_call_target="tpu_custom_call" | custom-call | flops 7000000000 | bytes 30000000 | tf_op jit(solution)/shard_map/expert_grads/pallas_call | solution.py:1718
  511.9 0.0 reduce-scatter.10.cloned.1.call-start
  511.9 12.7 %expert_grads.3 = bf16[4,4,384,512]{3,2,1,0:T(8,128)(2,1)} custom-call(bf16[4,256,1536]{2,1,0:T(8,128)(2,1)} %get-tuple-element.143.refs_0_, bf16[4,256,1536]{2,1,0:T(8,128)(2,1)} %get-tuple-element.144.refs_1_, bf16[4,256,1536]{2,1,0:T(8,128)(2,1)} %get-tuple-element.145.refs_2_, bf16[4,256,1536]{2,1,0:T(8,128)(2,1)} %get-tuple-element.146.refs_3_, ...), custom_call_target="tpu_custom_call" | custom-call | flops 7000000000 | bytes 30000000 | tf_op jit(solution)/shard_map/expert_grads/pallas_call | solution.py:1718
  524.7 0.8 dynamic-slice_bitcast_fusion
  525.6 0.1 iota_compare_fusion.3
  525.7 0.8 select_reduce_fusion
  526.5 3.4 all-to-all-start
  529.9 5.0 add_convert_fusion
  534.8 0.8 copy-done.2
  535.6 1.9 slice_bitcast_fusion
  537.5 0.7 reshape.116.refs_8_
  538.2 38.8 %block_end.1 = (f32[512,1536]{1,0:T(8,128)}, bf16[512,1536]{1,0:T(8,128)(2,1)}, bf16[512,512]{1,0:T(8,128)(2,1)}, bf16[512,512]{1,0:T(8,128)(2,1)}, bf16[512,153...) custom-call(bf16[4,8,528,384]{3,2,1,0:T(8,128)(2,1)} %get-tuple-element.90.refs_0_, ...), custom_call_target="tpu_custom_call" | custom-call | flops 20000000000 | bytes 40000000 | tf_op jit(solution)/shard_map/block_end/pallas_call | solution.py:361
  576.9 0.8 slice_reduce_fusion.1
  577.8 0.1 reshape_squeeze.6
  577.8 0.1 reshape_squeeze.7
  577.9 0.1 fusion.2
  578.0 1.0 pad.28
  578.9 180.5 %dense_sum.1 = (f32[528,384]{1,0:T(8,128)}, f32[384,256]{1,0:T(8,128)}, f32[2,192,128]{2,1,0:T(8,128)}, bf16[3,2,512,1536]{3,2,1,0:T(8,128)(2,1)}) custom-call(bf16[512,1536]{1,0:T(8,128)(2,1)} %get-tuple-element.128.refs_0_, bf16[512,512]{1,0:T(8,128)(2,1)} %get-tuple-element.129.refs_1_, bf16[512,512]{1,0:T(8,128)(2,1)} %get-tuple-element.130.refs_2_, ...), custom_call_target="tpu_custom_call" | custom-call | flops 6442450944 | bytes 350000000 | tf_op jit(solution)/shard_map/dense_sum/pallas_call | solution.py:1352
  759.4 1.3 slice_bitcast_fusion.7
  760.7 1.3 slice_bitcast_fusion.6
  762.0 1.6 slice_bitcast_fusion.4
  763.6 1.6 copy_bitcast_fusion
  765.2 1.8 fusion.10
  767.0 1.9 slice_bitcast_fusion.2
  769.0 5.6 fusion.1
  774.6 3.3 bitcast_convert_fusion
  777.9 3.5 bitcast_convert_fusion.1
  781.4 3.5 bitcast_convert_fusion.2
  (65 shorter events, 0.3 us)
Async XLA Ops:
  7.2 5.2 copy-start.24
  7.2 4.2 copy-start.7
  7.2 5.1 copy-start.14
  7.2 5.1 copy-start.15
  7.2 5.1 copy-start.8
  7.2 5.2 copy-start.23
  7.2 2.9 copy-start.4
  7.3 5.2 copy-start.12
  7.3 5.2 copy-start.11
  7.3 4.1 copy-start.10
  7.3 298.6 %all-gather.3.cloned.1.call-start = ((), (), s32[]{:S(2)}) async-start(), calls=%async_computation.4 | async-start | bytes 7864320 | tf_op jit(solution)/shard_map/all_gather | solution.py:1787
  10.2 3.0 copy-start.13
  10.2 3.6 copy-start.21
  13.8 0.8 copy-start.5
  158.7 2.0 copy-start.22
  158.8 2.2 copy-start.25
  158.8 5.0 copy-start.9
  158.8 6.9 copy-start.6
  158.8 153.0 %all-gather.5.cloned.1.call-start = ((), (), s32[]{:S(2)}) async-start(), calls=%async_computation.5 | async-start | bytes 7864320 | tf_op jit(solution)/shard_map/all_gather | solution.py:1788
  159.6 615.0 %reduce-scatter.14.cloned.1.call-start = ((), (), s32[]{:S(2)}) async-start(), calls=%async_computation.8 | async-start | bytes 7864320
  161.4 5.9 copy-start.20
  500.0 277.9 %reduce-scatter.12.cloned.1.call-start = ((), (), s32[]{:S(2)}) async-start(), calls=%async_computation.7 | async-start | bytes 7864320
  511.9 269.5 %reduce-scatter.10.cloned.1.call-start = ((), (), s32[]{:S(2)}) async-start(), calls=%async_computation.6 | async-start | bytes 7864320
  524.6 1.0 copy-start.16
  524.7 1.0 copy-start.17
  524.7 1.0 copy-start.18
  524.7 1.0 copy-start.19
  524.7 5.1 copy-start.3
  526.5 11.1 %all-to-all-start = ((f32[8,4,512]{2,1,0:T(4,128)}), f32[8,4,512]{2,1,0:T(4,128)S(1)}, u32[]{:S(2)}, u32[]{:S(2)}) async-start(f32[8,4,512]{2,1,0:T(4,128)} %bitcast.22), calls=%async_computation | async-start | bytes 131072 | tf_op jit(solution)/shard_map/all_to_all | solution.py:1828
  529.8 5.0 copy-start
  529.8 5.8 copy-start.2
  578.9 190.0 %copy-start.1 = (bf16[2,512,1536]{2,1,0:T(8,128)(2,1)S(1)}, bf16[2,512,1536]{2,1,0:T(8,128)(2,1)}, u32[]{:S(2)}) copy-start(bf16[2,512,1536]{2,1,0:T(8,128)(2,1)} %get-tuple-element.113.refs_18_) | copy-start | bytes 9437188
Sparse Core Ops, SparseCore 0:
  158.9 80.9 all-gather.2
  241.8 69.9 all-gather.4
  500.2 75.2 reduce-scatter.13
  578.3 116.3 reduce-scatter.11
  697.5 78.4 reduce-scatter.9
